TPU v7x, 256 devices: a whole 4x4x8 slice. The times are simulated.
256 devices in a mesh: gx: 64 (over z, y, x_lo), gy: 4 (over x_hi, core).
Axes of the slice: x: 4 (x_hi: 2, x_lo: 2; x = x_hi * 2 + x_lo), y: 4, z: 8, core: 2. Of those that a mesh axis runs over, the one named last changes fastest.
Arguments:
- inputs: bfloat16 [4, 1536, 64, 512], P(None, 'gx', 'gy'), may hold values from -6 to 6
- coverage: int32 [1536, 64], P(None, 'gy'), may hold values from 0 to 1, as said below
- encoded: bfloat16 [64, 8, 64, 512], P('gx', 'gy'), may hold values from -6 to 6
- cross_list: int32 [192, 8, 4], P('gx', 'gy'), may hold values from 0 to 511, as said below
- gain_self: float32 [512], replicated, may hold values from 0.1 to 1.9
- gain_cross: float32 [512], replicated, may hold values from 0.1 to 1.9
- gain_ffn: float32 [512], replicated, may hold values from 0.1 to 1.9
- self_wq: bfloat16 [512, 512], replicated, may hold values from -1.5 to 1.5
- self_wkv: bfloat16 [512, 1024], replicated, may hold values from -1.5 to 1.5
- self_wo: bfloat16 [512, 512], replicated, may hold values from -0.25 to 0.25
- cross_wq: bfloat16 [512, 512], replicated, may hold values from -1.5 to 1.5
- cross_wkv: bfloat16 [512, 1024], replicated, may hold values from -1.5 to 1.5
- cross_wo: bfloat16 [512, 512], replicated, may hold values from -0.25 to 0.25
- ffn_in: bfloat16 [512, 2048], replicated, may hold values from -0.25 to 0.25
- ffn_out: bfloat16 [2048, 512], replicated, may hold values from -0.125 to 0.125
Outputs:
- output: bfloat16 [4, 1536, 64, 512], P(None, 'gx', 'gy')
Inputs may be any that keep to these rules, and one draw needn't show every extreme that they name: 1 marks a cell with radar coverage. `cross_list`: for query cuboid (i, j), every entry e satisfies |e // 8 - i * 8 // 24| <= 1.
All inputs are finite; a program needn't handle non-finite values.
Results may differ from a plain program's by a relative error of at most 0.023.
Values may be sent and summed in bfloat16 or wider, within the bound.
No kernel may reach another device: no remote copies, remote signals or barrier semaphores. Data moves between devices by JAX's collectives and lax.ppermute only.
A program may use at most 128 MiB of HBM per device.

v0:
```python
import jax
import jax.numpy as jnp
from jax import lax
from jax.sharding import PartitionSpec as P

HEADS = 8
BX = 8
BY = 8


epsilon = 1e-05
mask_depth = 30.0


def padded(cells, sides, width):
    for axis, dim in sides:
        count = lax.axis_size(axis)
        ends = count - 1
        head = lax.slice_in_dim(cells, 0, width, axis=dim)
        tail = lax.slice_in_dim(cells, cells.shape[dim] - width, cells.shape[dim], axis=dim)
        cells = jnp.concatenate(
            [
                lax.ppermute(tail, axis, [(i, (i + 1) % count) for i in range(ends)]),
                cells,
                lax.ppermute(head, axis, [((i + 1) % count, i) for i in range(ends)]),
            ],
            axis=dim,
        )
    return cells


def layer_norm(values, gain_vec):
    widened = values.astype(jnp.float32)
    centre = widened - jnp.mean(widened, axis=-1, keepdims=True)
    spread = jnp.mean(centre * centre, axis=-1, keepdims=True)
    return (centre * lax.rsqrt(spread + epsilon) * gain_vec).astype(jnp.bfloat16)


def project(values, weight):
    return jnp.dot(values, weight, preferred_element_type=jnp.float32).astype(jnp.bfloat16)


def residual(base, update, weight):
    return (
        base.astype(jnp.float32) + jnp.dot(update, weight, preferred_element_type=jnp.float32)
    ).astype(jnp.bfloat16)


def to_cuboids(grid_in, size_x, size_y):
    frame_count, row_count, col_count, channels = grid_in.shape
    split_grid = grid_in.reshape(
        frame_count, row_count // size_x, size_x, col_count // size_y, size_y, channels
    )
    return split_grid.transpose(1, 3, 0, 2, 4, 5).reshape(
        row_count // size_x, col_count // size_y, frame_count * size_x * size_y, channels
    )


def from_cuboids(blocks, frame_count, size_x, size_y):
    blocks_x, blocks_y, length, channels = blocks.shape
    split_grid = blocks.reshape(blocks_x, blocks_y, frame_count, size_x, size_y, channels)
    return split_grid.transpose(2, 0, 3, 1, 4, 5).reshape(
        frame_count, blocks_x * size_x, blocks_y * size_y, channels
    )


def cuboid_bias(cover, frame_count):
    blocks_x = cover.shape[0] // BX
    blocks_y = cover.shape[1] // BY
    tiles = (
        cover.reshape(blocks_x, BX, blocks_y, BY)
        .transpose(0, 2, 1, 3)
        .reshape(blocks_x, blocks_y, 1, BX * BY)
    )
    tiles = jnp.broadcast_to(tiles, (blocks_x, blocks_y, frame_count, BX * BY))
    return (tiles.reshape(blocks_x, blocks_y, frame_count * BX * BY) - 1.0) * mask_depth


def attend(queries, keys, values, bias, head_count):
    batches, query_count, features = queries.shape
    key_count = keys.shape[1]
    head_dim = features // head_count
    q_heads = queries.reshape(batches, query_count, head_count, head_dim)
    k_heads = keys.reshape(batches, key_count, head_count, head_dim)
    v_heads = values.reshape(batches, key_count, head_count, head_dim)
    scores = jnp.einsum(
        "bqhd,bkhd->bhqk", q_heads, k_heads, preferred_element_type=jnp.float32
    ) * head_dim ** (-0.5)
    if bias is not None:
        scores = scores + bias[:, None, None, :]
    row_max = jnp.max(scores, axis=-1, keepdims=True)
    weights = jnp.exp(scores - row_max)
    weights = (weights / jnp.sum(weights, axis=-1, keepdims=True)).astype(jnp.bfloat16)
    mixed_out = jnp.einsum("bhqk,bkhd->bqhd", weights, v_heads, preferred_element_type=jnp.float32)
    return mixed_out.reshape(batches, query_count, features).astype(jnp.bfloat16)


def fetch_window(block_in):
    strip_all = lax.all_gather(block_in, "gy", axis=1, tiled=True)
    return padded(strip_all, (("gx", 0),), 1)


def shards(
    inputs,
    coverage,
    encoded,
    cross_list,
    gain_self,
    gain_cross,
    gain_ffn,
    self_wq,
    self_wkv,
    self_wo,
    cross_wq,
    cross_wkv,
    cross_wo,
    ffn_in,
    ffn_out,
):
    frame_count, row_count, col_count, features = inputs.shape
    offset_rows = BX // 2
    strip_index = lax.axis_index("gx")
    normed = layer_norm(inputs, gain_self)
    keyvals = padded(project(normed, self_wkv), (("gx", 1),), offset_rows)
    queries = jnp.pad(
        project(normed, self_wq), ((0, 0), (offset_rows, offset_rows), (0, 0), (0, 0))
    )
    cover = jnp.pad(coverage.astype(jnp.float32), ((offset_rows, offset_rows), (0, 0)))
    cover = lax.dynamic_slice_in_dim(cover, strip_index * row_count, row_count + 2 * offset_rows, 0)
    bias_blocks = cuboid_bias(cover, frame_count)
    q_blocks = to_cuboids(queries, BX, BY)
    grid_shape = q_blocks.shape
    length = grid_shape[2]
    flat_kv = to_cuboids(keyvals, BX, BY).reshape(-1, length, 2 * features)
    attended = attend(
        q_blocks.reshape(-1, length, features),
        flat_kv[..., :features],
        flat_kv[..., features:],
        bias_blocks.reshape(-1, length),
        HEADS,
    )
    attended = from_cuboids(attended.reshape(grid_shape), frame_count, BX, BY)[
        :, offset_rows : offset_rows + row_count
    ]
    first = residual(inputs, attended, self_wo)
    normed = layer_norm(first, gain_cross)
    cross_blocks = to_cuboids(project(normed, cross_wq), BX, BY)
    cube_shape = cross_blocks.shape
    window = fetch_window(project(encoded, cross_wkv))
    per_strip = window.shape[1]
    nearby = window.reshape(-1, window.shape[2], 2 * features)
    local_ids = (cross_list - (strip_index - 1) * per_strip).reshape(-1)
    chosen = jnp.take(nearby, local_ids, axis=0).reshape(
        cube_shape[0] * cube_shape[1], -1, 2 * features
    )
    attended = attend(
        cross_blocks.reshape(-1, cube_shape[2], features),
        chosen[..., :features],
        chosen[..., features:],
        None,
        HEADS,
    )
    attended = from_cuboids(attended.reshape(cube_shape), frame_count, BX, BY)
    second = residual(first, attended, cross_wo)
    normed = layer_norm(second, gain_ffn)
    hidden = jax.nn.gelu(jnp.dot(normed, ffn_in, preferred_element_type=jnp.float32)).astype(
        jnp.bfloat16
    )
    return residual(second, hidden, ffn_out)


def solution(mesh):
    return jax.shard_map(
        shards,
        mesh=mesh,
        in_specs=(
            P(None, "gx", "gy", None),
            P(None, "gy"),
            P("gx", "gy", None, None),
            P("gx", "gy", None),
            P(),
            P(),
            P(),
            P(),
            P(),
            P(),
            P(),
            P(),
            P(),
            P(),
            P(),
        ),
        out_specs=P(None, "gx", "gy", None),
        check_vma=False,
    )
```

profile of v0, /device:TPU:148, one launch (start us, length us, event | category | flops | bytes accessed | tf_op | source)
XLA Modules:
  0.0 246.8 jit_solution(1472087413937615596)
XLA Ops:
  6.6 1.8 convert_reduce_fusion.2
  8.4 2.1 fusion.35
  10.6 2.1 convolution_convert_fusion
  12.8 1.6 copy-done.2
  14.4 1.1 fusion.88
  15.5 3.1 %collective-permute-start = (bf16[4,4,16,1024]{3,2,1,0:T(8,128)(2,1)}, bf16[4,4,16,1024]{3,2,1,0:T(8,128)(2,1)S(1)}, u32[]{:S(2)}, u32[]{:S(2)}) collective-permute-start(bf16[4,4,16,1024]{3,2,1,0:T(8,128)(2,1)} %get-tuple-element.9), channel_id=1, source_target_pairs={{0,4},{4,8},{8,12},{12,16},{16,20},{20,24},{24,28},{28,32},{32,36}... | collective-permute-start | bytes 1572872 | tf_op jit(solution)/shard_map/ppermute | solution.py:23
  18.6 3.6 %collective-permute-start.1 = (bf16[4,4,16,1024]{3,2,1,0:T(8,128)(2,1)}, bf16[4,4,16,1024]{3,2,1,0:T(8,128)(2,1)S(1)}, u32[]{:S(2)}, u32[]{:S(2)}) collective-permute-start(bf16[4,4,16,1024]{3,2,1,0:T(8,128)(2,1)} %get-tuple-element.10), channel_id=1, source_target_pairs={{4,0},{8,4},{12,8},{16,12},{20,16},{24,20},{28,24},{32,28},{36,32}... | collective-permute-start | bytes 1572872 | tf_op jit(solution)/shard_map/ppermute | solution.py:25
  22.3 1.0 convolution_convert_fusion.3
  23.5 2.6 %convolution_convert_fusion.2 = bf16[4,24,16,512]{3,2,1,0:T(8,128)(2,1)S(1)} fusion(bf16[4,24,16,512]{3,2,1,0:T(8,128)(2,1)} %param.15, f32[512]{0:T(512)S(1)} %copy-done.16, f32[4,24,16]{2,1,0:T(8,128)S(1)} %add_rsqrt_fusion.2, f32[4,24,16]{2,1,0:T(8,128)S(1)} %broadcast_multiply_fusion.2, bf16[512,512]{1,0:T(8,128)(2,1)} %param.22), kind=kOutput, calls=%fused_computation.68 | convolution fusion | flops 810024960 | bytes 3684352 | tf_op jit(solution)/shard_map/dot_general | solution.py:40
  26.3 1.6 copy.97
  27.9 6.2 %reshape_reshape_reshape.6 = bf16[8,256,8,64]{3,2,1,0:T(8,128)(2,1)} reshape(bf16[4,2,4,8,8,512]{5,4,3,2,1,0:T(8,128)(2,1)} %bitcast.104) | data formatting | bytes 4194304 | tf_op jit(solution)/shard_map/reshape;reshape;reshape | solution.py:83
  34.8 12.8 %collective-permute-done.1 = bf16[4,4,16,1024]{3,2,1,0:T(8,128)(2,1)S(1)} collective-permute-done((bf16[4,4,16,1024]{3,2,1,0:T(8,128)(2,1)}, bf16[4,4,16,1024]{3,2,1,0:T(8,128)(2,1)S(1)}, u32[]{:S(2)}, u32[]{:S(2)}) %collective-permute-start.1) | collective-permute-done | bytes 524320 | tf_op jit(solution)/shard_map/ppermute | solution.py:25
  47.6 2.2 pad_maximum_fusion
  49.8 0.7 copy.66
  50.5 2.5 fusion.86
  52.9 3.9 %copy.69 = bf16[8,256,512]{1,2,0:T(8,128)(2,1)} copy(bf16[8,256,512]{2,1,0:T(8,128)(2,1)} %get-tuple-element.5) | data formatting | bytes 4194304 | tf_op jit(solution)/shard_map/slice | solution.py:137
  56.8 3.9 %copy.67 = bf16[8,256,512]{1,2,0:T(8,128)(2,1)} copy(bf16[8,256,512]{2,1,0:T(8,128)(2,1)} %get-tuple-element.6) | data formatting | bytes 4194304 | tf_op jit(solution)/shard_map/slice | solution.py:138
  60.7 11.0 %fusion.21 = f32[8,8,256,256]{2,3,1,0:T(8,128)} fusion(bf16[8,256,8,64]{1,3,2,0:T(8,128)(2,1)} %bitcast.107, bf16[8,256,8,64]{3,2,1,0:T(8,128)(2,1)} %reshape_reshape_reshape.6), kind=kOutput, calls=%fused_computation.36 | convolution fusion | flops 536870912 | bytes 20971520 | tf_op jit(solution)/shard_map/bqhd,bkhd->bhqk/dot_general | solution.py:86
  71.7 18.8 %fusion.89 = (f32[8,8,256]{2,1,0:T(8,128)S(1)}, f32[8,8,256,256]{2,3,1,0:T(8,128)}) fusion(f32[8,8,256,256]{2,3,1,0:T(8,128)} %fusion.21, f32[8,256]{1,0:T(8,128)S(1)} %mul.128), kind=kOutput, calls=%fused_computation.109 | output fusion | flops 25166080 | bytes 33628160 | tf_op jit(solution)/shard_map/sub | solution.py:92
  90.5 8.8 %convert_bitcast_fusion = bf16[8,256,8,64]{1,3,2,0:T(8,128)(2,1)} fusion(bf16[8,256,8,64]{1,3,2,0:T(8,128)(2,1)S(1)} %bitcast.112, f32[8,8,256,256]{2,3,1,0:T(8,128)} %get-tuple-element.12, f32[8,8,256]{2,1,0:T(8,128)S(1)} %get-tuple-element.11), kind=kOutput, calls=%fused_computation.65 | convolution fusion | flops 546308096 | bytes 21037056 | tf_op jit(solution)/shard_map/bhqk,bkhd->bqhd/dot_general | solution.py:94
  99.3 5.1 %copy.73 = bf16[8,256,8,64]{3,2,1,0:T(8,128)(2,1)} copy(bf16[8,256,8,64]{1,3,2,0:T(8,128)(2,1)} %convert_bitcast_fusion) | data formatting | bytes 4194304 | tf_op jit(solution)/shard_map/convert_element_type | solution.py:95
  104.4 6.4 %convert_element_type.89 = bf16[4,2,4,8,8,512]{5,4,3,2,1,0:T(8,128)(2,1)} reshape(bf16[8,256,8,64]{3,2,1,0:T(8,128)(2,1)} %copy.73) | data formatting | bytes 4194304 | tf_op jit(solution)/shard_map/convert_element_type | solution.py:95
  110.8 3.3 %copy.74 = bf16[4,4,8,2,8,512]{5,4,3,2,1,0:T(8,128)(2,1)} copy(bf16[4,4,8,2,8,512]{5,4,2,0,3,1:T(8,128)(2,1)} %bitcast.105) | data formatting | bytes 4194304 | tf_op jit(solution)/shard_map/transpose | solution.py:62
  114.1 2.8 %collective-permute-start.2 = (bf16[1,8,64,1024]{3,2,1,0:T(8,128)(2,1)}, bf16[1,8,64,1024]{3,2,1,0:T(8,128)(2,1)}, u32[]{:S(2)}, u32[]{:S(2)}) collective-permute-start(bf16[1,8,64,1024]{3,2,1,0:T(8,128)(2,1)} %bitcast.116), channel_id=1, source_target_pairs={{0,4},{4,8},{8,12},{12,16},{16,20},{20,24},{24,28},{28,32},{32,36}... | collective-permute-start | bytes 3145736 | tf_op jit(solution)/shard_map/ppermute | solution.py:23
  116.9 3.9 %collective-permute-start.3 = (bf16[1,8,64,1024]{3,2,1,0:T(8,128)(2,1)}, bf16[1,8,64,1024]{3,2,1,0:T(8,128)(2,1)}, u32[]{:S(2)}, u32[]{:S(2)}) collective-permute-start(bf16[1,8,64,1024]{3,2,1,0:T(8,128)(2,1)} %bitcast.117), channel_id=1, source_target_pairs={{4,0},{8,4},{12,8},{16,12},{20,16},{24,20},{28,24},{32,28},{36,32}... | collective-permute-start | bytes 3145736 | tf_op jit(solution)/shard_map/ppermute | solution.py:25
  120.8 3.0 %convert_reduce_fusion.1 = (f32[4,24,16]{2,1,0:T(8,128)S(1)}, bf16[4,24,16,512]{3,2,1,0:T(8,128)(2,1)S(1)}) fusion(bf16[4,32,16,512]{3,2,1,0:T(8,128)(2,1)} %bitcast.111, bf16[512,512]{1,0:T(8,128)(2,1)S(1)} %copy-done.13, bf16[4,24,16,512]{3,2,1,0:T(8,128)(2,1)} %param.15), kind=kOutput, calls=%fused_computation.31 | convolution fusion | flops 809236992 | bytes 5773312 | tf_op jit(solution)/shard_map/dot_general | solution.py:45
  123.9 0.7 fusion.32
  124.6 1.1 convolution_convert_fusion.1
  125.7 1.3 copy.98
  127.1 5.2 %reshape_reshape_reshape.7 = bf16[6,256,8,64]{3,2,1,0:T(8,128)(2,1)} reshape(bf16[3,2,4,8,8,512]{5,4,3,2,1,0:T(8,128)(2,1)} %bitcast.109) | data formatting | bytes 3145728 | tf_op jit(solution)/shard_map/reshape;reshape;reshape | solution.py:83
  132.3 11.0 %collective-permute-done.2 = bf16[1,8,64,1024]{3,2,1,0:T(8,128)(2,1)} collective-permute-done((bf16[1,8,64,1024]{3,2,1,0:T(8,128)(2,1)}, bf16[1,8,64,1024]{3,2,1,0:T(8,128)(2,1)}, u32[]{:S(2)}, u32[]{:S(2)}) %collective-permute-start.2) | collective-permute-done | bytes 1048608 | tf_op jit(solution)/shard_map/ppermute | solution.py:23
  143.3 22.2 %collective-permute-done.3 = bf16[1,8,64,1024]{3,2,1,0:T(8,128)(2,1)} collective-permute-done((bf16[1,8,64,1024]{3,2,1,0:T(8,128)(2,1)}, bf16[1,8,64,1024]{3,2,1,0:T(8,128)(2,1)}, u32[]{:S(2)}, u32[]{:S(2)}) %collective-permute-start.3) | collective-permute-done | bytes 1048608 | tf_op jit(solution)/shard_map/ppermute | solution.py:25
  165.5 3.5 %pad_maximum_fusion.1 = bf16[3,8,64,1024]{3,2,1,0:T(8,128)(2,1)} fusion(bf16[1,8,64,1024]{3,2,1,0:T(8,128)(2,1)} %collective-permute-done.3, bf16[1,8,64,1024]{3,2,1,0:T(8,128)(2,1)S(1)} %bitcast.118, bf16[1,8,64,1024]{3,2,1,0:T(8,128)(2,1)} %collective-permute-done.2), kind=kLoop, calls=%fused_computation.56 | loop fusion | flops 3145728 | bytes 6291456 | tf_op jit(solution)/shard_map/concatenate | solution.py:21
  169.0 4.4 %gather_fusion = bf16[24,64,1024]{2,1,0:T(8,128)(2,1)} fusion(bf16[24,64,1024]{2,1,0:T(8,128)(2,1)} %bitcast.102, s32[1024]{0:T(1024)S(1)} %pad_clamp_fusion), kind=kCustom, calls=%fused_computation | custom fusion | bytes 6291552 | tf_op jit(solution)/shard_map/jit(_take)/gather | solution.py:153
  173.4 2.1 bitcast_select_fusion
  175.5 1.9 fusion.87
  177.5 2.6 %copy.77 = bf16[6,256,512]{1,2,0:T(8,128)(2,1)} copy(bf16[6,256,512]{2,1,0:T(8,128)(2,1)} %get-tuple-element.7) | data formatting | bytes 3145728 | tf_op jit(solution)/shard_map/slice | solution.py:158
  180.0 8.7 %fusion.41 = f32[6,8,256,256]{2,3,1,0:T(8,128)} fusion(bf16[6,256,8,64]{1,3,2,0:T(8,128)(2,1)} %bitcast.108, bf16[6,256,8,64]{3,2,1,0:T(8,128)(2,1)} %reshape_reshape_reshape.7), kind=kOutput, calls=%fused_computation.58 | convolution fusion | flops 402653184 | bytes 15728640 | tf_op jit(solution)/shard_map/bqhd,bkhd->bhqk/dot_general | solution.py:86
  188.8 15.8 %fusion.90 = (f32[6,8,256]{2,1,0:T(8,128)S(1)}, f32[6,8,256,256]{2,3,1,0:T(8,128)}) fusion(f32[6,8,256,256]{2,3,1,0:T(8,128)} %fusion.41), kind=kOutput, calls=%fused_computation.110 | output fusion | flops 12583167 | bytes 25214976 | tf_op jit(solution)/shard_map/sub | solution.py:92
  204.6 2.6 %copy.75 = bf16[6,256,512]{1,2,0:T(8,128)(2,1)} copy(bf16[6,256,512]{2,1,0:T(8,128)(2,1)} %get-tuple-element.8) | data formatting | bytes 3145728 | tf_op jit(solution)/shard_map/slice | solution.py:159
  207.1 7.4 %fusion.67 = bf16[6,256,8,64]{1,3,2,0:T(8,128)(2,1)} fusion(bf16[6,256,8,64]{1,3,2,0:T(8,128)(2,1)} %bitcast.113, f32[6,8,256,256]{2,3,1,0:T(8,128)} %get-tuple-element.16, f32[6,8,256]{2,1,0:T(8,128)S(1)} %get-tuple-element.15), kind=kOutput, calls=%fused_computation.76 | convolution fusion | flops 409731072 | bytes 15777792 | tf_op jit(solution)/shard_map/bhqk,bkhd->bqhd/dot_general | solution.py:94
  214.6 4.5 %copy.80 = bf16[6,256,8,64]{3,2,1,0:T(8,128)(2,1)} copy(bf16[6,256,8,64]{1,3,2,0:T(8,128)(2,1)} %fusion.67) | data formatting | bytes 3145728 | tf_op jit(solution)/shard_map/convert_element_type | solution.py:95
  219.0 5.5 %convert_element_type.99 = bf16[3,2,4,8,8,512]{5,4,3,2,1,0:T(8,128)(2,1)} reshape(bf16[6,256,8,64]{3,2,1,0:T(8,128)(2,1)} %copy.80) | data formatting | bytes 3145728 | tf_op jit(solution)/shard_map/convert_element_type | solution.py:95
  224.5 1.7 copy.81
  226.4 1.1 convert_reduce_fusion
  227.5 1.1 copy-done.6
  228.6 0.7 fusion.29
  229.4 10.6 %fusion.40 = bf16[4,24,16,512]{3,2,1,0:T(8,128)(2,1)} fusion(bf16[4,24,16,512]{3,2,1,0:T(8,128)(2,1)} %copy-done.6, bf16[2048,512]{1,0:T(8,128)(2,1)S(1)} %copy-done, bf16[512,2048]{1,0:T(8,128)(2,1)} %param.28, f32[512]{0:T(512)S(1)} %copy-done.18, f32[4,24,16]{2,1,0:T(8,128)S(1)} %add_rsqrt_fusion, f32[4,24,16]{2,1,0:T(8,128)S(1)} %broadcast_multiply_fusion), kind=kOutput, calls=%fused_computation.55 | convolution fusion | flops 6477053952 | bytes 7354368 | tf_op jit(solution)/shard_map/dot_general | solution.py:45
  (62 shorter events, 1.3 us)
Async XLA Ops:
  6.5 222.8 %copy-start = (bf16[2048,512]{1,0:T(8,128)(2,1)S(1)}, bf16[2048,512]{1,0:T(8,128)(2,1)}, u32[]{:S(2)}) copy-start(bf16[2048,512]{1,0:T(8,128)(2,1)} %param.29) | copy-start | bytes 6291460
  6.5 4.0 %copy-start.16 = (f32[512]{0:T(512)S(1)}, f32[512]{0:T(512)}, u32[]{:S(2)}) copy-start(f32[512]{0:T(512)} %param.19) | copy-start | bytes 6148
  6.5 4.0 %copy-start.12 = (bf16[512,1024]{1,0:T(8,128)(2,1)S(1)}, bf16[512,1024]{1,0:T(8,128)(2,1)}, u32[]{:S(2)}) copy-start(bf16[512,1024]{1,0:T(8,128)(2,1)} %param.23) | copy-start | bytes 3145732
  6.5 107.5 %all-gather.3.cloned.1.call-start = ((), (), s32[]{:S(2)}) async-start(), calls=%async_computation | async-start | bytes 1310720 | tf_op jit(solution)/shard_map/all_gather | solution.py:99
  6.5 4.0 %copy-start.1 = (bf16[4,24,16,512]{3,2,1,0:T(8,128)(2,1)S(1)}, bf16[4,24,16,512]{3,2,1,0:T(8,128)(2,1)}, u32[]{:S(2)}) copy-start(bf16[4,24,16,512]{3,2,1,0:T(8,128)(2,1)} %param.15) | copy-start | bytes 4718596
  10.6 11.7 %copy-start.7 = (bf16[512,1024]{1,0:T(8,128)(2,1)S(1)}, bf16[512,1024]{1,0:T(8,128)(2,1)}, u32[]{:S(2)}) copy-start(bf16[512,1024]{1,0:T(8,128)(2,1)} %param.26) | copy-start | bytes 3145732
  10.6 11.7 %copy-start.9 = (bf16[1,2,64,512]{3,2,1,0:T(8,128)(2,1)S(1)}, bf16[1,2,64,512]{3,2,1,0:T(8,128)(2,1)}, u32[]{:S(2)}) copy-start(bf16[1,2,64,512]{3,2,1,0:T(8,128)(2,1)} %param.17) | copy-start | bytes 393220
  12.8 1.6 copy-start.2
  14.4 8.9 %copy-start.11 = (s32[3,2,4]{2,1,0:T(2,128)S(1)}, s32[3,2,4]{2,1,0:T(2,128)}, u32[]{:S(2)}) copy-start(s32[3,2,4]{2,1,0:T(2,128)} %param.18) | copy-start | bytes 292
  15.5 19.3 %collective-permute-start = (bf16[4,4,16,1024]{3,2,1,0:T(8,128)(2,1)}, bf16[4,4,16,1024]{3,2,1,0:T(8,128)(2,1)S(1)}, u32[]{:S(2)}, u32[]{:S(2)}) collective-permute-start(bf16[4,4,16,1024]{3,2,1,0:T(8,128)(2,1)} %get-tuple-element.9), channel_id=1, source_target_pairs={{0,4},{4,8},{8,12},{12,16},{16,20},{20,24},{24,28},{28,32},{32,36}... | collective-permute-start | bytes 1572872 | tf_op jit(solution)/shard_map/ppermute | solution.py:23
  18.6 29.0 %collective-permute-start.1 = (bf16[4,4,16,1024]{3,2,1,0:T(8,128)(2,1)}, bf16[4,4,16,1024]{3,2,1,0:T(8,128)(2,1)S(1)}, u32[]{:S(2)}, u32[]{:S(2)}) collective-permute-start(bf16[4,4,16,1024]{3,2,1,0:T(8,128)(2,1)} %get-tuple-element.10), channel_id=1, source_target_pairs={{4,0},{8,4},{12,8},{16,12},{20,16},{24,20},{28,24},{32,28},{36,32}... | collective-permute-start | bytes 1572872 | tf_op jit(solution)/shard_map/ppermute | solution.py:25
  27.9 6.2 %copy-start.10 = (s32[1536,16]{0,1:T(8,128)S(1)}, s32[1536,16]{0,1:T(8,128)}, u32[]{:S(2)}) copy-start(s32[1536,16]{0,1:T(8,128)} %param.16) | copy-start | bytes 294916
  71.7 18.8 %copy-start.3 = (bf16[8,256,512]{1,2,0:T(8,128)(2,1)S(1)}, bf16[8,256,512]{1,2,0:T(8,128)(2,1)}, u32[]{:S(2)}) copy-start(bf16[8,256,512]{1,2,0:T(8,128)(2,1)} %copy.67) | copy-start | bytes 6291460
  110.8 10.0 %copy-start.13 = (bf16[512,512]{1,0:T(8,128)(2,1)S(1)}, bf16[512,512]{1,0:T(8,128)(2,1)}, u32[]{:S(2)}) copy-start(bf16[512,512]{1,0:T(8,128)(2,1)} %param.24) | copy-start | bytes 1572868
  114.1 29.2 %collective-permute-start.2 = (bf16[1,8,64,1024]{3,2,1,0:T(8,128)(2,1)}, bf16[1,8,64,1024]{3,2,1,0:T(8,128)(2,1)}, u32[]{:S(2)}, u32[]{:S(2)}) collective-permute-start(bf16[1,8,64,1024]{3,2,1,0:T(8,128)(2,1)} %bitcast.116), channel_id=1, source_target_pairs={{0,4},{4,8},{8,12},{12,16},{16,20},{20,24},{24,28},{28,32},{32,36}... | collective-permute-start | bytes 3145736 | tf_op jit(solution)/shard_map/ppermute | solution.py:23
  116.9 48.6 %collective-permute-start.3 = (bf16[1,8,64,1024]{3,2,1,0:T(8,128)(2,1)}, bf16[1,8,64,1024]{3,2,1,0:T(8,128)(2,1)}, u32[]{:S(2)}, u32[]{:S(2)}) collective-permute-start(bf16[1,8,64,1024]{3,2,1,0:T(8,128)(2,1)} %bitcast.117), channel_id=1, source_target_pairs={{4,0},{8,4},{12,8},{16,12},{20,16},{24,20},{28,24},{32,28},{36,32}... | collective-permute-start | bytes 3145736 | tf_op jit(solution)/shard_map/ppermute | solution.py:25
  120.8 3.8 %copy-start.14 = (bf16[512,512]{1,0:T(8,128)(2,1)S(1)}, bf16[512,512]{1,0:T(8,128)(2,1)}, u32[]{:S(2)}) copy-start(bf16[512,512]{1,0:T(8,128)(2,1)} %param.25) | copy-start | bytes 1572868
  120.8 3.8 %copy-start.17 = (f32[512]{0:T(512)S(1)}, f32[512]{0:T(512)}, u32[]{:S(2)}) copy-start(f32[512]{0:T(512)} %param.20) | copy-start | bytes 6148
  123.9 1.8 copy-start.4
  127.1 38.4 %copy-start.8 = (bf16[8,64,1024]{2,1,0:T(8,128)(2,1)S(1)}, bf16[8,64,1024]{2,1,0:T(8,128)(2,1)}, u32[]{:S(2)}) copy-start(bf16[8,64,1024]{2,1,0:T(8,128)(2,1)} %all-gather.3.cloned.1.call-done) | copy-start | bytes 3145732
  219.0 7.2 %copy-start.15 = (bf16[512,512]{1,0:T(8,128)(2,1)S(1)}, bf16[512,512]{1,0:T(8,128)(2,1)}, u32[]{:S(2)}) copy-start(bf16[512,512]{1,0:T(8,128)(2,1)} %param.27) | copy-start | bytes 1572868
  224.5 1.9 copy-start.5
  226.4 3.0 %copy-start.18 = (f32[512]{0:T(512)S(1)}, f32[512]{0:T(512)}, u32[]{:S(2)}) copy-start(f32[512]{0:T(512)} %param.21) | copy-start | bytes 6148
  227.5 1.2 copy-start.6
Sparse Core Ops, SparseCore 0:
  23.5 26.0 all-gather.2
where the time goes:
time: 248 us; the launch traced here: 247 us
  local copies, waits for them, and re-layouts  68.2 us (28%)
  matrix products  57.4 us (23%)
  other arithmetic  47.9 us (19%)
  waiting for transfers between devices  46 us (19%)
  between operations  13.8 us (6%)
  starting transfers between devices  13.5 us (5%)
    ppermute x2, waiting for transfers between devices, padded(): lax.ppermute(head, axis, [((i + 1) % count, i) for i in range(ends)])  35 us
    sub x2, other arithmetic, attend(): weights = jnp.exp(scores - row_max)  34.6 us
    convert_element_type x4, local copies, waits for them, and re-layouts, attend(): mixed_out.reshape(batches, query_count, features).astype(jnp.bfloat16)  21.4 us
    dot_general x2, matrix products, attend(): jnp.einsum('bqhd,bkhd->bhqk', q_heads, k_heads, preferred_element_type=jn...  19.7 us
    dot_general x2, matrix products, attend(): jnp.einsum('bhqk,bkhd->bqhd', weights, v_heads, preferred_element_type=jn...  16.2 us
    dot_general x3, matrix products, residual(): jnp.dot(update, weight, preferred_element_type=jnp.float32)  14.7 us
    another operation x2, local copies, waits for them, and re-layouts, attend(): q_heads = queries.reshape(batches, query_count, head_count, head_dim)  11.4 us
    ppermute x2, waiting for transfers between devices, padded(): lax.ppermute(tail, axis, [(i, (i + 1) % count) for i in range(ends)])  11 us
  transfers between devices with their start and end apart: 5, of which 3 were waited for; matrix products, arithmetic and copies ran while one was open for 37% of the time, Pallas kernels for 0%

commit v1 on v0

v1 whole, which is shorter than its diff:
```python
import math

import jax
import jax.numpy as jnp
from jax import lax
from jax.experimental import pallas as pl
from jax.experimental.pallas import tpu as pltpu
from jax.sharding import PartitionSpec as P

HEADS = 8
BX = 8
BY = 8
HALF = BX // 2
LOG2E = math.log2(math.e)

epsilon = 1e-05
mask_depth = 30.0

F32 = jnp.float32
BF16 = jnp.bfloat16


def dot(a, b):
    return jnp.dot(a, b, preferred_element_type=F32)


def dot_nt(a, b):
    return lax.dot_general(a, b, (((1,), (1,)), ((), ())), preferred_element_type=F32)


def layer_norm(widened, gain_vec):
    centre = widened - jnp.mean(widened, axis=-1, keepdims=True)
    spread = jnp.mean(centre * centre, axis=-1, keepdims=True)
    return centre * lax.rsqrt(spread + epsilon) * gain_vec


def gelu(v):
    inner = v * (v * v * (math.sqrt(2 / math.pi) * 0.044715) + math.sqrt(2 / math.pi))
    half = 0.5 * v
    return half * jnp.tanh(inner) + half


def granules(block):
    wide = block.astype(F32)
    frames, rows, cols, features = wide.shape
    return [
        wide[:, :, j * BY : (j + 1) * BY].reshape(frames * rows * BY, features)
        for j in range(cols // BY)
    ]


def attend(q, k, v, bias):
    count, features = q.shape
    keys = k.shape[0]
    lane = lax.broadcasted_iota(jnp.int32, (count, 128), 1)
    low = lane < 64
    ones = jnp.ones((keys, 128), BF16)
    zero = jnp.zeros((count, 128), BF16)
    outs = []
    for p in range(features // 128):
        cols = slice(p * 128, p * 128 + 128)
        qp = q[:, cols]
        both = jnp.concatenate([jnp.where(low, qp, zero), jnp.where(low, zero, qp)], axis=0)
        scores = dot_nt(both, k[:, cols])
        if bias is not None:
            scores = scores + bias
        top = jnp.max(scores, axis=-1, keepdims=True)
        weights = jnp.exp2(scores - top).astype(BF16)
        mixed = dot(weights, jnp.concatenate([v[:, cols], ones], axis=1))
        num = jnp.where(low, mixed[:count, :128], mixed[count:, :128])
        den = jnp.where(low, mixed[:count, 128:], mixed[count:, 128:])
        outs.append((num / den).astype(BF16))
    return jnp.concatenate(outs, axis=1)


def finish_self(base, mixed, wo_ref, gain_cross, cwq_ref, first_ref, cq_ref):
    first = (base + dot(mixed, wo_ref[...])).astype(BF16)
    first_ref[...] = first.reshape(first_ref.shape)
    normed = layer_norm(first.astype(F32), gain_cross).astype(BF16)
    scale = LOG2E / 8.0
    cq_ref[...] = (dot(normed, cwq_ref[...]) * scale).astype(BF16).reshape(cq_ref.shape)


def inner_kernel(
    xa_ref, xb_ref, bias_ref, gs_ref, gc_ref, wq_ref, wkv_ref, wo_ref, cwq_ref, first_ref, cq_ref
):
    i = pl.program_id(0)
    features = wq_ref.shape[0]
    ga = granules(xa_ref[...])
    gb = granules(xb_ref[...])
    base = jnp.concatenate(ga + gb, axis=0)
    rows = ga[0].shape[0]
    normed = layer_norm(base, gs_ref[...]).astype(BF16)
    q = (dot(normed, wq_ref[...]) * (LOG2E / 8.0)).astype(BF16)
    kv = dot(normed, wkv_ref[...]).astype(BF16)
    parts = [None] * 4
    for j in range(2):
        def pick(a):
            return jnp.concatenate(
                [a[j * rows : (j + 1) * rows], a[(2 + j) * rows : (3 + j) * rows]], axis=0
            )

        bias = jnp.concatenate([bias_ref[2 + 2 * i, j], bias_ref[3 + 2 * i, j]], axis=1)
        kvj = pick(kv)
        mixed = attend(pick(q), kvj[:, :features], kvj[:, features:], bias)
        parts[j] = mixed[:rows]
        parts[2 + j] = mixed[rows:]
    finish_self(
        base, jnp.concatenate(parts, axis=0), wo_ref, gc_ref[...], cwq_ref, first_ref, cq_ref
    )


def edge_kernel(
    meta_ref,
    x_ref,
    pa_ref,
    pb_ref,
    bias_ref,
    gs_ref,
    gc_ref,
    wq_ref,
    wkv_ref,
    wo_ref,
    cwq_ref,
    first_in,
    cq_in,
    first_ref,
    cq_ref,
):
    del first_in, cq_in
    i = pl.program_id(0)
    features = wq_ref.shape[0]
    strip = meta_ref[0]
    from_row = ((strip + i) % 2) == 1
    outside = jnp.where(i == 0, strip == 0, strip == meta_ref[3] - 1)
    halo_block = jnp.where(from_row, pa_ref[...], pb_ref[...]).reshape(x_ref.shape)
    gh = granules(halo_block)
    go = granules(x_ref[...])
    rows = go[0].shape[0]
    keep = jnp.where(outside, 0.0, 1.0)
    own = jnp.concatenate(go, axis=0)
    normed_own = layer_norm(own, gs_ref[...]).astype(BF16)
    normed_halo = (layer_norm(jnp.concatenate(gh, axis=0), gs_ref[...]) * keep).astype(BF16)
    q = (dot(normed_own, wq_ref[...]) * (LOG2E / 8.0)).astype(BF16)
    kv = dot(jnp.concatenate([normed_halo, normed_own], axis=0), wkv_ref[...]).astype(BF16)
    parts = []
    for j in range(2):
        bias = jnp.concatenate([bias_ref[7 * i, j], bias_ref[1 + 5 * i, j]], axis=1)
        kvj = jnp.concatenate(
            [kv[j * rows : (j + 1) * rows], kv[(2 + j) * rows : (3 + j) * rows]], axis=0
        )
        parts.append(
            attend(q[j * rows : (j + 1) * rows], kvj[:, :features], kvj[:, features:], bias)
        )
    finish_self(
        own, jnp.concatenate(parts, axis=0), wo_ref, gc_ref[...], cwq_ref, first_ref, cq_ref
    )


def cross_kernel(
    meta_ref,
    list_ref,
    fa_ref,
    fb_ref,
    qa_ref,
    qb_ref,
    mine_ref,
    other_ref,
    ckv_ref,
    cwo_ref,
    gf_ref,
    fin_ref,
    fout_ref,
    out_ref,
):
    k = pl.program_id(0)
    strip, side, core = meta_ref[0], meta_ref[1], meta_ref[2]
    features = cwo_ref.shape[0]
    rows = fa_ref.shape[2]

    def entry(j, l):
        e = list_ref[(k * 2 + j) * 4 + l]
        delta = e // 8 - strip
        column = e % 8
        e_side, e_core, sub = column // 4, (column // 2) % 2, column % 2
        toward_row = jnp.where(strip % 2 == 0, 1, -1)
        slot = jnp.where(delta == 0, 0, jnp.where(delta == toward_row, 2, 4))
        slot = slot + jnp.where(e_side == side, 0, 1)
        place = slot * 2 + sub
        return jnp.where(e_core == core, mine_ref[place], other_ref[place])

    mixed = []
    for j in range(2):
        chosen = jnp.concatenate([entry(j, l) for l in range(4)], axis=0)
        kv = dot(chosen, ckv_ref[...]).astype(BF16)
        q = jnp.concatenate([qa_ref[0, j], qb_ref[0, j]], axis=0)
        mixed.append(attend(q, kv[:, :features], kv[:, features:], None))
    mixed = jnp.concatenate(mixed, axis=0)
    first = jnp.concatenate([fa_ref[0, 0], fb_ref[0, 0], fa_ref[0, 1], fb_ref[0, 1]], axis=0)
    second = (first.astype(F32) + dot(mixed, cwo_ref[...])).astype(BF16).astype(F32)
    normed = layer_norm(second, gf_ref[...]).astype(BF16)
    total = second
    hidden_units = fin_ref.shape[1]
    step = 512
    for c in range(0, hidden_units, step):
        hidden = gelu(dot(normed, fin_ref[:, c : c + step])).astype(BF16)
        total = total + dot(hidden, fout_ref[c : c + step, :])
    frames = out_ref.shape[0]
    shaped = total.reshape(2, 2, frames, HALF, BY, features)
    cols = jnp.concatenate([shaped[0], shaped[1]], axis=3).astype(BF16)
    out_ref[:, :HALF] = cols[0]
    out_ref[:, HALF:] = cols[1]


def whole(shape):
    return pl.BlockSpec(shape, lambda *_: (0,) * len(shape), pipeline_mode=pl.Buffered(1))


def pairs(strips, target):
    out = []
    for s in range(strips):
        for h in range(2):
            for c in range(2):
                s2, h2, c2 = target(s, h, c)
                out.append((s * 4 + h * 2 + c, s2 * 4 + h2 * 2 + c2))
    return out


def shards(
    inputs,
    coverage,
    encoded,
    cross_list,
    gain_self,
    gain_cross,
    gain_ffn,
    self_wq,
    self_wkv,
    self_wo,
    cross_wq,
    cross_wkv,
    cross_wo,
    ffn_in,
    ffn_out,
):
    frames, row_count, col_count, features = inputs.shape
    strips = lax.axis_size("gx")
    strip = lax.axis_index("gx")
    place = lax.axis_index("gy")
    meta = jnp.stack([strip, place // 2, place % 2, strips]).astype(jnp.int32)

    def across(s):
        far = s + 1 if s % 2 else s - 1
        return far if 0 <= far < strips else s

    def send(array, target):
        return lax.ppermute(array, ("gx", "gy"), pairs(strips, target))

    halo_tokens = frames * HALF * col_count
    piece = encoded.reshape(-1, features)
    tail = inputs[:, row_count - HALF :].reshape(halo_tokens, features)
    head = inputs[:, :HALF].reshape(halo_tokens, features)
    even = strip % 2 == 0
    to_row = jnp.concatenate([jnp.where(even, tail, head), piece], axis=0)
    to_across = jnp.concatenate([jnp.where(even, head, tail), piece], axis=0)
    got_row = send(to_row, lambda s, h, c: (s ^ 1, h, c))
    got_across = send(to_across, lambda s, h, c: (across(s), h, c))
    got_side = send(piece, lambda s, h, c: (s, 1 - h, c))
    got_row_side = send(piece, lambda s, h, c: (s ^ 1, 1 - h, c))
    got_across_side = send(piece, lambda s, h, c: (across(s), 1 - h, c))

    cover = jnp.pad(coverage.astype(F32), ((HALF, HALF), (0, 0)))
    cover = lax.dynamic_slice_in_dim(cover, strip * row_count, row_count + 2 * HALF, 0)
    quads = cover.shape[0] // HALF
    bias = (cover - 1.0) * (mask_depth * LOG2E)
    bias = bias.reshape(quads, 1, HALF, col_count // BY, BY).transpose(0, 3, 1, 2, 4)
    bias = jnp.broadcast_to(bias, (quads, col_count // BY, frames, HALF, BY))
    bias = bias.reshape(quads, col_count // BY, 1, frames * HALF * BY)

    gs = gain_self.reshape(1, features)
    gc = gain_cross.reshape(1, features)
    gf = gain_ffn.reshape(1, features)
    rows = frames * HALF * BY
    hidden_units = ffn_in.shape[1]
    quad_block = (frames, HALF, col_count, features)
    state = jax.ShapeDtypeStruct((6, 2, rows, features), BF16)
    params = pltpu.CompilerParams(vmem_limit_bytes=48 << 20)
    small = [
        whole((quads, 2, 1, rows)),
        whole((1, features)),
        whole((1, features)),
        whole((features, features)),
        whole((features, 2 * features)),
        whole((features, features)),
        whole((features, features)),
    ]
    small_args = (bias, gs, gc, self_wq, self_wkv, self_wo, cross_wq)

    first, cq = pl.pallas_call(
        inner_kernel,
        grid=(2,),
        in_specs=[
            pl.BlockSpec(quad_block, lambda i: (0, 1 + 2 * i, 0, 0)),
            pl.BlockSpec(quad_block, lambda i: (0, 2 + 2 * i, 0, 0)),
            *small,
        ],
        out_specs=[pl.BlockSpec((2, 2, rows, features), lambda i: (i, 0, 0, 0))] * 2,
        out_shape=[state, state],
        compiler_params=params,
        cost_estimate=pl.CostEstimate(flops=10 << 30, bytes_accessed=8 << 20, transcendentals=0),
    )(inputs, inputs, *small_args)

    edge_blocks = [pl.BlockSpec((1, 2, rows, features), lambda i: (4 + i, 0, 0, 0))] * 2
    first, cq = pl.pallas_call(
        edge_kernel,
        grid=(2,),
        in_specs=[
            pl.BlockSpec(memory_space=pltpu.SMEM),
            pl.BlockSpec(quad_block, lambda i: (0, 5 * i, 0, 0)),
            whole((halo_tokens, features)),
            whole((halo_tokens, features)),
            *small,
            pl.BlockSpec(memory_space=pl.ANY),
            pl.BlockSpec(memory_space=pl.ANY),
        ],
        out_specs=edge_blocks,
        out_shape=[state, state],
        input_output_aliases={11: 0, 12: 1},
        compiler_params=params,
        cost_estimate=pl.CostEstimate(flops=6 << 30, bytes_accessed=8 << 20, transcendentals=0),
    )(meta, inputs, got_row, got_across, *small_args, first, cq)

    mine = jnp.concatenate(
        [
            piece,
            got_side,
            got_row[halo_tokens:],
            got_row_side,
            got_across[halo_tokens:],
            got_across_side,
        ],
        axis=0,
    )
    other = send(mine, lambda s, h, c: (s, h, 1 - c))
    tokens = encoded.shape[2]
    window = (mine.shape[0] // tokens, tokens, features)
    lower = pl.BlockSpec((1, 2, rows, features), lambda k: (jnp.where(k == 0, 4, 2 * k - 1), 0, 0, 0))
    upper = pl.BlockSpec((1, 2, rows, features), lambda k: (jnp.where(k == 2, 5, 2 * k), 0, 0, 0))
    return pl.pallas_call(
        cross_kernel,
        grid=(3,),
        in_specs=[
            pl.BlockSpec(memory_space=pltpu.SMEM),
            pl.BlockSpec(memory_space=pltpu.SMEM),
            lower,
            upper,
            lower,
            upper,
            whole(window),
            whole(window),
            whole((features, 2 * features)),
            whole((features, features)),
            whole((1, features)),
            whole((features, hidden_units)),
            whole((hidden_units, features)),
        ],
        out_specs=pl.BlockSpec((frames, BX, col_count, features), lambda k: (0, k, 0, 0)),
        out_shape=jax.ShapeDtypeStruct(inputs.shape, BF16),
        compiler_params=params,
        cost_estimate=pl.CostEstimate(flops=20 << 30, bytes_accessed=16 << 20, transcendentals=0),
    )(
        meta,
        cross_list.reshape(-1),
        first,
        first,
        cq,
        cq,
        mine.reshape(window),
        other.reshape(window),
        cross_wkv,
        cross_wo,
        gf,
        ffn_in,
        ffn_out,
    )


def solution(mesh):
    return jax.shard_map(
        shards,
        mesh=mesh,
        in_specs=(
            P(None, "gx", "gy", None),
            P(None, "gy"),
            P("gx", "gy", None, None),
            P("gx", "gy", None),
            P(),
            P(),
            P(),
            P(),
            P(),
            P(),
            P(),
            P(),
            P(),
            P(),
            P(),
        ),
        out_specs=P(None, "gx", "gy", None),
        check_vma=False,
    )
```

time: 248 us -> 76.9 us (0.31)
  the two profiles are of different devices: /device:TPU:148 before, /device:TPU:1 now
where the time goes in v1:
time: 76.9 us; the launch traced here: 76.4 us
  Pallas kernels  34 us (44%)
  waiting for transfers between devices  18.8 us (24%)
  local copies, waits for them, and re-layouts  10.5 us (14%)
  starting transfers between devices  9.68 us (13%)
  other arithmetic  3.2 us (4%)
    pallas_call x1, Pallas kernels, shards(): pl.pallas_call(cross_kernel, grid=(3,), in_specs=[pl.BlockSpec(memory_spa...  19.3 us
    ppermute x6, waiting for transfers between devices, send(): return lax.ppermute(array, ('gx', 'gy'), pairs(strips, target))  18.8 us
    unnamed x41, local copies, waits for them, and re-layouts  10.1 us
    ppermute x6, starting transfers between devices, send(): return lax.ppermute(array, ('gx', 'gy'), pairs(strips, target))  9.68 us
    pallas_call x1, Pallas kernels, shards(): pl.pallas_call(inner_kernel, grid=(2,), in_specs=[pl.BlockSpec(quad_block...  7.88 us
    pallas_call x1, Pallas kernels, shards(): pl.pallas_call(edge_kernel, grid=(2,), in_specs=[pl.BlockSpec(memory_spac...  6.85 us
    concatenate x1, other arithmetic, shards(): to_across = jnp.concatenate([jnp.where(even, head, tail), piece], axis=0)  1.92 us
  transfers between devices with their start and end apart: 6, of which 2 were waited for; matrix products, arithmetic and copies ran while one was open for 1% of the time, Pallas kernels for 19%

profile of v1, /device:TPU:1, one launch (start us, length us, event | category | flops | bytes accessed | tf_op | source)
XLA Modules:
  0.0 76.4 jit_solution(9437376476671958658)
XLA Ops:
  0.0 0.0 copy-start.15
  0.0 0.0 copy-start.16
  0.0 1.1 %broadcast_select_fusion = (bf16[4,4,16,512]{3,2,1,0:T(8,128)(2,1)S(1)}, bf16[4,4,16,512]{3,2,1,0:T(8,128)(2,1)S(1)}) fusion(pred[]{:T(512)S(6)} %eq.6, bf16[4,24,16,512]{3,2,1,0:T(8,128)(2,1)} %x_ref.1), kind=kLoop, calls=%fused_computation.2 | loop fusion | flops 262144 | bytes 1048577 | tf_op jit(solution)/shard_map/jit(_where)/select_n | solution.py:265
  1.1 0.0 copy-start
  1.1 0.0 copy-start.9
  1.1 0.0 copy-start.10
  1.2 1.9 %pad_maximum_fusion = (bf16[384,512]{1,0:T(8,128)(2,1)}, bf16[384,512]{1,0:T(8,128)(2,1)}) fusion(bf16[128,512]{1,0:T(8,128)(2,1)} %bitcast.23, bf16[256,512]{1,0:T(8,128)(2,1)S(1)} %bitcast.21, bf16[256,512]{1,0:T(8,128)(2,1)S(1)} %bitcast.22), kind=kLoop, calls=%fused_computation | loop fusion | flops 1376256 | bytes 1441792 | tf_op jit(solution)/shard_map/concatenate | solution.py:265
  3.1 2.0 %collective-permute-start = (bf16[384,512]{1,0:T(8,128)(2,1)}, bf16[384,512]{1,0:T(8,128)(2,1)S(1)}, u32[]{:S(2)}, u32[]{:S(2)}) collective-permute-start(bf16[384,512]{1,0:T(8,128)(2,1)} %get-tuple-element.16), channel_id=1, source_target_pairs={{0,4},{1,5},{2,6},{3,7},{4,0},{5,1},{6,2},{7,3},{8,12},{9,13},{10,... | collective-permute-start | bytes 1179656 | tf_op jit(solution)/shard_map/ppermute | solution.py:257
  5.1 0.0 copy-done.15
  5.1 2.5 %collective-permute-start.2 = (bf16[128,512]{1,0:T(8,128)(2,1)S(1)}, bf16[128,512]{1,0:T(8,128)(2,1)S(1)}, u32[]{:S(2)}, u32[]{:S(2)}) collective-permute-start(bf16[128,512]{1,0:T(8,128)(2,1)S(1)} %bitcast.24), channel_id=1, source_target_pairs={{0,2},{1,3},{2,0},{3,1},{4,6},{5,7},{6,4},{7,5},{8,10},{9,11},{10,... | collective-permute-start | bytes 393224 | tf_op jit(solution)/shard_map/ppermute | solution.py:257
  7.6 0.0 collective-permute-start.3
  7.6 1.7 %collective-permute-start.4 = (bf16[128,512]{1,0:T(8,128)(2,1)S(1)}, bf16[128,512]{1,0:T(8,128)(2,1)S(1)}, u32[]{:S(2)}, u32[]{:S(2)}) collective-permute-start(bf16[128,512]{1,0:T(8,128)(2,1)S(1)} %bitcast.26), channel_id=1, source_target_pairs={{0,2},{1,3},{2,0},{3,1},{4,10},{5,11},{6,8},{7,9},{8,6},{9,7},{10,... | collective-permute-start | bytes 393224 | tf_op jit(solution)/shard_map/ppermute | solution.py:257
  9.3 1.6 %collective-permute-start.1 = (bf16[384,512]{1,0:T(8,128)(2,1)}, bf16[384,512]{1,0:T(8,128)(2,1)S(1)}, u32[]{:S(2)}, u32[]{:S(2)}) collective-permute-start(bf16[384,512]{1,0:T(8,128)(2,1)} %get-tuple-element.15), channel_id=1, source_target_pairs={{0,0},{1,1},{2,2},{3,3},{4,8},{5,9},{6,10},{7,11},{8,4},{9,5},{10,... | collective-permute-start | bytes 1179656 | tf_op jit(solution)/shard_map/ppermute | solution.py:257
  10.9 0.0 copy-done.16
  11.0 0.1 fusion.1
  11.0 0.1 copy.19
  11.1 0.1 reshape.35
  11.3 0.2 reshape.36.bias_ref
  11.4 7.7 %collective-permute-done.2 = bf16[128,512]{1,0:T(8,128)(2,1)S(1)} collective-permute-done((bf16[128,512]{1,0:T(8,128)(2,1)S(1)}, bf16[128,512]{1,0:T(8,128)(2,1)S(1)}, u32[]{:S(2)}, u32[]{:S(2)}) %collective-permute-start.2) | collective-permute-done | bytes 131104 | tf_op jit(solution)/shard_map/ppermute | solution.py:257
  19.1 0.0 collective-permute-done.pa_ref
  19.1 0.0 collective-permute-done.3
  19.2 0.0 collective-permute-done.1.pb_ref
  19.2 11.1 %collective-permute-done.4 = bf16[128,512]{1,0:T(8,128)(2,1)S(1)} collective-permute-done((bf16[128,512]{1,0:T(8,128)(2,1)S(1)}, bf16[128,512]{1,0:T(8,128)(2,1)S(1)}, u32[]{:S(2)}, u32[]{:S(2)}) %collective-permute-start.4) | collective-permute-done | bytes 131104 | tf_op jit(solution)/shard_map/ppermute | solution.py:257
  30.3 1.8 %collective-permute-start.5 = (bf16[768,512]{1,0:T(8,128)(2,1)S(1)}, bf16[768,512]{1,0:T(8,128)(2,1)S(1)}, u32[]{:S(2)}, u32[]{:S(2)}) collective-permute-start(bf16[768,512]{1,0:T(8,128)(2,1)S(1)} %constant_dynamic-update-slice_fusion), channel_id=1, source_target_pairs={{0,1},{1,0},{2,3},{3,2},{4,5},{5,4},{6,7},{7,6},{8,9},{9,8},{10,11... | collective-permute-start | bytes 2359304 | tf_op jit(solution)/shard_map/ppermute | solution.py:257
  32.2 0.0 copy-done
  32.2 0.0 copy-done.9
  32.2 0.0 copy-done.10
  32.2 0.0 copy-start.2
  32.2 1.0 %copy-done.2 = bf16[512,512]{1,0:T(8,128)(2,1)S(1)} copy-done((bf16[512,512]{1,0:T(8,128)(2,1)S(1)}, bf16[512,512]{1,0:T(8,128)(2,1)}, u32[]{:S(2)}) %copy-start.2) | copy-done | bytes 524312
  33.2 1.0 %copy-done.4 = bf16[512,512]{1,0:T(8,128)(2,1)S(1)} copy-done((bf16[512,512]{1,0:T(8,128)(2,1)S(1)}, bf16[512,512]{1,0:T(8,128)(2,1)}, u32[]{:S(2)}) %copy-start.4) | copy-done | bytes 524312
  34.3 1.0 %copy-done.6 = bf16[512,512]{1,0:T(8,128)(2,1)S(1)} copy-done((bf16[512,512]{1,0:T(8,128)(2,1)S(1)}, bf16[512,512]{1,0:T(8,128)(2,1)}, u32[]{:S(2)}) %copy-start.6) | copy-done | bytes 524312
  35.3 7.9 %shard_map.145 = (bf16[6,2,128,512]{3,2,1,0:T(8,128)(2,1)S(1)}, bf16[6,2,128,512]{3,2,1,0:T(8,128)(2,1)S(1)}) custom-call(bf16[4,24,16,512]{3,2,1,0:T(8,128)(2,1)} %x_ref.1, bf16[4,24,16,512]{3,2,1,0:T(8,128)(2,1)} %x_ref.1, f32[8,2,1,128]{3,2,1,0:T(1,128)S(1)} %reshape.36.bias_ref, f32[1,512]{1,0:T(1,128)S(1)} %bitcast.16, f32[1,512]{1,0:T(1,128)S(1)} %bitcast.18, ...), custom_call_target="tpu_custom_call" | custom-call | flops 10737418240 | bytes 8388608 | tf_op jit(solution)/shard_map/pallas_call | solution.py:299
  43.2 0.0 copy-start.12
  43.2 1.1 %copy-done.12 = bf16[6,2,128,512]{3,2,1,0:T(8,128)(2,1)} copy-done((bf16[6,2,128,512]{3,2,1,0:T(8,128)(2,1)}, bf16[6,2,128,512]{3,2,1,0:T(8,128)(2,1)S(1)}, u32[]{:S(2)}) %copy-start.12) | copy-done | bytes 1572888
  44.3 1.2 %copy-done.14 = bf16[6,2,128,512]{3,2,1,0:T(8,128)(2,1)} copy-done((bf16[6,2,128,512]{3,2,1,0:T(8,128)(2,1)}, bf16[6,2,128,512]{3,2,1,0:T(8,128)(2,1)S(1)}, u32[]{:S(2)}) %copy-start.14) | copy-done | bytes 1572888
  45.5 0.0 copy-done.17
  45.5 0.1 reshape.33.list_ref
  45.6 0.1 pad_add_fusion.meta_ref
  45.7 1.0 %copy-done.3 = bf16[512,512]{1,0:T(8,128)(2,1)S(1)} copy-done((bf16[512,512]{1,0:T(8,128)(2,1)S(1)}, bf16[512,512]{1,0:T(8,128)(2,1)}, u32[]{:S(2)}) %copy-start.3) | copy-done | bytes 524312
  46.7 1.0 %copy-done.5 = bf16[512,512]{1,0:T(8,128)(2,1)S(1)} copy-done((bf16[512,512]{1,0:T(8,128)(2,1)S(1)}, bf16[512,512]{1,0:T(8,128)(2,1)}, u32[]{:S(2)}) %copy-start.5) | copy-done | bytes 524312
  47.8 1.0 %copy-done.7 = bf16[512,512]{1,0:T(8,128)(2,1)S(1)} copy-done((bf16[512,512]{1,0:T(8,128)(2,1)S(1)}, bf16[512,512]{1,0:T(8,128)(2,1)}, u32[]{:S(2)}) %copy-start.7) | copy-done | bytes 524312
  48.8 1.4 %copy-done.13 = bf16[6,2,128,512]{3,2,1,0:T(8,128)(2,1)S(1)} copy-done((bf16[6,2,128,512]{3,2,1,0:T(8,128)(2,1)S(1)}, bf16[6,2,128,512]{3,2,1,0:T(8,128)(2,1)}, u32[]{:S(2)}) %copy-start.13) | copy-done | bytes 1572888
  50.2 6.9 %shard_map.146 = (bf16[6,2,128,512]{3,2,1,0:T(8,128)(2,1)S(1)}, bf16[6,2,128,512]{3,2,1,0:T(8,128)(2,1)}) custom-call(s32[4]{0:T(128)S(1)} %pad_add_fusion.meta_ref, bf16[4,24,16,512]{3,2,1,0:T(8,128)(2,1)} %x_ref.1, bf16[384,512]{1,0:T(8,128)(2,1)S(1)} %collective-permute-done.pa_ref, ...), custom_call_target="tpu_custom_call", output_to_operand_aliasing={{0}: (11, {}), {1}: (12, {})} | custom-call | flops 6442450944 | bytes 8388608 | tf_op jit(solution)/shard_map/pallas_call | solution.py:314
  57.1 0.0 collective-permute-done.5
  57.1 0.0 copy-done.1
  57.1 0.0 copy-done.8
  57.1 0.0 copy-done.11
  57.1 19.3 %shard_map.147 = bf16[4,24,16,512]{3,2,1,0:T(8,128)(2,1)} custom-call(s32[4]{0:T(128)S(1)} %pad_add_fusion.meta_ref, s32[24]{0:T(128)S(1)} %reshape.33.list_ref, bf16[6,2,128,512]{3,2,1,0:T(8,128)(2,1)S(1)} %get-tuple-element.11.fa_ref.fb_ref, bf16[6,2,128,512]{3,2,1,0:T(8,128)(2,1)S(1)} %get-tuple-element.11.fa_ref.fb_ref, ...), custom_call_target="tpu_custom_call" | custom-call | flops 21474836480 | bytes 16777216 | tf_op jit(solution)/shard_map/pallas_call | solution.py:349
  (20 shorter events, 0.1 us)
Async XLA Ops:
  0.0 5.1 %copy-start.15 = (bf16[1,2,64,512]{3,2,1,0:T(8,128)(2,1)S(1)}, bf16[1,2,64,512]{3,2,1,0:T(8,128)(2,1)}, u32[]{:S(2)}) copy-start(bf16[1,2,64,512]{3,2,1,0:T(8,128)(2,1)} %param.17) | copy-start | bytes 393220
  0.0 10.9 %copy-start.16 = (s32[1536,16]{0,1:T(8,128)S(1)}, s32[1536,16]{0,1:T(8,128)}, u32[]{:S(2)}) copy-start(s32[1536,16]{0,1:T(8,128)} %param.16) | copy-start | bytes 294916
  1.1 31.0 %copy-start = (bf16[512,1024]{1,0:T(8,128)(2,1)S(1)}, bf16[512,1024]{1,0:T(8,128)(2,1)}, u32[]{:S(2)}) copy-start(bf16[512,1024]{1,0:T(8,128)(2,1)} %wkv_ref.3) | copy-start | bytes 3145732
  1.1 31.0 %copy-start.9 = (f32[512]{0:T(512)S(1)}, f32[512]{0:T(512)}, u32[]{:S(2)}) copy-start(f32[512]{0:T(512)} %param.19) | copy-start | bytes 6148
  1.1 31.0 %copy-start.10 = (f32[512]{0:T(512)S(1)}, f32[512]{0:T(512)}, u32[]{:S(2)}) copy-start(f32[512]{0:T(512)} %param.20) | copy-start | bytes 6148
  3.1 16.0 %collective-permute-start = (bf16[384,512]{1,0:T(8,128)(2,1)}, bf16[384,512]{1,0:T(8,128)(2,1)S(1)}, u32[]{:S(2)}, u32[]{:S(2)}) collective-permute-start(bf16[384,512]{1,0:T(8,128)(2,1)} %get-tuple-element.16), channel_id=1, source_target_pairs={{0,4},{1,5},{2,6},{3,7},{4,0},{5,1},{6,2},{7,3},{8,12},{9,13},{10,... | collective-permute-start | bytes 1179656 | tf_op jit(solution)/shard_map/ppermute | solution.py:257
  5.1 14.0 %collective-permute-start.2 = (bf16[128,512]{1,0:T(8,128)(2,1)S(1)}, bf16[128,512]{1,0:T(8,128)(2,1)S(1)}, u32[]{:S(2)}, u32[]{:S(2)}) collective-permute-start(bf16[128,512]{1,0:T(8,128)(2,1)S(1)} %bitcast.24), channel_id=1, source_target_pairs={{0,2},{1,3},{2,0},{3,1},{4,6},{5,7},{6,4},{7,5},{8,10},{9,11},{10,... | collective-permute-start | bytes 393224 | tf_op jit(solution)/shard_map/ppermute | solution.py:257
  7.6 11.6 %collective-permute-start.3 = (bf16[128,512]{1,0:T(8,128)(2,1)S(1)}, bf16[128,512]{1,0:T(8,128)(2,1)S(1)}, u32[]{:S(2)}, u32[]{:S(2)}) collective-permute-start(bf16[128,512]{1,0:T(8,128)(2,1)S(1)} %bitcast.25), channel_id=1, source_target_pairs={{0,6},{1,7},{2,4},{3,5},{4,2},{5,3},{6,0},{7,1},{8,14},{9,15},{10,... | collective-permute-start | bytes 393224 | tf_op jit(solution)/shard_map/ppermute | solution.py:257
  7.6 22.8 %collective-permute-start.4 = (bf16[128,512]{1,0:T(8,128)(2,1)S(1)}, bf16[128,512]{1,0:T(8,128)(2,1)S(1)}, u32[]{:S(2)}, u32[]{:S(2)}) collective-permute-start(bf16[128,512]{1,0:T(8,128)(2,1)S(1)} %bitcast.26), channel_id=1, source_target_pairs={{0,2},{1,3},{2,0},{3,1},{4,10},{5,11},{6,8},{7,9},{8,6},{9,7},{10,... | collective-permute-start | bytes 393224 | tf_op jit(solution)/shard_map/ppermute | solution.py:257
  9.3 9.9 %collective-permute-start.1 = (bf16[384,512]{1,0:T(8,128)(2,1)}, bf16[384,512]{1,0:T(8,128)(2,1)S(1)}, u32[]{:S(2)}, u32[]{:S(2)}) collective-permute-start(bf16[384,512]{1,0:T(8,128)(2,1)} %get-tuple-element.15), channel_id=1, source_target_pairs={{0,0},{1,1},{2,2},{3,3},{4,8},{5,9},{6,10},{7,11},{8,4},{9,5},{10,... | collective-permute-start | bytes 1179656 | tf_op jit(solution)/shard_map/ppermute | solution.py:257
  30.3 26.7 %collective-permute-start.5 = (bf16[768,512]{1,0:T(8,128)(2,1)S(1)}, bf16[768,512]{1,0:T(8,128)(2,1)S(1)}, u32[]{:S(2)}, u32[]{:S(2)}) collective-permute-start(bf16[768,512]{1,0:T(8,128)(2,1)S(1)} %constant_dynamic-update-slice_fusion), channel_id=1, source_target_pairs={{0,1},{1,0},{2,3},{3,2},{4,5},{5,4},{6,7},{7,6},{8,9},{9,8},{10,11... | collective-permute-start | bytes 2359304 | tf_op jit(solution)/shard_map/ppermute | solution.py:257
  32.2 1.0 %copy-start.2 = (bf16[512,512]{1,0:T(8,128)(2,1)S(1)}, bf16[512,512]{1,0:T(8,128)(2,1)}, u32[]{:S(2)}) copy-start(bf16[512,512]{1,0:T(8,128)(2,1)} %wq_ref.3) | copy-start | bytes 1572868
  33.2 1.0 %copy-start.4 = (bf16[512,512]{1,0:T(8,128)(2,1)S(1)}, bf16[512,512]{1,0:T(8,128)(2,1)}, u32[]{:S(2)}) copy-start(bf16[512,512]{1,0:T(8,128)(2,1)} %wo_ref.3) | copy-start | bytes 1572868
  34.3 1.0 %copy-start.6 = (bf16[512,512]{1,0:T(8,128)(2,1)S(1)}, bf16[512,512]{1,0:T(8,128)(2,1)}, u32[]{:S(2)}) copy-start(bf16[512,512]{1,0:T(8,128)(2,1)} %cwq_ref.3) | copy-start | bytes 1572868
  35.3 10.2 %copy-start.17 = (s32[3,2,4]{2,1,0:T(2,128)S(1)}, s32[3,2,4]{2,1,0:T(2,128)}, u32[]{:S(2)}) copy-start(s32[3,2,4]{2,1,0:T(2,128)} %param.18) | copy-start | bytes 292
  43.2 1.1 %copy-start.12 = (bf16[6,2,128,512]{3,2,1,0:T(8,128)(2,1)}, bf16[6,2,128,512]{3,2,1,0:T(8,128)(2,1)S(1)}, u32[]{:S(2)}) copy-start(bf16[6,2,128,512]{3,2,1,0:T(8,128)(2,1)S(1)} %get-tuple-element.9.first_in) | copy-start | bytes 4718596
  44.3 1.2 %copy-start.14 = (bf16[6,2,128,512]{3,2,1,0:T(8,128)(2,1)}, bf16[6,2,128,512]{3,2,1,0:T(8,128)(2,1)S(1)}, u32[]{:S(2)}) copy-start(bf16[6,2,128,512]{3,2,1,0:T(8,128)(2,1)S(1)} %get-tuple-element.10.cq_in) | copy-start | bytes 4718596
  45.7 1.0 %copy-start.3 = (bf16[512,512]{1,0:T(8,128)(2,1)S(1)}, bf16[512,512]{1,0:T(8,128)(2,1)}, u32[]{:S(2)}) copy-start(bf16[512,512]{1,0:T(8,128)(2,1)} %wq_ref.3) | copy-start | bytes 1572868
  46.7 1.0 %copy-start.5 = (bf16[512,512]{1,0:T(8,128)(2,1)S(1)}, bf16[512,512]{1,0:T(8,128)(2,1)}, u32[]{:S(2)}) copy-start(bf16[512,512]{1,0:T(8,128)(2,1)} %wo_ref.3) | copy-start | bytes 1572868
  47.8 1.0 %copy-start.7 = (bf16[512,512]{1,0:T(8,128)(2,1)S(1)}, bf16[512,512]{1,0:T(8,128)(2,1)}, u32[]{:S(2)}) copy-start(bf16[512,512]{1,0:T(8,128)(2,1)} %cwq_ref.3) | copy-start | bytes 1572868
  48.8 1.4 %copy-start.13 = (bf16[6,2,128,512]{3,2,1,0:T(8,128)(2,1)S(1)}, bf16[6,2,128,512]{3,2,1,0:T(8,128)(2,1)}, u32[]{:S(2)}) copy-start(bf16[6,2,128,512]{3,2,1,0:T(8,128)(2,1)} %copy-done.12) | copy-start | bytes 4718596
  50.2 6.9 %copy-start.1 = (bf16[512,1024]{1,0:T(8,128)(2,1)S(1)}, bf16[512,1024]{1,0:T(8,128)(2,1)}, u32[]{:S(2)}) copy-start(bf16[512,1024]{1,0:T(8,128)(2,1)} %ckv_ref.1) | copy-start | bytes 3145732
  50.2 6.9 %copy-start.8 = (bf16[512,512]{1,0:T(8,128)(2,1)S(1)}, bf16[512,512]{1,0:T(8,128)(2,1)}, u32[]{:S(2)}) copy-start(bf16[512,512]{1,0:T(8,128)(2,1)} %cwo_ref.1) | copy-start | bytes 1572868
  50.2 6.9 %copy-start.11 = (f32[512]{0:T(512)S(1)}, f32[512]{0:T(512)}, u32[]{:S(2)}) copy-start(f32[512]{0:T(512)} %param.21) | copy-start | bytes 6148

commit v2 on v0

v2 whole, which is shorter than its diff:
```python
import functools
import math

import jax
import jax.numpy as jnp
from jax import lax
from jax.experimental import pallas as pl
from jax.experimental.pallas import tpu as pltpu
from jax.sharding import PartitionSpec as P

HEADS = 8
BX = 8
BY = 8
HALF = BX // 2
LOG2E = math.log2(math.e)

epsilon = 1e-05
mask_depth = 30.0

F32 = jnp.float32
BF16 = jnp.bfloat16


def dot(a, b):
    return jnp.dot(a, b, preferred_element_type=F32)


def dot_nt(a, b):
    return lax.dot_general(a, b, (((1,), (1,)), ((), ())), preferred_element_type=F32)


def layer_norm(widened, gain_vec):
    centre = widened - jnp.mean(widened, axis=-1, keepdims=True)
    spread = jnp.mean(centre * centre, axis=-1, keepdims=True)
    return centre * lax.rsqrt(spread + epsilon) * gain_vec


def gelu(v):
    inner = v * (v * v * (math.sqrt(2 / math.pi) * 0.044715) + math.sqrt(2 / math.pi))
    half = 0.5 * v
    return half * jnp.tanh(inner) + half


def granules(block):
    wide = block.astype(F32)
    frames, rows, cols, features = wide.shape
    return [
        wide[:, :, j * BY : (j + 1) * BY].reshape(frames * rows * BY, features)
        for j in range(cols // BY)
    ]


def attend(q, k, v, bias):
    count, features = q.shape
    keys = k.shape[0]
    lane = lax.broadcasted_iota(jnp.int32, (count, 128), 1)
    low = lane < 64
    ones = jnp.ones((keys, 128), BF16)
    zero = jnp.zeros((count, 128), BF16)
    outs = []
    for p in range(features // 128):
        cols = slice(p * 128, p * 128 + 128)
        qp = q[:, cols]
        both = jnp.concatenate([jnp.where(low, qp, zero), jnp.where(low, zero, qp)], axis=0)
        scores = dot_nt(both, k[:, cols])
        if bias is not None:
            scores = scores + bias
        top = jnp.max(scores, axis=-1, keepdims=True)
        weights = jnp.exp2(scores - top).astype(BF16)
        mixed = dot(weights, jnp.concatenate([v[:, cols], ones], axis=1))
        num = jnp.where(low, mixed[:count, :128], mixed[count:, :128])
        den = jnp.where(low, mixed[:count, 128:], mixed[count:, 128:])
        outs.append((num / den).astype(BF16))
    return jnp.concatenate(outs, axis=1)


def position():
    place = lax.axis_index("gy")
    return lax.axis_index("gx"), place // 2, place % 2


def first_cell(strip, row_count, total, window):
    block = jnp.maximum(strip * row_count - HALF, 0) // 128
    return pl.multiple_of(jnp.minimum(block, (total - window) // 128) * 128, 128)


def bias_rows(cover_ref, first_row, quads):
    cols, cells = cover_ref.shape
    cover = cover_ref[...].astype(BF16)
    key = lax.broadcasted_iota(jnp.int32, (128, cells), 0)
    cell = lax.broadcasted_iota(jnp.int32, (128, cells), 1)
    same_row = (cell % HALF) == (key // BY) % HALF
    line = lax.broadcasted_iota(jnp.int32, (8, cells), 0)
    wanted = jnp.full((8, cells), -9, jnp.int32)
    for n, quad in enumerate(quads):
        wanted = jnp.where(line == n, quad, wanted)
    grid_row = lax.broadcasted_iota(jnp.int32, (8, cells), 1) + first_row
    member = jnp.where(grid_row // HALF == wanted, 1.0, 0.0).astype(BF16)
    spot = lax.broadcasted_iota(jnp.int32, (128, cols), 0)
    col = lax.broadcasted_iota(jnp.int32, (128, cols), 1)
    out = []
    for j in range(cols // BY):
        pick = jnp.where(col == j * BY + spot % BY, 1.0, 0.0).astype(BF16)
        spread = jnp.where(same_row, dot(pick, cover), 0.0).astype(BF16)
        out.append((dot_nt(member, spread) - 1.0) * (mask_depth * LOG2E))
    return out


def copies(sems, moves):
    made = [pltpu.make_async_copy(src, dst, sems.at[n]) for n, (src, dst) in enumerate(moves)]
    for copy in made:
        copy.start()
    return made


def self_kernel(inner, edge, handoff, *refs):
    refs = list(refs)

    def take(count):
        out = refs[:count]
        del refs[:count]
        return out

    x_hbm, cover_hbm, gs_ref, gc_ref, wq_hbm, wkv_hbm, wo_hbm, cwq_hbm = take(8)
    halo_ref = take(1)[0] if edge else None
    piece_hbm = take(1)[0] if handoff else None
    first_hbm, cq_hbm = take(2)
    send_hbm = take(1)[0] if handoff else None
    x_buf, cover_buf, wq_buf, wkv_buf, wo_buf, cwq_buf, first_buf, cq_buf = take(8)
    sems, out_sems = refs

    strip = position()[0]
    even = strip % 2 == 0
    strips = lax.axis_size("gx")
    frames, row_count, cols, features = x_hbm.shape
    per_strip = row_count // HALF
    above = even if edge == "row" else jnp.logical_not(even)
    own_row = jnp.where(above, row_count - HALF, 0)
    start = first_cell(strip, row_count, cover_hbm.shape[1], cover_buf.shape[1])
    inputs = []
    if inner is not None:
        lo = HALF + inner * BX
        inputs.append((x_hbm.at[:, lo : lo + BX], x_buf.at[:, :BX]))
    if edge:
        at = x_buf.shape[1] - HALF
        inputs.append((x_hbm.at[:, pl.ds(own_row, HALF)], x_buf.at[:, at:]))
    tokens_at = len(inputs)
    inputs += [
        (wkv_hbm, wkv_buf),
        (wq_hbm, wq_buf),
        (cover_hbm.at[:, pl.ds(start, cover_buf.shape[1])], cover_buf),
        (wo_hbm, wo_buf),
        (cwq_hbm, cwq_buf),
    ]
    if handoff:
        far_row = jnp.where(even, 0, row_count - HALF)
        inputs.append((x_hbm.at[:, pl.ds(far_row, HALF)], send_hbm.at[:frames]))
        inputs.append((piece_hbm, send_hbm.at[frames:]))
    moves = copies(sems, inputs)
    for move in moves[:tokens_at]:
        move.wait()

    parts, quads, cuboids = [], [], []
    base_quad = strip * per_strip
    if inner is not None:
        for t in range(2):
            parts += granules(x_buf[:, t * HALF : (t + 1) * HALF])
            quads.append(base_quad + 1 + 2 * inner + t)
        cuboids += [((j, 2 + j), (j, 2 + j), (0, 1), j) for j in range(2)]
    if edge:
        n = len(parts)
        parts += granules(x_buf[:, at:])
        quads.append(base_quad + jnp.where(above, per_strip - 1, 0))
    own = len(parts)
    rows = parts[0].shape[0]
    base = jnp.concatenate(parts, axis=0)
    gs = gs_ref[...]
    normed = layer_norm(base, gs).astype(BF16)
    every = normed
    if edge:
        halo = layer_norm(jnp.concatenate(granules(halo_ref[:frames]), axis=0), gs)
        outside = jnp.where(above, strip == strips - 1, strip == 0)
        halo = (halo * jnp.where(outside, 0.0, 1.0)).astype(BF16)
        every = jnp.concatenate([normed, halo], axis=0)
        quads.append(quads[-1] + jnp.where(above, 1, -1))
        q_at = len(quads) - 2
        cuboids += [((n + j, own + j), (n + j,), (q_at, q_at + 1), j) for j in range(2)]
    for move in moves[tokens_at : tokens_at + 5]:
        move.wait()
    bias = bias_rows(cover_buf, start, quads)
    kv = dot(every, wkv_buf[...]).astype(BF16)
    q = (dot(normed, wq_buf[...]) * (LOG2E / 8.0)).astype(BF16)

    def pick(a, which):
        return jnp.concatenate([a[n * rows : (n + 1) * rows] for n in which], axis=0)

    mixed = [None] * own
    for keys, queries, lines, j in cuboids:
        keep = jnp.concatenate([bias[j][n : n + 1] for n in lines], axis=1)
        kvj = pick(kv, keys)
        out = attend(pick(q, queries), kvj[:, :features], kvj[:, features:], keep)
        for n, g in enumerate(queries):
            mixed[g] = out[n * rows : (n + 1) * rows]
    first = (base + dot(jnp.concatenate(mixed, axis=0), wo_buf[...])).astype(BF16)
    first_buf[...] = first.reshape(first_buf.shape)
    first_copy = pltpu.make_async_copy(first_buf, first_hbm, out_sems.at[0])
    first_copy.start()
    normed = layer_norm(first.astype(F32), gc_ref[...]).astype(BF16)
    cq_buf[...] = (dot(normed, cwq_buf[...]) * (LOG2E / 8.0)).astype(BF16).reshape(cq_buf.shape)
    cq_copy = pltpu.make_async_copy(cq_buf, cq_hbm, out_sems.at[1])
    cq_copy.start()
    for move in moves[tokens_at + 5 :]:
        move.wait()
    first_copy.wait()
    cq_copy.wait()


def cross_kernel(
    states,
    list_ref, mine_ref, other_ref, ckv_hbm, cwo_hbm, gf_ref, fin_hbm, fout_hbm, *refs,
):
    first_hbm, cq_hbm, refs = refs[:states], refs[states : 2 * states], refs[2 * states :]
    out_hbm, first_buf, cq_buf, ckv_buf, cwo_buf, fin_buf, fout_buf, out_buf = refs[:8]
    sems, out_sems = refs[8:]
    strip, side, core = position()
    features = cwo_hbm.shape[0]

    def laid(arrays, buf):
        out, at = [], 0
        for a in arrays:
            out.append((a, buf.at[at : at + a.shape[0]]))
            at += a.shape[0]
        return out

    early = [(ckv_hbm, ckv_buf), *laid(cq_hbm, cq_buf)]
    late = [(cwo_hbm, cwo_buf), *laid(first_hbm, first_buf), (fin_hbm, fin_buf), (fout_hbm, fout_buf)]
    moves = copies(sems, early + late)
    toward_row = jnp.where(strip % 2 == 0, 1, -1)

    def entry(n):
        e = list_ref[n // 8, n // 4 % 2, n % 4]
        delta = e // 8 - strip
        column = e % 8
        e_side, e_core, sub = column // 4, (column // 2) % 2, column % 2
        slot = jnp.where(delta == 0, 0, jnp.where(delta == toward_row, 2, 4))
        slot = slot + jnp.where(e_side == side, 0, 1)
        at = slot * 2 + sub
        return jnp.where(e_core == core, mine_ref[at], other_ref[at])

    for move in moves[: len(early)]:
        move.wait()
    tiles = out_hbm.shape[1] // BX
    top = jnp.where(strip % 2 == 0, 4, 5)
    slots = [(9 - top, 0), (1, 2), (3, top)]
    mixed = []
    for k in range(tiles):
        for j in range(2):
            chosen = jnp.concatenate([entry((k * 2 + j) * 4 + l) for l in range(4)], axis=0)
            kv = dot(chosen, ckv_buf[...]).astype(BF16)
            q = jnp.concatenate([cq_buf[s, j] for s in slots[k]], axis=0)
            mixed.append(attend(q, kv[:, :features], kv[:, features:], None))
    for move in moves[len(early) :]:
        move.wait()
    outs = []
    hidden_units = fin_hbm.shape[1]
    step = 1024
    frames = out_buf.shape[0]
    for k in range(tiles):
        first = jnp.concatenate([first_buf[s, j] for j in range(2) for s in slots[k]], axis=0)
        both = jnp.concatenate(mixed[2 * k : 2 * k + 2], axis=0)
        second = (first.astype(F32) + dot(both, cwo_buf[...])).astype(BF16).astype(F32)
        normed = layer_norm(second, gf_ref[...]).astype(BF16)
        total = second
        for c in range(0, hidden_units, step):
            hidden = gelu(dot(normed, fin_buf[:, c : c + step])).astype(BF16)
            total = total + dot(hidden, fout_buf[c : c + step, :])
        shaped = total.reshape(2, 2, frames, HALF, BY, features)
        cols = jnp.concatenate([shaped[0], shaped[1]], axis=3).astype(BF16)
        out_buf[:, k * BX : k * BX + HALF] = cols[0]
        out_buf[:, k * BX + HALF : (k + 1) * BX] = cols[1]
        here = slice(k * BX, (k + 1) * BX)
        outs.append(pltpu.make_async_copy(out_buf.at[:, here], out_hbm.at[:, here], out_sems.at[k]))
        outs[-1].start()
    for copy in outs:
        copy.wait()


def pairs(strips, target):
    out = []
    for s in range(strips):
        for h in range(2):
            for c in range(2):
                s2, h2, c2 = target(s, h, c)
                out.append((s * 4 + h * 2 + c, s2 * 4 + h2 * 2 + c2))
    return out


ANY = pl.BlockSpec(memory_space=pl.ANY)
SCALARS = pl.BlockSpec(memory_space=pltpu.SMEM)
FULL = pl.BlockSpec(memory_space=pltpu.VMEM)
COVER_CELLS = 256


def call(kernel, kinds, out_shape, scratch, copies_in, copies_out, mflops, mbytes, limit):
    return pl.pallas_call(
        kernel,
        in_specs=kinds,
        out_specs=jax.tree.map(lambda _: ANY, out_shape),
        out_shape=out_shape,
        scratch_shapes=[
            *scratch,
            pltpu.SemaphoreType.DMA((copies_in,)),
            pltpu.SemaphoreType.DMA((copies_out,)),
        ],
        compiler_params=pltpu.CompilerParams(vmem_limit_bytes=limit << 20),
        cost_estimate=pl.CostEstimate(
            flops=mflops * 10**6, bytes_accessed=mbytes << 20, transcendentals=0
        ),
    )


def self_call(x, cover, weights, inner, edge, halo=None, piece=None):
    frames, row_count, cols, features = x.shape
    rows = frames * HALF * BY
    quads = (0 if inner is None else 2) + (1 if edge else 0)
    state = jax.ShapeDtypeStruct((quads, cols // BY, rows, features), BF16)
    held = pltpu.VMEM(state.shape, BF16)
    outs = [state, state]
    extra, kinds = [], []
    if edge:
        extra.append(halo)
        kinds.append(FULL)
    if piece is not None:
        extra.append(piece)
        kinds.append(ANY)
        outs.append(jax.ShapeDtypeStruct((frames + piece.shape[0], *piece.shape[1:]), BF16))
    return call(
        functools.partial(self_kernel, inner, edge, piece is not None),
        [ANY, ANY, FULL, FULL, ANY, ANY, ANY, ANY, *kinds],
        outs,
        [
            pltpu.VMEM((frames, quads * HALF, cols, features), BF16),
            pltpu.VMEM((cols, COVER_CELLS), jnp.int32),
            pltpu.VMEM((features, features), BF16),
            pltpu.VMEM((features, 2 * features), BF16),
            pltpu.VMEM((features, features), BF16),
            pltpu.VMEM((features, features), BF16),
            held,
            held,
        ],
        10,
        2,
        2500 * quads,
        6,
        24,
    )(x, cover, *weights, *extra)


def cross_call(listed, mine, other, ckv, cwo, gf, fin, fout, firsts, cqs, frames=4):
    columns, rows, features = firsts[0].shape[1:]
    quads = sum(a.shape[0] for a in firsts)
    held = pltpu.VMEM((quads, columns, rows, features), BF16)
    out = jax.ShapeDtypeStruct((frames, quads * HALF, columns * BY, features), BF16)
    count = 2 * len(firsts)
    return call(
        functools.partial(cross_kernel, len(firsts)),
        [SCALARS, FULL, FULL, ANY, ANY, FULL, ANY, ANY, *[ANY] * count],
        out,
        [
            held,
            held,
            pltpu.VMEM(ckv.shape, BF16),
            pltpu.VMEM(cwo.shape, BF16),
            pltpu.VMEM(fin.shape, BF16),
            pltpu.VMEM(fout.shape, BF16),
            pltpu.VMEM(out.shape, BF16),
        ],
        4 + count,
        3,
        15000,
        12,
        40,
    )(listed, mine, other, ckv, cwo, gf, fin, fout, *firsts, *cqs)


def shards(
    inputs,
    coverage,
    encoded,
    cross_list,
    gain_self,
    gain_cross,
    gain_ffn,
    self_wq,
    self_wkv,
    self_wo,
    cross_wq,
    cross_wkv,
    cross_wo,
    ffn_in,
    ffn_out,
):
    frames, row_count, col_count, features = inputs.shape
    strips = lax.axis_size("gx")
    even = lax.axis_index("gx") % 2 == 0

    def across(s):
        far = s + 1 if s % 2 else s - 1
        return far if 0 <= far < strips else s

    def send(array, target):
        return lax.ppermute(array, ("gx", "gy"), pairs(strips, target))

    def to_row(s, h, c):
        return (s ^ 1, h, c)

    def to_across(s, h, c):
        return (across(s), h, c)

    def to_side(s, h, c):
        return (s, 1 - h, c)

    def to_row_side(s, h, c):
        return (s ^ 1, 1 - h, c)

    def to_across_side(s, h, c):
        return (across(s), 1 - h, c)

    def to_core(s, h, c):
        return (s, h, 1 - c)

    columns, tokens = encoded.shape[1:3]
    piece = encoded.reshape(columns, HALF, tokens // HALF, features)
    cover = coverage.T
    weights = (
        gain_self.reshape(1, features),
        gain_cross.reshape(1, features),
        self_wq,
        self_wkv,
        self_wo,
        cross_wq,
    )
    barrier = lax.optimization_barrier

    near_row = jnp.where(even, row_count - HALF, 0)
    near = lax.dynamic_slice_in_dim(inputs, near_row, HALF, axis=1)
    got_row = send(jnp.concatenate([near, piece], axis=0), to_row)
    first_a, cq_a, to_far = self_call(inputs, cover, weights, 0, None, piece=piece)
    piece_b, first_a, cq_a = barrier((piece, first_a, cq_a))
    got_across = send(to_far, to_across)
    got_side = send(piece_b, to_side)
    got_row_side = send(piece_b, to_row_side)
    got_across_side = send(piece_b, to_across_side)
    first_b, cq_b = self_call(inputs, cover, weights, 1, "row", halo=got_row)
    first_b, cq_b, got_across, got_side, got_row_side, got_across_side = barrier(
        (first_b, cq_b, got_across, got_side, got_row_side, got_across_side)
    )
    pieces = [piece, got_side, got_row[frames:], got_row_side, got_across[frames:], got_across_side]
    mine = jnp.concatenate([p.reshape(columns, tokens, features) for p in pieces], axis=0)
    other = send(mine, to_core)
    first_c, cq_c = self_call(inputs, cover, weights, None, "across", halo=got_across)

    return cross_call(
        cross_list,
        mine,
        other,
        cross_wkv,
        cross_wo,
        gain_ffn.reshape(1, features),
        ffn_in,
        ffn_out,
        [first_a, first_b, first_c],
        [cq_a, cq_b, cq_c],
    )


def solution(mesh):
    return jax.shard_map(
        shards,
        mesh=mesh,
        in_specs=(
            P(None, "gx", "gy", None),
            P(None, "gy"),
            P("gx", "gy", None, None),
            P("gx", "gy", None),
            P(),
            P(),
            P(),
            P(),
            P(),
            P(),
            P(),
            P(),
            P(),
            P(),
            P(),
        ),
        out_specs=P(None, "gx", "gy", None),
        check_vma=False,
    )
```

time: 248 us -> 59.5 us (0.24)
  the two profiles are of different devices: /device:TPU:148 before, /device:TPU:129 now
where the time goes in v2:
time: 59.5 us; the launch traced here: 59.1 us
  Pallas kernels  30.6 us (51%)
  starting transfers between devices  13.7 us (23%)
  local copies, waits for them, and re-layouts  10 us (17%)
  waiting for transfers between devices  3.34 us (6%)
  other arithmetic  0.94 us (2%)
    pallas_call x1, Pallas kernels, cross_call(): call(functools.partial(cross_kernel, len(firsts)), [SCALARS, FULL, FULL,...  17.1 us
    ppermute x6, starting transfers between devices, send(): return lax.ppermute(array, ('gx', 'gy'), pairs(strips, target))  13.7 us
    pallas_call x3, Pallas kernels, self_call(): call(functools.partial(self_kernel, inner, edge, piece is not None), [ANY...  13.6 us
    unnamed x33, local copies, waits for them, and re-layouts  9.01 us
    ppermute x6, waiting for transfers between devices, send(): return lax.ppermute(array, ('gx', 'gy'), pairs(strips, target))  3.34 us
  transfers between devices with their start and end apart: 6, of which 1 were waited for; matrix products, arithmetic and copies ran while one was open for 2% of the time, Pallas kernels for 23%

profile of v2, /device:TPU:129, one launch (start us, length us, event | category | flops | bytes accessed | tf_op | source)
XLA Modules:
  0.0 59.1 jit_solution(6842604315902580535)
XLA Ops:
  0.0 1.0 %constant_dynamic-slice_fusion = bf16[4,4,16,512]{3,2,1,0:T(8,128)(2,1)S(1)} fusion(bf16[4,24,16,512]{3,2,1,0:T(8,128)(2,1)} %refs_0_.5, s32[]{:T(128)S(6)} %select_n.13), kind=kLoop, calls=%fused_computation.7 | loop fusion | bytes 524292 | tf_op jit(solution)/shard_map/dynamic_slice | solution.py:446
  1.0 0.9 %pad_maximum_fusion = bf16[6,4,16,512]{3,2,1,0:T(8,128)(2,1)S(1)} fusion(bf16[2,4,16,512]{3,2,1,0:T(8,128)(2,1)} %bitcast.4.refs_8_, bf16[4,4,16,512]{3,2,1,0:T(8,128)(2,1)S(1)} %constant_dynamic-slice_fusion), kind=kLoop, calls=%fused_computation | loop fusion | flops 196608 | bytes 786432 | tf_op jit(solution)/shard_map/concatenate | solution.py:447
  1.9 1.3 %collective-permute-start = (bf16[6,4,16,512]{3,2,1,0:T(8,128)(2,1)S(1)}, bf16[6,4,16,512]{3,2,1,0:T(8,128)(2,1)S(1)}, u32[]{:S(2)}, u32[]{:S(2)}) collective-permute-start(bf16[6,4,16,512]{3,2,1,0:T(8,128)(2,1)S(1)} %pad_maximum_fusion), channel_id=1, source_target_pairs={{0,4},{1,5},{2,6},{3,7},{4,0},{5,1},{6,2},{7,3},{8,12},{9,13},{10,... | collective-permute-start | bytes 1179656 | tf_op jit(solution)/shard_map/ppermute | solution.py:412
  3.2 0.0 copy-start
  3.2 1.4 %copy-done = bf16[4,24,16,512]{3,2,1,0:T(8,128)(2,1)S(1)} copy-done((bf16[4,24,16,512]{3,2,1,0:T(8,128)(2,1)S(1)}, bf16[4,24,16,512]{3,2,1,0:T(8,128)(2,1)}, u32[]{:S(2)}) %copy-start) | copy-done | bytes 1572888
  4.6 0.0 copy-start.3
  4.6 1.2 %copy-done.3 = bf16[512,1024]{1,0:T(8,128)(2,1)S(1)} copy-done((bf16[512,1024]{1,0:T(8,128)(2,1)S(1)}, bf16[512,1024]{1,0:T(8,128)(2,1)}, u32[]{:S(2)}) %copy-start.3) | copy-done | bytes 1048600
  5.8 0.0 copy-start.5
  5.9 1.0 %copy-done.5 = bf16[512,512]{1,0:T(8,128)(2,1)S(1)} copy-done((bf16[512,512]{1,0:T(8,128)(2,1)S(1)}, bf16[512,512]{1,0:T(8,128)(2,1)}, u32[]{:S(2)}) %copy-start.5) | copy-done | bytes 524312
  6.9 0.0 copy-start.6
  6.9 1.0 %copy-done.6 = bf16[512,512]{1,0:T(8,128)(2,1)S(1)} copy-done((bf16[512,512]{1,0:T(8,128)(2,1)S(1)}, bf16[512,512]{1,0:T(8,128)(2,1)}, u32[]{:S(2)}) %copy-start.6) | copy-done | bytes 524312
  7.9 0.0 copy-start.7
  7.9 1.0 %copy-done.7 = bf16[512,512]{1,0:T(8,128)(2,1)S(1)} copy-done((bf16[512,512]{1,0:T(8,128)(2,1)S(1)}, bf16[512,512]{1,0:T(8,128)(2,1)}, u32[]{:S(2)}) %copy-start.7) | copy-done | bytes 524312
  9.0 0.0 copy-start.9
  9.0 0.9 %copy-done.9 = s32[1536,16]{0,1:T(8,128)S(1)} copy-done((s32[1536,16]{0,1:T(8,128)S(1)}, s32[1536,16]{0,1:T(8,128)}, u32[]{:S(2)}) %copy-start.9) | copy-done | bytes 98328
  9.9 0.0 copy-start.11
  9.9 0.7 %copy-done.11 = f32[512]{0:T(512)S(1)} copy-done((f32[512]{0:T(512)S(1)}, f32[512]{0:T(512)}, u32[]{:S(2)}) %copy-start.11) | copy-done | bytes 2072
  10.6 0.0 copy-start.12
  10.6 0.7 %copy-done.12 = f32[512]{0:T(512)S(1)} copy-done((f32[512]{0:T(512)S(1)}, f32[512]{0:T(512)}, u32[]{:S(2)}) %copy-start.12) | copy-done | bytes 2072
  11.2 4.2 %shard_map.146 = (bf16[2,2,128,512]{3,2,1,0:T(8,128)(2,1)S(1)}, bf16[2,2,128,512]{3,2,1,0:T(8,128)(2,1)S(1)}, bf16[6,4,16,512]{3,2,1,0:T(8,128)(2,1)S(1)}) custom-call(bf16[4,24,16,512]{3,2,1,0:T(8,128)(2,1)S(1)} %copy-done, s32[16,1536]{1,0:T(8,128)S(1)} %bitcast.12, f32[1,512]{1,0:T(1,128)S(1)} %bitcast.15, f32[1,512]{1,0:T(1,128)S(1)} %bitcast.18, ...), custom_call_target="tpu_custom_call" | custom-call | flops 5000000000 | bytes 6291456 | tf_op jit(solution)/shard_map/pallas_call | solution.py:337
  15.4 3.9 %collective-permute-start.4 = (bf16[2,4,16,512]{3,2,1,0:T(8,128)(2,1)}, bf16[2,4,16,512]{3,2,1,0:T(8,128)(2,1)S(1)}, u32[]{:S(2)}, u32[]{:S(2)}) collective-permute-start(bf16[2,4,16,512]{3,2,1,0:T(8,128)(2,1)} %bitcast.4.refs_8_), channel_id=1, source_target_pairs={{0,2},{1,3},{2,0},{3,1},{4,10},{5,11},{6,8},{7,9},{8,6},{9,7},{10,... | collective-permute-start | bytes 393224 | tf_op jit(solution)/shard_map/ppermute | solution.py:412
  19.3 0.0 collective-permute-start.3
  19.3 1.1 %collective-permute-start.2 = (bf16[2,4,16,512]{3,2,1,0:T(8,128)(2,1)}, bf16[2,4,16,512]{3,2,1,0:T(8,128)(2,1)S(1)}, u32[]{:S(2)}, u32[]{:S(2)}) collective-permute-start(bf16[2,4,16,512]{3,2,1,0:T(8,128)(2,1)} %bitcast.4.refs_8_), channel_id=1, source_target_pairs={{0,2},{1,3},{2,0},{3,1},{4,6},{5,7},{6,4},{7,5},{8,10},{9,11},{10,... | collective-permute-start | bytes 393224 | tf_op jit(solution)/shard_map/ppermute | solution.py:412
  20.5 4.4 %collective-permute-start.1 = (bf16[6,4,16,512]{3,2,1,0:T(8,128)(2,1)S(1)}, bf16[6,4,16,512]{3,2,1,0:T(8,128)(2,1)S(1)}, u32[]{:S(2)}, u32[]{:S(2)}) collective-permute-start(bf16[6,4,16,512]{3,2,1,0:T(8,128)(2,1)S(1)} %get-tuple-element.23), channel_id=1, source_target_pairs={{0,0},{1,1},{2,2},{3,3},{4,8},{5,9},{6,10},{7,11},{8,4},{9,5},{10,... | collective-permute-start | bytes 1179656 | tf_op jit(solution)/shard_map/ppermute | solution.py:412
  24.9 0.9 %bitcast_dynamic-update-slice_fusion = bf16[12,64,512]{2,1,0:T(8,128)(2,1)S(1)} fusion(bf16[1,2,64,512]{3,2,1,0:T(8,128)(2,1)} %param.17), kind=kLoop, calls=%fused_computation.1 | loop fusion | bytes 262144
  25.8 0.0 collective-permute-done.refs_8_
  25.8 6.2 %shard_map.145 = (bf16[3,2,128,512]{3,2,1,0:T(8,128)(2,1)S(1)}, bf16[3,2,128,512]{3,2,1,0:T(8,128)(2,1)S(1)}) custom-call(bf16[4,24,16,512]{3,2,1,0:T(8,128)(2,1)S(1)} %copy-done, s32[16,1536]{1,0:T(8,128)S(1)} %bitcast.13, f32[1,512]{1,0:T(1,128)S(1)} %bitcast.16, f32[1,512]{1,0:T(1,128)S(1)} %bitcast.19, bf16[512,512]{1,0:T(8,128)(2,1)S(1)} %copy-done.5, ...), custom_call_target="tpu_custom_call" | custom-call | flops 7500000256 | bytes 6291456 | tf_op jit(solution)/shard_map/pallas_call | solution.py:337
  32.0 0.0 collective-permute-done.4
  32.0 0.0 collective-permute-done.3
  32.0 0.0 collective-permute-done.2
  32.1 3.3 %collective-permute-done.1.refs_8_ = bf16[6,4,16,512]{3,2,1,0:T(8,128)(2,1)S(1)} collective-permute-done((bf16[6,4,16,512]{3,2,1,0:T(8,128)(2,1)S(1)}, bf16[6,4,16,512]{3,2,1,0:T(8,128)(2,1)S(1)}, u32[]{:S(2)}, u32[]{:S(2)}) %collective-permute-start.1) | collective-permute-done | bytes 393248 | tf_op jit(solution)/shard_map/ppermute | solution.py:412
  35.5 0.0 copy-start.1
  35.5 0.0 copy-start.2
  35.5 0.0 copy-start.4
  35.5 0.0 copy-start.8
  35.6 0.0 copy-start.10
  35.6 0.0 copy-start.13
  35.6 3.0 %collective-permute-start.5 = (bf16[12,64,512]{2,1,0:T(8,128)(2,1)S(1)}, bf16[12,64,512]{2,1,0:T(8,128)(2,1)S(1)}, u32[]{:S(2)}, u32[]{:S(2)}) collective-permute-start(bf16[12,64,512]{2,1,0:T(8,128)(2,1)S(1)} %constant_dynamic-update-slice_fusion.mine_ref), channel_id=1, source_target_pairs={{0,1},{1,0},{2,3},{3,2},{4,5},{5,4},{6,7},{7,6},{8,9},{9,8},{10,11... | collective-permute-start | bytes 2359304 | tf_op jit(solution)/shard_map/ppermute | solution.py:412
  38.6 3.2 %shard_map.147 = (bf16[1,2,128,512]{3,2,1,0:T(8,128)(2,1)S(1)}, bf16[1,2,128,512]{3,2,1,0:T(8,128)(2,1)S(1)}) custom-call(bf16[4,24,16,512]{3,2,1,0:T(8,128)(2,1)S(1)} %copy-done, s32[16,1536]{1,0:T(8,128)S(1)} %bitcast.14, f32[1,512]{1,0:T(1,128)S(1)} %bitcast.17, f32[1,512]{1,0:T(1,128)S(1)} %bitcast.20, bf16[512,512]{1,0:T(8,128)(2,1)S(1)} %copy-done.5, ...), custom_call_target="tpu_custom_call" | custom-call | flops 2500000000 | bytes 6291456 | tf_op jit(solution)/shard_map/pallas_call | solution.py:337
  41.7 0.0 collective-permute-done.5.other_ref
  41.8 0.0 copy-done.1
  41.8 0.0 copy-done.2
  41.8 0.0 copy-done.4
  41.8 0.0 copy-done.8
  41.8 0.0 copy-done.10
  41.8 0.0 copy-done.13
  41.8 17.1 %shard_map.148 = bf16[4,24,16,512]{3,2,1,0:T(8,128)(2,1)} custom-call(s32[3,2,4]{2,1,0:T(2,128)S(1)} %copy-done.10, bf16[12,64,512]{2,1,0:T(8,128)(2,1)S(1)} %constant_dynamic-update-slice_fusion.mine_ref, bf16[12,64,512]{2,1,0:T(8,128)(2,1)S(1)} %collective-permute-done.5.other_ref, bf16[512,1024]{1,0:T(8,128)(2,1)S(1)} %copy-done.4, ...), custom_call_target="tpu_custom_call" | custom-call | flops 15000000512 | bytes 12582912 | tf_op jit(solution)/shard_map/pallas_call | solution.py:365
  (7 shorter events, 0.1 us)
Async XLA Ops:
  1.9 23.9 %collective-permute-start = (bf16[6,4,16,512]{3,2,1,0:T(8,128)(2,1)S(1)}, bf16[6,4,16,512]{3,2,1,0:T(8,128)(2,1)S(1)}, u32[]{:S(2)}, u32[]{:S(2)}) collective-permute-start(bf16[6,4,16,512]{3,2,1,0:T(8,128)(2,1)S(1)} %pad_maximum_fusion), channel_id=1, source_target_pairs={{0,4},{1,5},{2,6},{3,7},{4,0},{5,1},{6,2},{7,3},{8,12},{9,13},{10,... | collective-permute-start | bytes 1179656 | tf_op jit(solution)/shard_map/ppermute | solution.py:412
  3.2 1.4 %copy-start = (bf16[4,24,16,512]{3,2,1,0:T(8,128)(2,1)S(1)}, bf16[4,24,16,512]{3,2,1,0:T(8,128)(2,1)}, u32[]{:S(2)}) copy-start(bf16[4,24,16,512]{3,2,1,0:T(8,128)(2,1)} %refs_0_.5) | copy-start | bytes 4718596
  4.6 1.2 %copy-start.3 = (bf16[512,1024]{1,0:T(8,128)(2,1)S(1)}, bf16[512,1024]{1,0:T(8,128)(2,1)}, u32[]{:S(2)}) copy-start(bf16[512,1024]{1,0:T(8,128)(2,1)} %refs_5_.5) | copy-start | bytes 3145732
  5.8 1.0 %copy-start.5 = (bf16[512,512]{1,0:T(8,128)(2,1)S(1)}, bf16[512,512]{1,0:T(8,128)(2,1)}, u32[]{:S(2)}) copy-start(bf16[512,512]{1,0:T(8,128)(2,1)} %refs_4_.5) | copy-start | bytes 1572868
  6.9 1.0 %copy-start.6 = (bf16[512,512]{1,0:T(8,128)(2,1)S(1)}, bf16[512,512]{1,0:T(8,128)(2,1)}, u32[]{:S(2)}) copy-start(bf16[512,512]{1,0:T(8,128)(2,1)} %refs_6_.5) | copy-start | bytes 1572868
  7.9 1.0 %copy-start.7 = (bf16[512,512]{1,0:T(8,128)(2,1)S(1)}, bf16[512,512]{1,0:T(8,128)(2,1)}, u32[]{:S(2)}) copy-start(bf16[512,512]{1,0:T(8,128)(2,1)} %refs_7_.5) | copy-start | bytes 1572868
  9.0 0.9 %copy-start.9 = (s32[1536,16]{0,1:T(8,128)S(1)}, s32[1536,16]{0,1:T(8,128)}, u32[]{:S(2)}) copy-start(s32[1536,16]{0,1:T(8,128)} %param.16) | copy-start | bytes 294916
  9.9 0.7 %copy-start.11 = (f32[512]{0:T(512)S(1)}, f32[512]{0:T(512)}, u32[]{:S(2)}) copy-start(f32[512]{0:T(512)} %param.19) | copy-start | bytes 6148
  10.6 0.7 %copy-start.12 = (f32[512]{0:T(512)S(1)}, f32[512]{0:T(512)}, u32[]{:S(2)}) copy-start(f32[512]{0:T(512)} %param.20) | copy-start | bytes 6148
  15.4 16.6 %collective-permute-start.4 = (bf16[2,4,16,512]{3,2,1,0:T(8,128)(2,1)}, bf16[2,4,16,512]{3,2,1,0:T(8,128)(2,1)S(1)}, u32[]{:S(2)}, u32[]{:S(2)}) collective-permute-start(bf16[2,4,16,512]{3,2,1,0:T(8,128)(2,1)} %bitcast.4.refs_8_), channel_id=1, source_target_pairs={{0,2},{1,3},{2,0},{3,1},{4,10},{5,11},{6,8},{7,9},{8,6},{9,7},{10,... | collective-permute-start | bytes 393224 | tf_op jit(solution)/shard_map/ppermute | solution.py:412
  19.3 12.7 %collective-permute-start.3 = (bf16[2,4,16,512]{3,2,1,0:T(8,128)(2,1)}, bf16[2,4,16,512]{3,2,1,0:T(8,128)(2,1)S(1)}, u32[]{:S(2)}, u32[]{:S(2)}) collective-permute-start(bf16[2,4,16,512]{3,2,1,0:T(8,128)(2,1)} %bitcast.4.refs_8_), channel_id=1, source_target_pairs={{0,6},{1,7},{2,4},{3,5},{4,2},{5,3},{6,0},{7,1},{8,14},{9,15},{10,... | collective-permute-start | bytes 393224 | tf_op jit(solution)/shard_map/ppermute | solution.py:412
  19.3 12.7 %collective-permute-start.2 = (bf16[2,4,16,512]{3,2,1,0:T(8,128)(2,1)}, bf16[2,4,16,512]{3,2,1,0:T(8,128)(2,1)S(1)}, u32[]{:S(2)}, u32[]{:S(2)}) collective-permute-start(bf16[2,4,16,512]{3,2,1,0:T(8,128)(2,1)} %bitcast.4.refs_8_), channel_id=1, source_target_pairs={{0,2},{1,3},{2,0},{3,1},{4,6},{5,7},{6,4},{7,5},{8,10},{9,11},{10,... | collective-permute-start | bytes 393224 | tf_op jit(solution)/shard_map/ppermute | solution.py:412
  20.5 14.9 %collective-permute-start.1 = (bf16[6,4,16,512]{3,2,1,0:T(8,128)(2,1)S(1)}, bf16[6,4,16,512]{3,2,1,0:T(8,128)(2,1)S(1)}, u32[]{:S(2)}, u32[]{:S(2)}) collective-permute-start(bf16[6,4,16,512]{3,2,1,0:T(8,128)(2,1)S(1)} %get-tuple-element.23), channel_id=1, source_target_pairs={{0,0},{1,1},{2,2},{3,3},{4,8},{5,9},{6,10},{7,11},{8,4},{9,5},{10,... | collective-permute-start | bytes 1179656 | tf_op jit(solution)/shard_map/ppermute | solution.py:412
  35.5 6.3 %copy-start.1 = (bf16[512,2048]{1,0:T(8,128)(2,1)S(1)}, bf16[512,2048]{1,0:T(8,128)(2,1)}, u32[]{:S(2)}) copy-start(bf16[512,2048]{1,0:T(8,128)(2,1)} %fin_hbm.1) | copy-start | bytes 6291460
  35.5 6.2 %copy-start.2 = (bf16[2048,512]{1,0:T(8,128)(2,1)S(1)}, bf16[2048,512]{1,0:T(8,128)(2,1)}, u32[]{:S(2)}) copy-start(bf16[2048,512]{1,0:T(8,128)(2,1)} %fout_hbm.1) | copy-start | bytes 6291460
  35.5 6.2 %copy-start.4 = (bf16[512,1024]{1,0:T(8,128)(2,1)S(1)}, bf16[512,1024]{1,0:T(8,128)(2,1)}, u32[]{:S(2)}) copy-start(bf16[512,1024]{1,0:T(8,128)(2,1)} %ckv_hbm.1) | copy-start | bytes 3145732
  35.5 6.2 %copy-start.8 = (bf16[512,512]{1,0:T(8,128)(2,1)S(1)}, bf16[512,512]{1,0:T(8,128)(2,1)}, u32[]{:S(2)}) copy-start(bf16[512,512]{1,0:T(8,128)(2,1)} %cwo_hbm.1) | copy-start | bytes 1572868
  35.6 6.2 %copy-start.10 = (s32[3,2,4]{2,1,0:T(2,128)S(1)}, s32[3,2,4]{2,1,0:T(2,128)}, u32[]{:S(2)}) copy-start(s32[3,2,4]{2,1,0:T(2,128)} %list_ref.1) | copy-start | bytes 292
  35.6 6.2 %copy-start.13 = (f32[512]{0:T(512)S(1)}, f32[512]{0:T(512)}, u32[]{:S(2)}) copy-start(f32[512]{0:T(512)} %param.21) | copy-start | bytes 6148
  35.6 6.2 %collective-permute-start.5 = (bf16[12,64,512]{2,1,0:T(8,128)(2,1)S(1)}, bf16[12,64,512]{2,1,0:T(8,128)(2,1)S(1)}, u32[]{:S(2)}, u32[]{:S(2)}) collective-permute-start(bf16[12,64,512]{2,1,0:T(8,128)(2,1)S(1)} %constant_dynamic-update-slice_fusion.mine_ref), channel_id=1, source_target_pairs={{0,1},{1,0},{2,3},{3,2},{4,5},{5,4},{6,7},{7,6},{8,9},{9,8},{10,11... | collective-permute-start | bytes 2359304 | tf_op jit(solution)/shard_map/ppermute | solution.py:412

commit v3 on v2

v3 whole, which is shorter than its diff:
```python
import functools
import math

import jax
import jax.numpy as jnp
from jax import lax
from jax.experimental import pallas as pl
from jax.experimental.pallas import tpu as pltpu
from jax.sharding import PartitionSpec as P

HEADS = 8
BX = 8
BY = 8
HALF = BX // 2
LOG2E = math.log2(math.e)

epsilon = 1e-05
mask_depth = 30.0

F32 = jnp.float32
BF16 = jnp.bfloat16


def dot(a, b):
    return jnp.dot(a, b, preferred_element_type=F32)


def dot_nt(a, b):
    return lax.dot_general(a, b, (((1,), (1,)), ((), ())), preferred_element_type=F32)


def layer_norm(widened, gain_vec):
    centre = widened - jnp.mean(widened, axis=-1, keepdims=True)
    spread = jnp.mean(centre * centre, axis=-1, keepdims=True)
    return centre * lax.rsqrt(spread + epsilon) * gain_vec


def gelu(v):
    inner = v * (v * v * (math.sqrt(2 / math.pi) * 0.044715) + math.sqrt(2 / math.pi))
    half = 0.5 * v
    return half * jnp.tanh(inner) + half


def granules(block):
    wide = block.astype(F32)
    frames, rows, cols, features = wide.shape
    return [
        wide[:, :, j * BY : (j + 1) * BY].reshape(frames * rows * BY, features)
        for j in range(cols // BY)
    ]


def attend(q, k, v, bias):
    count, features = q.shape
    keys = k.shape[0]
    lane = lax.broadcasted_iota(jnp.int32, (count, 128), 1)
    low = lane < 64
    ones = jnp.ones((keys, 128), BF16)
    zero = jnp.zeros((count, 128), BF16)
    outs = []
    for p in range(features // 128):
        cols = slice(p * 128, p * 128 + 128)
        qp = q[:, cols]
        both = jnp.concatenate([jnp.where(low, qp, zero), jnp.where(low, zero, qp)], axis=0)
        scores = dot_nt(both, k[:, cols])
        if bias is not None:
            scores = scores + bias
        top = jnp.max(scores, axis=-1, keepdims=True)
        weights = jnp.exp2(scores - top).astype(BF16)
        mixed = dot(weights, jnp.concatenate([v[:, cols], ones], axis=1))
        num = jnp.where(low, mixed[:count, :128], mixed[count:, :128])
        den = jnp.where(low, mixed[:count, 128:], mixed[count:, 128:])
        outs.append((num / den).astype(BF16))
    return jnp.concatenate(outs, axis=1)


def position():
    place = lax.axis_index("gy")
    return lax.axis_index("gx"), place // 2, place % 2


def first_cell(strip, row_count, total, window):
    block = jnp.maximum(strip * row_count - HALF, 0) // 128
    return pl.multiple_of(jnp.minimum(block, (total - window) // 128) * 128, 128)


def bias_rows(cover_ref, first_row, quads):
    cols, cells = cover_ref.shape
    cover = cover_ref[...].astype(BF16)
    key = lax.broadcasted_iota(jnp.int32, (128, cells), 0)
    cell = lax.broadcasted_iota(jnp.int32, (128, cells), 1)
    same_row = (cell % HALF) == (key // BY) % HALF
    line = lax.broadcasted_iota(jnp.int32, (8, cells), 0)
    wanted = jnp.full((8, cells), -9, jnp.int32)
    for n, quad in enumerate(quads):
        wanted = jnp.where(line == n, quad, wanted)
    grid_row = lax.broadcasted_iota(jnp.int32, (8, cells), 1) + first_row
    member = jnp.where(grid_row // HALF == wanted, 1.0, 0.0).astype(BF16)
    spot = lax.broadcasted_iota(jnp.int32, (128, cols), 0)
    col = lax.broadcasted_iota(jnp.int32, (128, cols), 1)
    out = []
    for j in range(cols // BY):
        pick = jnp.where(col == j * BY + spot % BY, 1.0, 0.0).astype(BF16)
        spread = jnp.where(same_row, dot(pick, cover), 0.0).astype(BF16)
        out.append((dot_nt(member, spread) - 1.0) * (mask_depth * LOG2E))
    return out


def copies(sems, moves):
    made = [pltpu.make_async_copy(src, dst, sems.at[n]) for n, (src, dst) in enumerate(moves)]
    for copy in made:
        copy.start()
    return made


def pack_kernel(x_hbm, piece_hbm, row_ref, across_ref, sems):
    even = position()[0] % 2 == 0
    frames, row_count = x_hbm.shape[:2]
    last = row_count - HALF
    moves = copies(
        sems,
        [
            (x_hbm.at[:, pl.ds(jnp.where(even, last, 0), HALF)], row_ref.at[:frames]),
            (piece_hbm, row_ref.at[frames:]),
            (x_hbm.at[:, pl.ds(jnp.where(even, 0, last), HALF)], across_ref.at[:frames]),
            (piece_hbm, across_ref.at[frames:]),
        ],
    )
    for move in moves:
        move.wait()


def shifted_attention(strip, cover_buf, start, quads, cuboids, parts, halo, gs, gc, wq, wkv, wo, cwq, moves=()):
    features = wq.shape[0]
    rows = parts[0].shape[0]
    base = jnp.concatenate(parts, axis=0)
    normed = layer_norm(base, gs).astype(BF16)
    every = normed if halo is None else jnp.concatenate([normed, halo], axis=0)
    for move in moves[:3]:
        move.wait()
    bias = bias_rows(cover_buf, start, quads)
    kv = dot(every, wkv[...]).astype(BF16)
    q = (dot(normed, wq[...]) * (LOG2E / 8.0)).astype(BF16)

    def pick(a, which):
        return jnp.concatenate([a[n * rows : (n + 1) * rows] for n in which], axis=0)

    mixed = [None] * len(parts)
    for keys, queries, lines, j in cuboids:
        keep = jnp.concatenate([bias[j][n : n + 1] for n in lines], axis=1)
        kvj = pick(kv, keys)
        out = attend(pick(q, queries), kvj[:, :features], kvj[:, features:], keep)
        for n, g in enumerate(queries):
            mixed[g] = out[n * rows : (n + 1) * rows]
    for move in moves[3:]:
        move.wait()
    first = (base + dot(jnp.concatenate(mixed, axis=0), wo[...])).astype(BF16)
    normed = layer_norm(first.astype(F32), gc).astype(BF16)
    return first, (dot(normed, cwq[...]) * (LOG2E / 8.0)).astype(BF16)


def inner_kernel(
    x_hbm, cover_hbm, gs_ref, gc_ref, wq_hbm, wkv_hbm, wo_hbm, cwq_hbm, ckv_hbm, cwo_hbm,
    first_ref, cq_ref, sides_ref, cover_ref, wq, wkv, wo, cwq, ckv, cwo,
    x_buf, sems,
):
    strip = position()[0]
    even = strip % 2 == 0
    row_count = x_hbm.shape[1]
    last = row_count - HALF
    start = first_cell(strip, row_count, cover_hbm.shape[1], cover_ref.shape[1])
    inner = x_buf.shape[1]
    moves = copies(
        sems,
        [
            (x_hbm.at[:, HALF:last], x_buf),
            (wkv_hbm, wkv),
            (cover_hbm.at[:, pl.ds(start, cover_ref.shape[1])], cover_ref),
            (wq_hbm, wq),
            (wo_hbm, wo),
            (cwq_hbm, cwq),
            (x_hbm.at[:, pl.ds(jnp.where(even, last, 0), HALF)], sides_ref.at[0]),
            (x_hbm.at[:, pl.ds(jnp.where(even, 0, last), HALF)], sides_ref.at[1]),
            (ckv_hbm, ckv),
            (cwo_hbm, cwo),
        ],
    )
    moves[0].wait()
    parts, quads, cuboids = [], [], []
    for t in range(inner // HALF):
        parts += granules(x_buf[:, t * HALF : (t + 1) * HALF])
        quads.append(strip * (row_count // HALF) + 1 + t)
    for c in range(inner // BX):
        for j in range(2):
            pair = (4 * c + j, 4 * c + 2 + j)
            cuboids.append((pair, pair, (2 * c, 2 * c + 1), j))
    first, cq = shifted_attention(
        strip,
        cover_ref,
        start,
        quads,
        cuboids,
        parts,
        None,
        gs_ref[...],
        gc_ref[...],
        wq,
        wkv,
        wo,
        cwq,
        moves[1:6],
    )
    first_ref[...] = first.reshape(first_ref.shape)
    cq_ref[...] = cq.reshape(cq_ref.shape)
    for move in moves[6:]:
        move.wait()


def edge_kernel(
    row_ref, across_ref, sides_ref, cover_ref, gs_ref, gc_ref, wq, wkv, wo, cwq, first_ref, cq_ref, *, per_strip, cells
):
    strip = position()[0]
    strips = lax.axis_size("gx")
    even = strip % 2 == 0
    frames = sides_ref.shape[1]
    start = first_cell(strip, per_strip * HALF, cells, cover_ref.shape[1])
    gs = gs_ref[...]
    parts, quads, cuboids, halos = [], [], [], []
    for n, halo_ref in enumerate((row_ref, across_ref)):
        above = even if n == 0 else jnp.logical_not(even)
        parts += granules(sides_ref[n])
        own = strip * per_strip + jnp.where(above, per_strip - 1, 0)
        quads += [own, own + jnp.where(above, 1, -1)]
        halo = layer_norm(jnp.concatenate(granules(halo_ref[:frames]), axis=0), gs)
        outside = jnp.where(above, strip == strips - 1, strip == 0)
        halos.append((halo * jnp.where(outside, 0.0, 1.0)).astype(BF16))
        for j in range(2):
            g = 2 * n + j
            cuboids.append(((g, 4 + g), (g,), (2 * n, 2 * n + 1), j))
    first, cq = shifted_attention(
        strip,
        cover_ref,
        start,
        quads,
        cuboids,
        parts,
        jnp.concatenate(halos, axis=0),
        gs,
        gc_ref[...],
        wq,
        wkv,
        wo,
        cwq,
    )
    first_ref[...] = first.reshape(first_ref.shape)
    cq_ref[...] = cq.reshape(cq_ref.shape)


def cross_kernel(states, list_ref, mine_ref, other_ref, ckv_ref, cwo_ref, gf_ref, fin_hbm, fout_hbm, *refs):
    first_refs, cq_refs, refs = refs[:states], refs[states : 2 * states], refs[2 * states :]
    out_hbm, first_buf, cq_buf, out_buf, fin_ref, fout_ref, sems, out_sems = refs
    moves = copies(sems, [(fin_hbm, fin_ref), (fout_hbm, fout_ref)])
    strip, side, core = position()
    features = cwo_ref.shape[0]

    def gather(arrays, buf):
        at = 0
        for a in arrays:
            buf[at : at + a.shape[0]] = a[...]
            at += a.shape[0]

    gather(first_refs, first_buf)
    gather(cq_refs, cq_buf)
    toward_row = jnp.where(strip % 2 == 0, 1, -1)

    def entry(n):
        e = list_ref[n // 8, n // 4 % 2, n % 4]
        delta = e // 8 - strip
        column = e % 8
        e_side, e_core, sub = column // 4, (column // 2) % 2, column % 2
        slot = jnp.where(delta == 0, 0, jnp.where(delta == toward_row, 2, 4))
        slot = slot + jnp.where(e_side == side, 0, 1)
        at = slot * 2 + sub
        return jnp.where(e_core == core, mine_ref[at], other_ref[at])

    tiles = out_hbm.shape[1] // BX
    top = jnp.where(strip % 2 == 0, 4, 5)
    slots = [(9 - top, 0), (1, 2), (3, top)]
    kvs = []
    for n in range(2 * tiles):
        chosen = jnp.concatenate([entry(n * 4 + l) for l in range(4)], axis=0)
        kvs.append(dot(chosen, ckv_ref[...]).astype(BF16))
    mixed = []
    for k in range(tiles):
        for j in range(2):
            kv = kvs[2 * k + j]
            q = jnp.concatenate([cq_buf[s, j] for s in slots[k]], axis=0)
            mixed.append(attend(q, kv[:, :features], kv[:, features:], None))
    for move in moves:
        move.wait()
    outs = []
    hidden_units = fin_ref.shape[1]
    step = 2048
    frames = out_buf.shape[0]
    for k in range(tiles):
        first = jnp.concatenate([first_buf[s, j] for j in range(2) for s in slots[k]], axis=0)
        both = jnp.concatenate(mixed[2 * k : 2 * k + 2], axis=0)
        second = (first.astype(F32) + dot(both, cwo_ref[...])).astype(BF16).astype(F32)
        normed = layer_norm(second, gf_ref[...]).astype(BF16)
        total = second
        for c in range(0, hidden_units, step):
            hidden = gelu(dot(normed, fin_ref[:, c : c + step])).astype(BF16)
            total = total + dot(hidden, fout_ref[c : c + step, :])
        shaped = total.reshape(2, 2, frames, HALF, BY, features)
        cols = jnp.concatenate([shaped[0], shaped[1]], axis=3).astype(BF16)
        out_buf[:, k * BX : k * BX + HALF] = cols[0]
        out_buf[:, k * BX + HALF : (k + 1) * BX] = cols[1]
        here = slice(k * BX, (k + 1) * BX)
        outs.append(pltpu.make_async_copy(out_buf.at[:, here], out_hbm.at[:, here], out_sems.at[k]))
        outs[-1].start()
    for copy in outs:
        copy.wait()


def pairs(strips, target):
    out = []
    for s in range(strips):
        for h in range(2):
            for c in range(2):
                s2, h2, c2 = target(s, h, c)
                out.append((s * 4 + h * 2 + c, s2 * 4 + h2 * 2 + c2))
    return out


ANY = pl.BlockSpec(memory_space=pl.ANY)
HBM = pl.BlockSpec(memory_space=pltpu.HBM)
SCALARS = pl.BlockSpec(memory_space=pltpu.SMEM)
FULL = pl.BlockSpec(memory_space=pltpu.VMEM)
COVER_CELLS = 256


def call(kernel, kinds, out_shape, scratch, sems, out_kind, mflops, mbytes, limit):
    return pl.pallas_call(
        kernel,
        in_specs=kinds,
        out_specs=jax.tree.map(lambda _: out_kind, out_shape),
        out_shape=out_shape,
        scratch_shapes=[*scratch, *sems],
        compiler_params=pltpu.CompilerParams(vmem_limit_bytes=limit << 20),
        cost_estimate=pl.CostEstimate(
            flops=mflops * 10**6, bytes_accessed=mbytes << 20, transcendentals=0
        ),
    )


def pack_call(x, piece):
    frames, _, cols, features = x.shape
    out = jax.ShapeDtypeStruct((frames + piece.shape[0], HALF, cols, features), BF16)
    return pl.pallas_call(
        pack_kernel,
        in_specs=[ANY, ANY],
        out_specs=[FULL, FULL],
        out_shape=[out, out],
        scratch_shapes=[pltpu.SemaphoreType.DMA((4,))],
        cost_estimate=pl.CostEstimate(flops=0, bytes_accessed=2 << 20, transcendentals=0),
    )(x, piece)


def inner_call(x, cover, gs, gc, weights):
    frames, row_count, cols, features = x.shape
    rows = frames * HALF * BY
    quads = row_count // HALF - 2
    state = jax.ShapeDtypeStruct((quads, cols // BY, rows, features), BF16)
    return call(
        inner_kernel,
        [HBM, HBM, FULL, FULL, *[HBM] * len(weights)],
        [
            state,
            state,
            jax.ShapeDtypeStruct((2, frames, HALF, cols, features), BF16),
            jax.ShapeDtypeStruct((cols, COVER_CELLS), jnp.int32),
            *[jax.ShapeDtypeStruct(w.shape, w.dtype) for w in weights],
        ],
        [pltpu.VMEM((frames, row_count - BX, cols, features), BF16)],
        [pltpu.SemaphoreType.DMA((10,))],
        FULL,
        8000,
        10,
        53,
    )(x, cover, gs, gc, *weights)


def edge_call(row, across, sides, cover_part, gs, gc, wq, wkv, wo, cwq, row_count, cells):
    _, frames, _, cols, features = sides.shape
    rows = frames * HALF * BY
    state = jax.ShapeDtypeStruct((2, cols // BY, rows, features), BF16)
    return call(
        functools.partial(edge_kernel, per_strip=row_count // HALF, cells=cells),
        [FULL] * 10,
        [state, state],
        [],
        [],
        FULL,
        6000,
        4,
        28,
    )(row, across, sides, cover_part, gs, gc, wq, wkv, wo, cwq)


def cross_call(listed, mine, other, ckv, cwo, gf, fin, fout, firsts, cqs, frames=4):
    columns, rows, features = firsts[0].shape[1:]
    quads = sum(a.shape[0] for a in firsts)
    held = pltpu.VMEM((quads, columns, rows, features), BF16)
    out = jax.ShapeDtypeStruct((frames, quads * HALF, columns * BY, features), BF16)
    count = 2 * len(firsts)
    return call(
        functools.partial(cross_kernel, len(firsts)),
        [SCALARS, *[FULL] * 5, HBM, HBM, *[FULL] * count],
        out,
        [
            held,
            held,
            pltpu.VMEM(out.shape, BF16),
            pltpu.VMEM(fin.shape, BF16),
            pltpu.VMEM(fout.shape, BF16),
        ],
        [pltpu.SemaphoreType.DMA((2,)), pltpu.SemaphoreType.DMA((3,))],
        ANY,
        15000,
        12,
        40,
    )(listed, mine, other, ckv, cwo, gf, fin, fout, *firsts, *cqs)


def shards(
    inputs,
    coverage,
    encoded,
    cross_list,
    gain_self,
    gain_cross,
    gain_ffn,
    self_wq,
    self_wkv,
    self_wo,
    cross_wq,
    cross_wkv,
    cross_wo,
    ffn_in,
    ffn_out,
):
    frames, row_count, col_count, features = inputs.shape
    strips = lax.axis_size("gx")
    even = lax.axis_index("gx") % 2 == 0

    def across(s):
        far = s + 1 if s % 2 else s - 1
        return far if 0 <= far < strips else s

    def send(array, target):
        return lax.ppermute(array, ("gx", "gy"), pairs(strips, target))

    def to_row(s, h, c):
        return (s ^ 1, h, c)

    def to_across(s, h, c):
        return (across(s), h, c)

    def to_side(s, h, c):
        return (s, 1 - h, c)

    def to_row_side(s, h, c):
        return (s ^ 1, 1 - h, c)

    def to_across_side(s, h, c):
        return (across(s), 1 - h, c)

    def to_core(s, h, c):
        return (s, h, 1 - c)

    columns, tokens = encoded.shape[1:3]
    piece = encoded.reshape(columns, HALF, tokens // HALF, features)
    cover = coverage.T
    gs = gain_self.reshape(1, features)
    gc = gain_cross.reshape(1, features)
    barrier = lax.optimization_barrier

    to_near, to_far = pack_call(inputs, piece)
    got_row = send(to_near, to_row)
    got_across = send(to_far, to_across)
    got_side = send(piece, to_side)
    got_row_side = send(piece, to_row_side)
    got_across_side = send(piece, to_across_side)
    first_a, cq_a, sides, cover_part, *weights = inner_call(
        inputs,
        cover,
        gs,
        gc,
        (self_wq, self_wkv, self_wo, cross_wq, cross_wkv, cross_wo),
    )
    first_a, cq_a, got_row, got_across, got_side, got_row_side, got_across_side = barrier(
        (first_a, cq_a, got_row, got_across, got_side, got_row_side, got_across_side)
    )
    pieces = [piece, got_side, got_row[frames:], got_row_side, got_across[frames:], got_across_side]
    mine = jnp.concatenate([p.reshape(columns, tokens, features) for p in pieces], axis=0)
    other = send(mine, to_core)
    first_b, cq_b = edge_call(
        got_row, got_across, sides, cover_part, gs, gc, *weights[:4], row_count, cover.shape[1]
    )
    return cross_call(
        cross_list,
        mine,
        other,
        *weights[4:6],
        gain_ffn.reshape(1, features),
        ffn_in,
        ffn_out,
        [first_a, first_b],
        [cq_a, cq_b],
    )


def solution(mesh):
    return jax.shard_map(
        shards,
        mesh=mesh,
        in_specs=(
            P(None, "gx", "gy", None),
            P(None, "gy"),
            P("gx", "gy", None, None),
            P("gx", "gy", None),
            P(),
            P(),
            P(),
            P(),
            P(),
            P(),
            P(),
            P(),
            P(),
            P(),
            P(),
        ),
        out_specs=P(None, "gx", "gy", None),
        check_vma=False,
    )
```

time: 59.5 us -> 53 us (0.89)
  the two profiles are of different devices: /device:TPU:129 before, /device:TPU:169 now
where the time goes in v3:
time: 53 us; the launch traced here: 52.7 us
  Pallas kernels  33.2 us (63%)
  starting transfers between devices  14.4 us (27%)
  local copies, waits for them, and re-layouts  3.43 us (6%)
  waiting for transfers between devices  1.31 us (2%)
    pallas_call x1, Pallas kernels, cross_call(): call(functools.partial(cross_kernel, len(firsts)), [SCALARS, *[FULL] * 5,...  16.3 us
    ppermute x6, starting transfers between devices, send(): return lax.ppermute(array, ('gx', 'gy'), pairs(strips, target))  14.4 us
    pallas_call x1, Pallas kernels, inner_call(): call(inner_kernel, [HBM, HBM, FULL, FULL, *[HBM] * len(weights)], [state,...  10.7 us
    pallas_call x1, Pallas kernels, edge_call(): call(functools.partial(edge_kernel, per_strip=row_count // HALF, cells=ce...  4.15 us
    unnamed x37, local copies, waits for them, and re-layouts  3.39 us
    pallas_call x1, Pallas kernels, pack_call(): pl.pallas_call(pack_kernel, in_specs=[ANY, ANY], out_specs=[FULL, FULL],...  2.05 us
    ppermute x6, waiting for transfers between devices, send(): return lax.ppermute(array, ('gx', 'gy'), pairs(strips, target))  1.31 us
  transfers between devices with their start and end apart: 6, of which 1 were waited for; matrix products, arithmetic and copies ran while one was open for 0% of the time, Pallas kernels for 32%

profile of v3, /device:TPU:169, one launch (start us, length us, event | category | flops | bytes accessed | tf_op | source)
XLA Modules:
  0.0 52.7 jit_solution(14817721920926966267)
XLA Ops:
  0.0 2.7 %collective-permute-start.2 = (bf16[2,4,16,512]{3,2,1,0:T(8,128)(2,1)}, bf16[2,4,16,512]{3,2,1,0:T(8,128)(2,1)S(1)}, u32[]{:S(2)}, u32[]{:S(2)}) collective-permute-start(bf16[2,4,16,512]{3,2,1,0:T(8,128)(2,1)} %bitcast.20), channel_id=1, source_target_pairs={{0,2},{1,3},{2,0},{3,1},{4,6},{5,7},{6,4},{7,5},{8,10},{9,11},{10,... | collective-permute-start | bytes 393224 | tf_op jit(solution)/shard_map/ppermute | solution.py:461
  2.7 0.9 %collective-permute-start.3 = (bf16[2,4,16,512]{3,2,1,0:T(8,128)(2,1)}, bf16[2,4,16,512]{3,2,1,0:T(8,128)(2,1)S(1)}, u32[]{:S(2)}, u32[]{:S(2)}) collective-permute-start(bf16[2,4,16,512]{3,2,1,0:T(8,128)(2,1)} %bitcast.21), channel_id=1, source_target_pairs={{0,6},{1,7},{2,4},{3,5},{4,2},{5,3},{6,0},{7,1},{8,14},{9,15},{10,... | collective-permute-start | bytes 393224 | tf_op jit(solution)/shard_map/ppermute | solution.py:461
  3.6 1.7 %collective-permute-start.4 = (bf16[2,4,16,512]{3,2,1,0:T(8,128)(2,1)}, bf16[2,4,16,512]{3,2,1,0:T(8,128)(2,1)S(1)}, u32[]{:S(2)}, u32[]{:S(2)}) collective-permute-start(bf16[2,4,16,512]{3,2,1,0:T(8,128)(2,1)} %bitcast.22), channel_id=1, source_target_pairs={{0,2},{1,3},{2,0},{3,1},{4,10},{5,11},{6,8},{7,9},{8,6},{9,7},{10,... | collective-permute-start | bytes 393224 | tf_op jit(solution)/shard_map/ppermute | solution.py:461
  5.3 2.0 %shard_map.146 = (bf16[6,4,16,512]{3,2,1,0:T(8,128)(2,1)}, bf16[6,4,16,512]{3,2,1,0:T(8,128)(2,1)}) custom-call(bf16[4,24,16,512]{3,2,1,0:T(8,128)(2,1)} %x_hbm.3, bf16[2,4,16,512]{3,2,1,0:T(8,128)(2,1)} %bitcast.23), custom_call_target="tpu_custom_call" | custom-call | bytes 2097152 | tf_op jit(solution)/shard_map/pallas_call | solution.py:359
  7.4 0.3 collective-permute-start
  7.7 6.0 %collective-permute-start.1 = (bf16[6,4,16,512]{3,2,1,0:T(8,128)(2,1)}, bf16[6,4,16,512]{3,2,1,0:T(8,128)(2,1)S(1)}, u32[]{:S(2)}, u32[]{:S(2)}) collective-permute-start(bf16[6,4,16,512]{3,2,1,0:T(8,128)(2,1)} %get-tuple-element.29), channel_id=1, source_target_pairs={{0,0},{1,1},{2,2},{3,3},{4,8},{5,9},{6,10},{7,11},{8,4},{9,5},{10,... | collective-permute-start | bytes 1179656 | tf_op jit(solution)/shard_map/ppermute | solution.py:461
  13.7 0.0 copy-start.2
  13.7 0.9 %copy-done.2 = s32[1536,16]{0,1:T(8,128)S(1)} copy-done((s32[1536,16]{0,1:T(8,128)S(1)}, s32[1536,16]{0,1:T(8,128)}, u32[]{:S(2)}) %copy-start.2) | copy-done | bytes 98328
  14.6 0.0 copy-start.4
  14.6 0.7 %copy-done.4 = f32[512]{0:T(512)S(1)} copy-done((f32[512]{0:T(512)S(1)}, f32[512]{0:T(512)}, u32[]{:S(2)}) %copy-start.4) | copy-done | bytes 2072
  15.3 0.0 copy-start.5
  15.3 0.7 %copy-done.5 = f32[512]{0:T(512)S(1)} copy-done((f32[512]{0:T(512)S(1)}, f32[512]{0:T(512)}, u32[]{:S(2)}) %copy-start.5) | copy-done | bytes 2072
  16.0 0.0 copy-start.15
  16.0 10.7 %shard_map.145 = (bf16[4,2,128,512]{3,2,1,0:T(8,128)(2,1)}, bf16[4,2,128,512]{3,2,1,0:T(8,128)(2,1)}, bf16[2,4,4,16,512]{4,3,2,1,0:T(8,128)(2,1)S(1)}, s32[16,25...) custom-call(bf16[4,24,16,512]{3,2,1,0:T(8,128)(2,1)} %x_hbm.3, ...), custom_call_target="tpu_custom_call" | custom-call | flops 8000000000 | bytes 10485760 | tf_op jit(solution)/shard_map/pallas_call | solution.py:374
  26.7 0.0 copy-done.15
  26.7 0.0 copy-start.7
  26.7 0.0 copy-start.11
  26.7 0.0 copy-start.12
  26.7 0.0 collective-permute-done.2
  26.7 0.0 collective-permute-done.3
  26.8 0.0 collective-permute-done.4
  26.8 0.0 collective-permute-done.row_ref
  26.8 1.3 %collective-permute-done.1.across_ref = bf16[6,4,16,512]{3,2,1,0:T(8,128)(2,1)S(1)} collective-permute-done((bf16[6,4,16,512]{3,2,1,0:T(8,128)(2,1)}, bf16[6,4,16,512]{3,2,1,0:T(8,128)(2,1)S(1)}, u32[]{:S(2)}, u32[]{:S(2)}) %collective-permute-start.1) | collective-permute-done | bytes 393248 | tf_op jit(solution)/shard_map/ppermute | solution.py:461
  28.2 2.7 %collective-permute-start.5 = (bf16[12,64,512]{2,1,0:T(8,128)(2,1)S(1)}, bf16[12,64,512]{2,1,0:T(8,128)(2,1)S(1)}, u32[]{:S(2)}, u32[]{:S(2)}) collective-permute-start(bf16[12,64,512]{2,1,0:T(8,128)(2,1)S(1)} %constant_dynamic-update-slice_fusion.mine_ref), channel_id=1, source_target_pairs={{0,1},{1,0},{2,3},{3,2},{4,5},{5,4},{6,7},{7,6},{8,9},{9,8},{10,11... | collective-permute-start | bytes 2359304 | tf_op jit(solution)/shard_map/ppermute | solution.py:461
  30.9 0.0 copy-done.7
  30.9 0.0 copy-done.11
  30.9 0.0 copy-done.12
  30.9 0.0 copy-start.13
  30.9 1.0 %copy-done.13 = bf16[512,512]{1,0:T(8,128)(2,1)S(1)} copy-done((bf16[512,512]{1,0:T(8,128)(2,1)S(1)}, bf16[512,512]{1,0:T(8,128)(2,1)}, u32[]{:S(2)}) %copy-start.13) | copy-done | bytes 524312
  32.0 0.0 copy-start
  32.0 0.0 copy-start.1
  32.0 0.0 copy-start.3
  32.0 0.0 copy-start.6
  32.0 0.0 copy-start.8
  32.0 0.0 copy-start.9
  32.0 0.0 copy-start.10
  32.0 0.0 copy-start.14
  32.0 4.1 %shard_map.147 = (bf16[2,2,128,512]{3,2,1,0:T(8,128)(2,1)S(1)}, bf16[2,2,128,512]{3,2,1,0:T(8,128)(2,1)S(1)}) custom-call(bf16[6,4,16,512]{3,2,1,0:T(8,128)(2,1)S(1)} %collective-permute-done.row_ref, bf16[6,4,16,512]{3,2,1,0:T(8,128)(2,1)S(1)} %collective-permute-done.1.across_ref, bf16[2,4,4,16,512]{4,3,2,1,0:T(8,128)(2,1)S(1)} %get-tuple-element.38.sides_ref, ...), custom_call_target="tpu_custom_call" | custom-call | flops 6000000000 | bytes 4194304 | tf_op jit(solution)/shard_map/pallas_call | solution.py:397
  36.2 0.0 collective-permute-done.5.other_ref
  36.2 0.0 copy-done
  36.2 0.0 copy-done.1
  36.2 0.0 copy-done.3
  36.2 0.0 copy-done.6
  36.2 0.0 copy-done.8
  36.2 0.0 copy-done.9
  36.2 0.0 copy-done.10
  36.2 0.0 copy-done.14
  36.3 16.3 %shard_map.148 = bf16[4,24,16,512]{3,2,1,0:T(8,128)(2,1)} custom-call(s32[3,2,4]{2,1,0:T(2,128)S(1)} %copy-done.3, bf16[12,64,512]{2,1,0:T(8,128)(2,1)S(1)} %constant_dynamic-update-slice_fusion.mine_ref, bf16[12,64,512]{2,1,0:T(8,128)(2,1)S(1)} %collective-permute-done.5.other_ref, bf16[512,1024]{1,0:T(8,128)(2,1)S(1)} %copy-done.10, ...), custom_call_target="tpu_custom_call" | custom-call | flops 15000000512 | bytes 12582912 | tf_op jit(solution)/shard_map/pallas_call | solution.py:416
  (8 shorter events, 0.1 us)
Async XLA Ops:
  0.0 26.7 %collective-permute-start.2 = (bf16[2,4,16,512]{3,2,1,0:T(8,128)(2,1)}, bf16[2,4,16,512]{3,2,1,0:T(8,128)(2,1)S(1)}, u32[]{:S(2)}, u32[]{:S(2)}) collective-permute-start(bf16[2,4,16,512]{3,2,1,0:T(8,128)(2,1)} %bitcast.20), channel_id=1, source_target_pairs={{0,2},{1,3},{2,0},{3,1},{4,6},{5,7},{6,4},{7,5},{8,10},{9,11},{10,... | collective-permute-start | bytes 393224 | tf_op jit(solution)/shard_map/ppermute | solution.py:461
  2.7 24.0 %collective-permute-start.3 = (bf16[2,4,16,512]{3,2,1,0:T(8,128)(2,1)}, bf16[2,4,16,512]{3,2,1,0:T(8,128)(2,1)S(1)}, u32[]{:S(2)}, u32[]{:S(2)}) collective-permute-start(bf16[2,4,16,512]{3,2,1,0:T(8,128)(2,1)} %bitcast.21), channel_id=1, source_target_pairs={{0,6},{1,7},{2,4},{3,5},{4,2},{5,3},{6,0},{7,1},{8,14},{9,15},{10,... | collective-permute-start | bytes 393224 | tf_op jit(solution)/shard_map/ppermute | solution.py:461
  3.6 23.1 %collective-permute-start.4 = (bf16[2,4,16,512]{3,2,1,0:T(8,128)(2,1)}, bf16[2,4,16,512]{3,2,1,0:T(8,128)(2,1)S(1)}, u32[]{:S(2)}, u32[]{:S(2)}) collective-permute-start(bf16[2,4,16,512]{3,2,1,0:T(8,128)(2,1)} %bitcast.22), channel_id=1, source_target_pairs={{0,2},{1,3},{2,0},{3,1},{4,10},{5,11},{6,8},{7,9},{8,6},{9,7},{10,... | collective-permute-start | bytes 393224 | tf_op jit(solution)/shard_map/ppermute | solution.py:461
  7.4 19.4 %collective-permute-start = (bf16[6,4,16,512]{3,2,1,0:T(8,128)(2,1)}, bf16[6,4,16,512]{3,2,1,0:T(8,128)(2,1)S(1)}, u32[]{:S(2)}, u32[]{:S(2)}) collective-permute-start(bf16[6,4,16,512]{3,2,1,0:T(8,128)(2,1)} %get-tuple-element.28), channel_id=1, source_target_pairs={{0,4},{1,5},{2,6},{3,7},{4,0},{5,1},{6,2},{7,3},{8,12},{9,13},{10,... | collective-permute-start | bytes 1179656 | tf_op jit(solution)/shard_map/ppermute | solution.py:461
  7.7 20.4 %collective-permute-start.1 = (bf16[6,4,16,512]{3,2,1,0:T(8,128)(2,1)}, bf16[6,4,16,512]{3,2,1,0:T(8,128)(2,1)S(1)}, u32[]{:S(2)}, u32[]{:S(2)}) collective-permute-start(bf16[6,4,16,512]{3,2,1,0:T(8,128)(2,1)} %get-tuple-element.29), channel_id=1, source_target_pairs={{0,0},{1,1},{2,2},{3,3},{4,8},{5,9},{6,10},{7,11},{8,4},{9,5},{10,... | collective-permute-start | bytes 1179656 | tf_op jit(solution)/shard_map/ppermute | solution.py:461
  13.7 0.9 %copy-start.2 = (s32[1536,16]{0,1:T(8,128)S(1)}, s32[1536,16]{0,1:T(8,128)}, u32[]{:S(2)}) copy-start(s32[1536,16]{0,1:T(8,128)} %param.16) | copy-start | bytes 294916
  14.6 0.7 %copy-start.4 = (f32[512]{0:T(512)S(1)}, f32[512]{0:T(512)}, u32[]{:S(2)}) copy-start(f32[512]{0:T(512)} %param.19) | copy-start | bytes 6148
  15.3 0.7 %copy-start.5 = (f32[512]{0:T(512)S(1)}, f32[512]{0:T(512)}, u32[]{:S(2)}) copy-start(f32[512]{0:T(512)} %param.20) | copy-start | bytes 6148
  16.0 10.7 %copy-start.15 = (bf16[1,2,64,512]{3,2,1,0:T(8,128)(2,1)S(1)}, bf16[1,2,64,512]{3,2,1,0:T(8,128)(2,1)}, u32[]{:S(2)}) copy-start(bf16[1,2,64,512]{3,2,1,0:T(8,128)(2,1)} %param.17) | copy-start | bytes 393220
  26.7 4.2 %copy-start.7 = (bf16[512,1024]{1,0:T(8,128)(2,1)S(1)}, bf16[512,1024]{1,0:T(8,128)(2,1)}, u32[]{:S(2)}) copy-start(bf16[512,1024]{1,0:T(8,128)(2,1)} %get-tuple-element.41.wkv) | copy-start | bytes 3145732
  26.7 4.2 %copy-start.11 = (bf16[512,512]{1,0:T(8,128)(2,1)S(1)}, bf16[512,512]{1,0:T(8,128)(2,1)}, u32[]{:S(2)}) copy-start(bf16[512,512]{1,0:T(8,128)(2,1)} %get-tuple-element.40.wq) | copy-start | bytes 1572868
  26.7 4.2 %copy-start.12 = (bf16[512,512]{1,0:T(8,128)(2,1)S(1)}, bf16[512,512]{1,0:T(8,128)(2,1)}, u32[]{:S(2)}) copy-start(bf16[512,512]{1,0:T(8,128)(2,1)} %get-tuple-element.42.wo) | copy-start | bytes 1572868
  28.2 8.0 %collective-permute-start.5 = (bf16[12,64,512]{2,1,0:T(8,128)(2,1)S(1)}, bf16[12,64,512]{2,1,0:T(8,128)(2,1)S(1)}, u32[]{:S(2)}, u32[]{:S(2)}) collective-permute-start(bf16[12,64,512]{2,1,0:T(8,128)(2,1)S(1)} %constant_dynamic-update-slice_fusion.mine_ref), channel_id=1, source_target_pairs={{0,1},{1,0},{2,3},{3,2},{4,5},{5,4},{6,7},{7,6},{8,9},{9,8},{10,11... | collective-permute-start | bytes 2359304 | tf_op jit(solution)/shard_map/ppermute | solution.py:461
  30.9 1.0 %copy-start.13 = (bf16[512,512]{1,0:T(8,128)(2,1)S(1)}, bf16[512,512]{1,0:T(8,128)(2,1)}, u32[]{:S(2)}) copy-start(bf16[512,512]{1,0:T(8,128)(2,1)} %get-tuple-element.43.cwq) | copy-start | bytes 1572868
  32.0 4.2 %copy-start = (bf16[512,2048]{1,0:T(8,128)(2,1)S(1)}, bf16[512,2048]{1,0:T(8,128)(2,1)}, u32[]{:S(2)}) copy-start(bf16[512,2048]{1,0:T(8,128)(2,1)} %fin_hbm.1) | copy-start | bytes 6291460
  32.0 4.2 %copy-start.1 = (bf16[2048,512]{1,0:T(8,128)(2,1)S(1)}, bf16[2048,512]{1,0:T(8,128)(2,1)}, u32[]{:S(2)}) copy-start(bf16[2048,512]{1,0:T(8,128)(2,1)} %fout_hbm.1) | copy-start | bytes 6291460
  32.0 4.2 %copy-start.3 = (s32[3,2,4]{2,1,0:T(2,128)S(1)}, s32[3,2,4]{2,1,0:T(2,128)}, u32[]{:S(2)}) copy-start(s32[3,2,4]{2,1,0:T(2,128)} %list_ref.1) | copy-start | bytes 292
  32.0 4.2 %copy-start.6 = (f32[512]{0:T(512)S(1)}, f32[512]{0:T(512)}, u32[]{:S(2)}) copy-start(f32[512]{0:T(512)} %param.21) | copy-start | bytes 6148
  32.0 4.2 %copy-start.8 = (bf16[4,2,128,512]{3,2,1,0:T(8,128)(2,1)S(1)}, bf16[4,2,128,512]{3,2,1,0:T(8,128)(2,1)}, u32[]{:S(2)}) copy-start(bf16[4,2,128,512]{3,2,1,0:T(8,128)(2,1)} %get-tuple-element.37.refs_0_) | copy-start | bytes 3145732
  32.0 4.2 %copy-start.9 = (bf16[4,2,128,512]{3,2,1,0:T(8,128)(2,1)S(1)}, bf16[4,2,128,512]{3,2,1,0:T(8,128)(2,1)}, u32[]{:S(2)}) copy-start(bf16[4,2,128,512]{3,2,1,0:T(8,128)(2,1)} %get-tuple-element.45.refs_2_) | copy-start | bytes 3145732
  32.0 4.2 %copy-start.10 = (bf16[512,1024]{1,0:T(8,128)(2,1)S(1)}, bf16[512,1024]{1,0:T(8,128)(2,1)}, u32[]{:S(2)}) copy-start(bf16[512,1024]{1,0:T(8,128)(2,1)} %get-tuple-element.35.ckv_ref) | copy-start | bytes 3145732
  32.0 4.2 %copy-start.14 = (bf16[512,512]{1,0:T(8,128)(2,1)S(1)}, bf16[512,512]{1,0:T(8,128)(2,1)}, u32[]{:S(2)}) copy-start(bf16[512,512]{1,0:T(8,128)(2,1)} %get-tuple-element.36.cwo_ref) | copy-start | bytes 1572868

commit v4 on v3

--- a/solution.py
+++ b/solution.py
@@ -160,12 +160,11 @@
 
 
 def inner_kernel(
-    x_hbm, cover_hbm, gs_ref, gc_ref, wq_hbm, wkv_hbm, wo_hbm, cwq_hbm, ckv_hbm, cwo_hbm,
-    first_ref, cq_ref, sides_ref, cover_ref, wq, wkv, wo, cwq, ckv, cwo,
-    x_buf, sems,
+    x_hbm, cover_hbm, gs_ref, gc_ref, wq_hbm, wkv_hbm, wo_hbm, cwq_hbm,
+    first_ref, cq_ref,
+    x_buf, cover_ref, wq, wkv, wo, cwq, sems,
 ):
     strip = position()[0]
-    even = strip % 2 == 0
     row_count = x_hbm.shape[1]
     last = row_count - HALF
     start = first_cell(strip, row_count, cover_hbm.shape[1], cover_ref.shape[1])
@@ -179,10 +178,6 @@
             (wq_hbm, wq),
             (wo_hbm, wo),
             (cwq_hbm, cwq),
-            (x_hbm.at[:, pl.ds(jnp.where(even, last, 0), HALF)], sides_ref.at[0]),
-            (x_hbm.at[:, pl.ds(jnp.where(even, 0, last), HALF)], sides_ref.at[1]),
-            (ckv_hbm, ckv),
-            (cwo_hbm, cwo),
         ],
     )
     moves[0].wait()
@@ -217,13 +212,31 @@
 
 
 def edge_kernel(
-    row_ref, across_ref, sides_ref, cover_ref, gs_ref, gc_ref, wq, wkv, wo, cwq, first_ref, cq_ref, *, per_strip, cells
+    row_ref, across_ref, x_hbm, cover_hbm, gs_ref, gc_ref, wq_hbm, wkv_hbm, wo_hbm, cwq_hbm,
+    first_ref, cq_ref, sides_ref, cover_ref, wq, wkv, wo, cwq, sems,
 ):
     strip = position()[0]
+    row_count = x_hbm.shape[1]
+    per_strip = row_count // HALF
     strips = lax.axis_size("gx")
     even = strip % 2 == 0
     frames = sides_ref.shape[1]
-    start = first_cell(strip, per_strip * HALF, cells, cover_ref.shape[1])
+    start = first_cell(strip, row_count, cover_hbm.shape[1], cover_ref.shape[1])
+    last = row_count - HALF
+    moves = copies(
+        sems,
+        [
+            (x_hbm.at[:, pl.ds(jnp.where(even, last, 0), HALF)], sides_ref.at[0]),
+            (x_hbm.at[:, pl.ds(jnp.where(even, 0, last), HALF)], sides_ref.at[1]),
+            (cover_hbm.at[:, pl.ds(start, cover_ref.shape[1])], cover_ref),
+            (wkv_hbm, wkv),
+            (wq_hbm, wq),
+            (wo_hbm, wo),
+            (cwq_hbm, cwq),
+        ],
+    )
+    for move in moves[:2]:
+        move.wait()
     gs = gs_ref[...]
     parts, quads, cuboids, halos = [], [], [], []
     for n, halo_ref in enumerate((row_ref, across_ref)):
@@ -251,26 +264,33 @@
         wkv,
         wo,
         cwq,
+        moves[2:],
     )
     first_ref[...] = first.reshape(first_ref.shape)
     cq_ref[...] = cq.reshape(cq_ref.shape)
 
 
-def cross_kernel(states, list_ref, mine_ref, other_ref, ckv_ref, cwo_ref, gf_ref, fin_hbm, fout_hbm, *refs):
+def cross_kernel(states, list_ref, w0_ref, w1_ref, w2_ref, w3_ref, ckv_ref, cwo_ref, gf_ref, fin_hbm, fout_hbm, *refs):
     first_refs, cq_refs, refs = refs[:states], refs[states : 2 * states], refs[2 * states :]
-    out_hbm, first_buf, cq_buf, out_buf, fin_ref, fout_ref, sems, out_sems = refs
+    out_hbm, window, out_buf, fin_ref, fout_ref, sems, out_sems = refs
     moves = copies(sems, [(fin_hbm, fin_ref), (fout_hbm, fout_ref)])
     strip, side, core = position()
     features = cwo_ref.shape[0]
-
-    def gather(arrays, buf):
-        at = 0
-        for a in arrays:
-            buf[at : at + a.shape[0]] = a[...]
-            at += a.shape[0]
-
-    gather(first_refs, first_buf)
-    gather(cq_refs, cq_buf)
+    tiles = out_hbm.shape[1] // BX
+
+    def granule(refs, quad, j):
+        inner, edges = refs
+        at_top = strip % 2 == 0
+        if quad == 0:
+            return edges[jnp.where(at_top, 1, 0), j]
+        if quad == 2 * tiles - 1:
+            return edges[jnp.where(at_top, 0, 1), j]
+        return inner[quad - 1, j]
+
+    at = 0
+    for part in (w0_ref, w1_ref, w2_ref, w3_ref):
+        window[at : at + part.shape[0]] = part[...]
+        at += part.shape[0]
     toward_row = jnp.where(strip % 2 == 0, 1, -1)
 
     def entry(n):
@@ -278,14 +298,13 @@
         delta = e // 8 - strip
         column = e % 8
         e_side, e_core, sub = column // 4, (column // 2) % 2, column % 2
-        slot = jnp.where(delta == 0, 0, jnp.where(delta == toward_row, 2, 4))
-        slot = slot + jnp.where(e_side == side, 0, 1)
-        at = slot * 2 + sub
-        return jnp.where(e_core == core, mine_ref[at], other_ref[at])
-
-    tiles = out_hbm.shape[1] // BX
-    top = jnp.where(strip % 2 == 0, 4, 5)
-    slots = [(9 - top, 0), (1, 2), (3, top)]
+        same = e_side == side
+        near = jnp.where(delta == toward_row, 0, 1)
+        slot = jnp.where(same, 2, 4) + near
+        slot = jnp.where(delta == 0, jnp.where(same, 0, 1), slot)
+        half = window.shape[0] // 2
+        return window[jnp.where(e_core == core, 0, half) + slot * 2 + sub]
+
     kvs = []
     for n in range(2 * tiles):
         chosen = jnp.concatenate([entry(n * 4 + l) for l in range(4)], axis=0)
@@ -294,7 +313,7 @@
     for k in range(tiles):
         for j in range(2):
             kv = kvs[2 * k + j]
-            q = jnp.concatenate([cq_buf[s, j] for s in slots[k]], axis=0)
+            q = jnp.concatenate([granule(cq_refs, 2 * k + t, j) for t in range(2)], axis=0)
             mixed.append(attend(q, kv[:, :features], kv[:, features:], None))
     for move in moves:
         move.wait()
@@ -303,7 +322,9 @@
     step = 2048
     frames = out_buf.shape[0]
     for k in range(tiles):
-        first = jnp.concatenate([first_buf[s, j] for j in range(2) for s in slots[k]], axis=0)
+        first = jnp.concatenate(
+            [granule(first_refs, 2 * k + t, j) for j in range(2) for t in range(2)], axis=0
+        )
         both = jnp.concatenate(mixed[2 * k : 2 * k + 2], axis=0)
         second = (first.astype(F32) + dot(both, cwo_ref[...])).astype(BF16).astype(F32)
         normed = layer_norm(second, gf_ref[...]).astype(BF16)
@@ -377,49 +398,52 @@
         [
             state,
             state,
-            jax.ShapeDtypeStruct((2, frames, HALF, cols, features), BF16),
-            jax.ShapeDtypeStruct((cols, COVER_CELLS), jnp.int32),
-            *[jax.ShapeDtypeStruct(w.shape, w.dtype) for w in weights],
-        ],
-        [pltpu.VMEM((frames, row_count - BX, cols, features), BF16)],
-        [pltpu.SemaphoreType.DMA((10,))],
+        ],
+        [
+            pltpu.VMEM((frames, row_count - BX, cols, features), BF16),
+            pltpu.VMEM((cols, COVER_CELLS), jnp.int32),
+            *[pltpu.VMEM(w.shape, w.dtype) for w in weights],
+        ],
+        [pltpu.SemaphoreType.DMA((6,))],
         FULL,
         8000,
         10,
-        53,
+        56,
     )(x, cover, gs, gc, *weights)
 
 
-def edge_call(row, across, sides, cover_part, gs, gc, wq, wkv, wo, cwq, row_count, cells):
-    _, frames, _, cols, features = sides.shape
+def edge_call(row, across, x, cover, gs, gc, weights):
+    frames, _, cols, features = x.shape
     rows = frames * HALF * BY
     state = jax.ShapeDtypeStruct((2, cols // BY, rows, features), BF16)
     return call(
-        functools.partial(edge_kernel, per_strip=row_count // HALF, cells=cells),
-        [FULL] * 10,
+        edge_kernel,
+        [FULL, FULL, HBM, HBM, FULL, FULL, *[HBM] * 4],
         [state, state],
-        [],
-        [],
+        [
+            pltpu.VMEM((2, frames, HALF, cols, features), BF16),
+            pltpu.VMEM((cols, COVER_CELLS), jnp.int32),
+            *[pltpu.VMEM(w.shape, w.dtype) for w in weights],
+        ],
+        [pltpu.SemaphoreType.DMA((7,))],
         FULL,
         6000,
         4,
-        28,
-    )(row, across, sides, cover_part, gs, gc, wq, wkv, wo, cwq)
-
-
-def cross_call(listed, mine, other, ckv, cwo, gf, fin, fout, firsts, cqs, frames=4):
+        48,
+    )(row, across, x, cover, gs, gc, *weights)
+
+
+def cross_call(listed, windows, ckv, cwo, gf, fin, fout, firsts, cqs, frames=4):
     columns, rows, features = firsts[0].shape[1:]
     quads = sum(a.shape[0] for a in firsts)
-    held = pltpu.VMEM((quads, columns, rows, features), BF16)
     out = jax.ShapeDtypeStruct((frames, quads * HALF, columns * BY, features), BF16)
     count = 2 * len(firsts)
     return call(
         functools.partial(cross_kernel, len(firsts)),
-        [SCALARS, *[FULL] * 5, HBM, HBM, *[FULL] * count],
+        [SCALARS, *[FULL] * 7, HBM, HBM, *[FULL] * count],
         out,
         [
-            held,
-            held,
+            pltpu.VMEM((sum(w.shape[0] for w in windows), *windows[0].shape[1:]), BF16),
             pltpu.VMEM(out.shape, BF16),
             pltpu.VMEM(fin.shape, BF16),
             pltpu.VMEM(fout.shape, BF16),
@@ -429,7 +453,7 @@
         15000,
         12,
         40,
-    )(listed, mine, other, ckv, cwo, gf, fin, fout, *firsts, *cqs)
+    )(listed, *windows, ckv, cwo, gf, fin, fout, *firsts, *cqs)
 
 
 def shards(
@@ -469,12 +493,6 @@
     def to_side(s, h, c):
         return (s, 1 - h, c)
 
-    def to_row_side(s, h, c):
-        return (s ^ 1, 1 - h, c)
-
-    def to_across_side(s, h, c):
-        return (across(s), 1 - h, c)
-
     def to_core(s, h, c):
         return (s, h, 1 - c)
 
@@ -483,35 +501,36 @@
     cover = coverage.T
     gs = gain_self.reshape(1, features)
     gc = gain_cross.reshape(1, features)
+    weights = (self_wq, self_wkv, self_wo, cross_wq)
     barrier = lax.optimization_barrier
 
     to_near, to_far = pack_call(inputs, piece)
+    got_side = send(piece, to_side)
     got_row = send(to_near, to_row)
     got_across = send(to_far, to_across)
-    got_side = send(piece, to_side)
-    got_row_side = send(piece, to_row_side)
-    got_across_side = send(piece, to_across_side)
-    first_a, cq_a, sides, cover_part, *weights = inner_call(
+    first_a, cq_a = inner_call(
         inputs,
         cover,
         gs,
         gc,
-        (self_wq, self_wkv, self_wo, cross_wq, cross_wkv, cross_wo),
-    )
-    first_a, cq_a, got_row, got_across, got_side, got_row_side, got_across_side = barrier(
-        (first_a, cq_a, got_row, got_across, got_side, got_row_side, got_across_side)
-    )
-    pieces = [piece, got_side, got_row[frames:], got_row_side, got_across[frames:], got_across_side]
-    mine = jnp.concatenate([p.reshape(columns, tokens, features) for p in pieces], axis=0)
+        weights,
+    )
+    first_a, cq_a, got_row, got_across, got_side = barrier(
+        (first_a, cq_a, got_row, got_across, got_side)
+    )
+    passed = jnp.concatenate([got_row[frames:], got_across[frames:]], axis=0)
+    mine_late = send(passed, to_side)
+    mine = jnp.concatenate([piece, got_side, passed], axis=0)
     other = send(mine, to_core)
-    first_b, cq_b = edge_call(
-        got_row, got_across, sides, cover_part, gs, gc, *weights[:4], row_count, cover.shape[1]
-    )
+    first_b, cq_b = edge_call(got_row, got_across, inputs, cover, gs, gc, weights)
+    first_b, cq_b, mine_late = barrier((first_b, cq_b, mine_late))
+    other_late = send(mine_late, to_core)
+    windows = [w.reshape(-1, tokens, features) for w in (mine, mine_late, other, other_late)]
     return cross_call(
         cross_list,
-        mine,
-        other,
-        *weights[4:6],
+        windows,
+        cross_wkv,
+        cross_wo,
         gain_ffn.reshape(1, features),
         ffn_in,
         ffn_out,

time: 53 us -> 52.3 us (0.987)
  the two profiles are of different devices: /device:TPU:169 before, /device:TPU:35 now
where the time goes in v4:
time: 52.3 us; the launch traced here: 52.2 us
  Pallas kernels  33.4 us (64%)
  starting transfers between devices  11.4 us (22%)
  waiting for transfers between devices  6.7 us (13%)
    pallas_call x1, Pallas kernels, cross_call(): call(functools.partial(cross_kernel, len(firsts)), [SCALARS, *[FULL] * 7,...  16.4 us
    ppermute x6, starting transfers between devices, send(): return lax.ppermute(array, ('gx', 'gy'), pairs(strips, target))  11.4 us
    pallas_call x1, Pallas kernels, inner_call(): call(inner_kernel, [HBM, HBM, FULL, FULL, *[HBM] * len(weights)], [state,...  9.89 us
    ppermute x6, waiting for transfers between devices, send(): return lax.ppermute(array, ('gx', 'gy'), pairs(strips, target))  6.7 us
    pallas_call x1, Pallas kernels, edge_call(): call(edge_kernel, [FULL, FULL, HBM, HBM, FULL, FULL, *[HBM] * 4], [state,...  5.02 us
    pallas_call x1, Pallas kernels, pack_call(): pl.pallas_call(pack_kernel, in_specs=[ANY, ANY], out_specs=[FULL, FULL],...  2.05 us
  transfers between devices with their start and end apart: 6, of which 3 were waited for; matrix products, arithmetic and copies ran while one was open for 0% of the time, Pallas kernels for 33%

profile of v4, /device:TPU:35, one launch (start us, length us, event | category | flops | bytes accessed | tf_op | source)
XLA Modules:
  0.0 52.2 jit_solution(16606019948386199889)
XLA Ops:
  0.0 1.8 %collective-permute-start.2 = (bf16[2,4,16,512]{3,2,1,0:T(8,128)(2,1)}, bf16[2,4,16,512]{3,2,1,0:T(8,128)(2,1)S(1)}, u32[]{:S(2)}, u32[]{:S(2)}) collective-permute-start(bf16[2,4,16,512]{3,2,1,0:T(8,128)(2,1)} %bitcast.24), channel_id=1, source_target_pairs={{0,2},{1,3},{2,0},{3,1},{4,6},{5,7},{6,4},{7,5},{8,10},{9,11},{10,... | collective-permute-start | bytes 393224 | tf_op jit(solution)/shard_map/ppermute | solution.py:485
  1.8 2.1 %shard_map.146 = (bf16[6,4,16,512]{3,2,1,0:T(8,128)(2,1)}, bf16[6,4,16,512]{3,2,1,0:T(8,128)(2,1)}) custom-call(bf16[4,24,16,512]{3,2,1,0:T(8,128)(2,1)} %x_hbm.5, bf16[2,4,16,512]{3,2,1,0:T(8,128)(2,1)} %bitcast.25), custom_call_target="tpu_custom_call" | custom-call | bytes 2097152 | tf_op jit(solution)/shard_map/pallas_call | solution.py:380
  3.9 1.2 %collective-permute-start = (bf16[6,4,16,512]{3,2,1,0:T(8,128)(2,1)}, bf16[6,4,16,512]{3,2,1,0:T(8,128)(2,1)S(1)}, u32[]{:S(2)}, u32[]{:S(2)}) collective-permute-start(bf16[6,4,16,512]{3,2,1,0:T(8,128)(2,1)} %get-tuple-element.21), channel_id=1, source_target_pairs={{0,4},{1,5},{2,6},{3,7},{4,0},{5,1},{6,2},{7,3},{8,12},{9,13},{10,... | collective-permute-start | bytes 1179656 | tf_op jit(solution)/shard_map/ppermute | solution.py:485
  5.1 3.2 %collective-permute-start.1 = (bf16[6,4,16,512]{3,2,1,0:T(8,128)(2,1)}, bf16[6,4,16,512]{3,2,1,0:T(8,128)(2,1)S(1)}, u32[]{:S(2)}, u32[]{:S(2)}) collective-permute-start(bf16[6,4,16,512]{3,2,1,0:T(8,128)(2,1)} %get-tuple-element.22), channel_id=1, source_target_pairs={{0,0},{1,1},{2,2},{3,3},{4,8},{5,9},{6,10},{7,11},{8,4},{9,5},{10,... | collective-permute-start | bytes 1179656 | tf_op jit(solution)/shard_map/ppermute | solution.py:485
  8.4 0.0 copy-start.16
  8.4 0.0 copy-start.3
  8.4 0.0 copy-start.6
  8.4 0.0 copy-start.7
  8.4 0.0 copy-start.9
  8.4 0.0 copy-start.12
  8.4 9.9 %shard_map.145 = (bf16[4,2,128,512]{3,2,1,0:T(8,128)(2,1)}, bf16[4,2,128,512]{3,2,1,0:T(8,128)(2,1)}) custom-call(bf16[4,24,16,512]{3,2,1,0:T(8,128)(2,1)} %x_hbm.5, s32[16,1536]{1,0:T(8,128)} %bitcast.15, f32[1,512]{1,0:T(1,128)} %bitcast.17, f32[1,512]{1,0:T(1,128)} %bitcast.19, bf16[512,512]{1,0:T(8,128)(2,1)} %wq_hbm.3, bf16[512,1024]{1,0:T(8,128)(2,1)} %wkv_hbm.3, ...), custom_call_target="tpu_custom_call" | custom-call | flops 8000000000 | bytes 10485760 | tf_op jit(solution)/shard_map/pallas_call | solution.py:395
  18.4 0.0 copy-start
  18.4 0.0 copy-start.5
  18.4 0.0 copy-start.11
  18.4 0.0 collective-permute-done.2
  18.4 4.6 %collective-permute-done.row_ref = bf16[6,4,16,512]{3,2,1,0:T(8,128)(2,1)S(1)} collective-permute-done((bf16[6,4,16,512]{3,2,1,0:T(8,128)(2,1)}, bf16[6,4,16,512]{3,2,1,0:T(8,128)(2,1)S(1)}, u32[]{:S(2)}, u32[]{:S(2)}) %collective-permute-start) | collective-permute-done | bytes 393248 | tf_op jit(solution)/shard_map/ppermute | solution.py:485
  23.0 1.0 %collective-permute-done.1.across_ref = bf16[6,4,16,512]{3,2,1,0:T(8,128)(2,1)S(1)} collective-permute-done((bf16[6,4,16,512]{3,2,1,0:T(8,128)(2,1)}, bf16[6,4,16,512]{3,2,1,0:T(8,128)(2,1)S(1)}, u32[]{:S(2)}, u32[]{:S(2)}) %collective-permute-start.1) | collective-permute-done | bytes 393248 | tf_op jit(solution)/shard_map/ppermute | solution.py:485
  24.1 0.5 collective-permute-start.3
  24.6 0.0 copy-done.16
  24.6 0.1 pad_maximum_fusion.1
  24.7 0.0 copy-start.1
  24.7 0.0 copy-start.2
  24.7 0.0 copy-start.4
  24.7 0.0 copy-start.8
  24.7 0.0 copy-start.10
  24.7 0.0 copy-start.13
  24.7 0.0 copy-start.14
  24.7 0.0 copy-start.15
  24.8 2.4 %collective-permute-start.4 = (bf16[8,4,16,512]{3,2,1,0:T(8,128)(2,1)S(1)}, bf16[8,4,16,512]{3,2,1,0:T(8,128)(2,1)S(1)}, u32[]{:S(2)}, u32[]{:S(2)}) collective-permute-start(bf16[8,4,16,512]{3,2,1,0:T(8,128)(2,1)S(1)} %pad_maximum_fusion.1), channel_id=1, source_target_pairs={{0,1},{1,0},{2,3},{3,2},{4,5},{5,4},{6,7},{7,6},{8,9},{9,8},{10,11... | collective-permute-start | bytes 1572872 | tf_op jit(solution)/shard_map/ppermute | solution.py:485
  27.2 0.0 copy-done.3
  27.2 0.0 copy-done.6
  27.2 0.0 copy-done.7
  27.2 0.0 copy-done.9
  27.2 0.0 copy-done.12
  27.2 0.0 copy-done
  27.2 0.0 copy-done.5
  27.2 0.0 copy-done.11
  27.2 5.0 %shard_map.147 = (bf16[2,2,128,512]{3,2,1,0:T(8,128)(2,1)S(1)}, bf16[2,2,128,512]{3,2,1,0:T(8,128)(2,1)S(1)}) custom-call(bf16[6,4,16,512]{3,2,1,0:T(8,128)(2,1)S(1)} %collective-permute-done.row_ref, bf16[6,4,16,512]{3,2,1,0:T(8,128)(2,1)S(1)} %collective-permute-done.1.across_ref, bf16[4,24,16,512]{3,2,1,0:T(8,128)(2,1)S(1)} %copy-done, ...), custom_call_target="tpu_custom_call" | custom-call | flops 6000000000 | bytes 4194304 | tf_op jit(solution)/shard_map/pallas_call | solution.py:419
  32.3 0.0 collective-permute-done.3
  32.3 2.1 %collective-permute-start.5 = (bf16[4,4,16,512]{3,2,1,0:T(8,128)(2,1)S(1)}, bf16[4,4,16,512]{3,2,1,0:T(8,128)(2,1)S(1)}, u32[]{:S(2)}, u32[]{:S(2)}) collective-permute-start(bf16[4,4,16,512]{3,2,1,0:T(8,128)(2,1)S(1)} %collective-permute-done.3), channel_id=1, source_target_pairs={{0,1},{1,0},{2,3},{3,2},{4,5},{5,4},{6,7},{7,6},{8,9},{9,8},{10,11... | collective-permute-start | bytes 786440 | tf_op jit(solution)/shard_map/ppermute | solution.py:485
  34.4 0.1 pad_maximum_fusion.w0_ref
  34.5 1.1 %collective-permute-done.5 = bf16[4,4,16,512]{3,2,1,0:T(8,128)(2,1)S(1)} collective-permute-done((bf16[4,4,16,512]{3,2,1,0:T(8,128)(2,1)S(1)}, bf16[4,4,16,512]{3,2,1,0:T(8,128)(2,1)S(1)}, u32[]{:S(2)}, u32[]{:S(2)}) %collective-permute-start.5) | collective-permute-done | bytes 262176 | tf_op jit(solution)/shard_map/ppermute | solution.py:485
  35.5 0.0 collective-permute-done.4
  35.5 0.0 copy-done.1
  35.6 0.0 copy-done.2
  35.6 0.0 copy-done.4
  35.6 0.0 copy-done.8
  35.6 16.4 %shard_map.148 = bf16[4,24,16,512]{3,2,1,0:T(8,128)(2,1)} custom-call(s32[3,2,4]{2,1,0:T(2,128)S(1)} %copy-done.10, bf16[8,64,512]{2,1,0:T(8,128)(2,1)S(1)} %pad_maximum_fusion.w0_ref, bf16[4,64,512]{2,1,0:T(8,128)(2,1)S(1)} %bitcast.13, bf16[8,64,512]{2,1,0:T(8,128)(2,1)S(1)} %bitcast.12, bf16[4,64,512]{2,1,0:T(8,128)(2,1)S(1)} %bitcast.14, ...), custom_call_target="tpu_custom_call" | custom-call | flops 15000000512 | bytes 12582912 | tf_op jit(solution)/shard_map/pallas_call | solution.py:441
  (7 shorter events, 0.1 us)
Async XLA Ops:
  0.0 18.4 %collective-permute-start.2 = (bf16[2,4,16,512]{3,2,1,0:T(8,128)(2,1)}, bf16[2,4,16,512]{3,2,1,0:T(8,128)(2,1)S(1)}, u32[]{:S(2)}, u32[]{:S(2)}) collective-permute-start(bf16[2,4,16,512]{3,2,1,0:T(8,128)(2,1)} %bitcast.24), channel_id=1, source_target_pairs={{0,2},{1,3},{2,0},{3,1},{4,6},{5,7},{6,4},{7,5},{8,10},{9,11},{10,... | collective-permute-start | bytes 393224 | tf_op jit(solution)/shard_map/ppermute | solution.py:485
  3.9 19.1 %collective-permute-start = (bf16[6,4,16,512]{3,2,1,0:T(8,128)(2,1)}, bf16[6,4,16,512]{3,2,1,0:T(8,128)(2,1)S(1)}, u32[]{:S(2)}, u32[]{:S(2)}) collective-permute-start(bf16[6,4,16,512]{3,2,1,0:T(8,128)(2,1)} %get-tuple-element.21), channel_id=1, source_target_pairs={{0,4},{1,5},{2,6},{3,7},{4,0},{5,1},{6,2},{7,3},{8,12},{9,13},{10,... | collective-permute-start | bytes 1179656 | tf_op jit(solution)/shard_map/ppermute | solution.py:485
  5.1 18.9 %collective-permute-start.1 = (bf16[6,4,16,512]{3,2,1,0:T(8,128)(2,1)}, bf16[6,4,16,512]{3,2,1,0:T(8,128)(2,1)S(1)}, u32[]{:S(2)}, u32[]{:S(2)}) collective-permute-start(bf16[6,4,16,512]{3,2,1,0:T(8,128)(2,1)} %get-tuple-element.22), channel_id=1, source_target_pairs={{0,0},{1,1},{2,2},{3,3},{4,8},{5,9},{6,10},{7,11},{8,4},{9,5},{10,... | collective-permute-start | bytes 1179656 | tf_op jit(solution)/shard_map/ppermute | solution.py:485
  8.4 16.2 %copy-start.16 = (bf16[1,2,64,512]{3,2,1,0:T(8,128)(2,1)S(1)}, bf16[1,2,64,512]{3,2,1,0:T(8,128)(2,1)}, u32[]{:S(2)}) copy-start(bf16[1,2,64,512]{3,2,1,0:T(8,128)(2,1)} %param.17) | copy-start | bytes 393220
  8.4 18.8 %copy-start.3 = (bf16[512,1024]{1,0:T(8,128)(2,1)S(1)}, bf16[512,1024]{1,0:T(8,128)(2,1)}, u32[]{:S(2)}) copy-start(bf16[512,1024]{1,0:T(8,128)(2,1)} %wkv_hbm.3) | copy-start | bytes 3145732
  8.4 18.8 %copy-start.6 = (bf16[512,512]{1,0:T(8,128)(2,1)S(1)}, bf16[512,512]{1,0:T(8,128)(2,1)}, u32[]{:S(2)}) copy-start(bf16[512,512]{1,0:T(8,128)(2,1)} %wo_hbm.3) | copy-start | bytes 1572868
  8.4 18.8 %copy-start.7 = (bf16[512,512]{1,0:T(8,128)(2,1)S(1)}, bf16[512,512]{1,0:T(8,128)(2,1)}, u32[]{:S(2)}) copy-start(bf16[512,512]{1,0:T(8,128)(2,1)} %cwq_hbm.3) | copy-start | bytes 1572868
  8.4 18.8 %copy-start.9 = (s32[1536,16]{0,1:T(8,128)S(1)}, s32[1536,16]{0,1:T(8,128)}, u32[]{:S(2)}) copy-start(s32[1536,16]{0,1:T(8,128)} %param.16) | copy-start | bytes 294916
  8.4 18.7 %copy-start.12 = (f32[512]{0:T(512)S(1)}, f32[512]{0:T(512)}, u32[]{:S(2)}) copy-start(f32[512]{0:T(512)} %param.20) | copy-start | bytes 6148
  18.4 8.8 %copy-start = (bf16[4,24,16,512]{3,2,1,0:T(8,128)(2,1)S(1)}, bf16[4,24,16,512]{3,2,1,0:T(8,128)(2,1)}, u32[]{:S(2)}) copy-start(bf16[4,24,16,512]{3,2,1,0:T(8,128)(2,1)} %x_hbm.5) | copy-start | bytes 4718596
  18.4 8.8 %copy-start.5 = (bf16[512,512]{1,0:T(8,128)(2,1)S(1)}, bf16[512,512]{1,0:T(8,128)(2,1)}, u32[]{:S(2)}) copy-start(bf16[512,512]{1,0:T(8,128)(2,1)} %wq_hbm.3) | copy-start | bytes 1572868
  18.4 8.8 %copy-start.11 = (f32[512]{0:T(512)S(1)}, f32[512]{0:T(512)}, u32[]{:S(2)}) copy-start(f32[512]{0:T(512)} %param.19) | copy-start | bytes 6148
  24.1 8.2 %collective-permute-start.3 = (bf16[4,4,16,512]{3,2,1,0:T(8,128)(2,1)S(1)}, bf16[4,4,16,512]{3,2,1,0:T(8,128)(2,1)S(1)}, u32[]{:S(2)}, u32[]{:S(2)}) collective-permute-start(bf16[4,4,16,512]{3,2,1,0:T(8,128)(2,1)S(1)} %pad_maximum_fusion.2), channel_id=1, source_target_pairs={{0,2},{1,3},{2,0},{3,1},{4,6},{5,7},{6,4},{7,5},{8,10},{9,11},{10,... | collective-permute-start | bytes 786440 | tf_op jit(solution)/shard_map/ppermute | solution.py:485
  24.7 10.9 %copy-start.1 = (bf16[512,2048]{1,0:T(8,128)(2,1)S(1)}, bf16[512,2048]{1,0:T(8,128)(2,1)}, u32[]{:S(2)}) copy-start(bf16[512,2048]{1,0:T(8,128)(2,1)} %fin_hbm.1) | copy-start | bytes 6291460
  24.7 10.9 %copy-start.2 = (bf16[2048,512]{1,0:T(8,128)(2,1)S(1)}, bf16[2048,512]{1,0:T(8,128)(2,1)}, u32[]{:S(2)}) copy-start(bf16[2048,512]{1,0:T(8,128)(2,1)} %fout_hbm.1) | copy-start | bytes 6291460
  24.7 10.9 %copy-start.4 = (bf16[512,1024]{1,0:T(8,128)(2,1)S(1)}, bf16[512,1024]{1,0:T(8,128)(2,1)}, u32[]{:S(2)}) copy-start(bf16[512,1024]{1,0:T(8,128)(2,1)} %ckv_ref.1) | copy-start | bytes 3145732
  24.7 10.9 %copy-start.8 = (bf16[512,512]{1,0:T(8,128)(2,1)S(1)}, bf16[512,512]{1,0:T(8,128)(2,1)}, u32[]{:S(2)}) copy-start(bf16[512,512]{1,0:T(8,128)(2,1)} %cwo_ref.1) | copy-start | bytes 1572868
  24.7 10.9 %copy-start.10 = (s32[3,2,4]{2,1,0:T(2,128)S(1)}, s32[3,2,4]{2,1,0:T(2,128)}, u32[]{:S(2)}) copy-start(s32[3,2,4]{2,1,0:T(2,128)} %list_ref.1) | copy-start | bytes 292
  24.7 10.9 %copy-start.13 = (f32[512]{0:T(512)S(1)}, f32[512]{0:T(512)}, u32[]{:S(2)}) copy-start(f32[512]{0:T(512)} %param.21) | copy-start | bytes 6148
  24.7 10.9 %copy-start.14 = (bf16[4,2,128,512]{3,2,1,0:T(8,128)(2,1)S(1)}, bf16[4,2,128,512]{3,2,1,0:T(8,128)(2,1)}, u32[]{:S(2)}) copy-start(bf16[4,2,128,512]{3,2,1,0:T(8,128)(2,1)} %get-tuple-element.29.refs_0_) | copy-start | bytes 3145732
  24.7 10.9 %copy-start.15 = (bf16[4,2,128,512]{3,2,1,0:T(8,128)(2,1)S(1)}, bf16[4,2,128,512]{3,2,1,0:T(8,128)(2,1)}, u32[]{:S(2)}) copy-start(bf16[4,2,128,512]{3,2,1,0:T(8,128)(2,1)} %get-tuple-element.31.refs_2_) | copy-start | bytes 3145732
  24.8 10.8 %collective-permute-start.4 = (bf16[8,4,16,512]{3,2,1,0:T(8,128)(2,1)S(1)}, bf16[8,4,16,512]{3,2,1,0:T(8,128)(2,1)S(1)}, u32[]{:S(2)}, u32[]{:S(2)}) collective-permute-start(bf16[8,4,16,512]{3,2,1,0:T(8,128)(2,1)S(1)} %pad_maximum_fusion.1), channel_id=1, source_target_pairs={{0,1},{1,0},{2,3},{3,2},{4,5},{5,4},{6,7},{7,6},{8,9},{9,8},{10,11... | collective-permute-start | bytes 1572872 | tf_op jit(solution)/shard_map/ppermute | solution.py:485
  32.3 3.3 %collective-permute-start.5 = (bf16[4,4,16,512]{3,2,1,0:T(8,128)(2,1)S(1)}, bf16[4,4,16,512]{3,2,1,0:T(8,128)(2,1)S(1)}, u32[]{:S(2)}, u32[]{:S(2)}) collective-permute-start(bf16[4,4,16,512]{3,2,1,0:T(8,128)(2,1)S(1)} %collective-permute-done.3), channel_id=1, source_target_pairs={{0,1},{1,0},{2,3},{3,2},{4,5},{5,4},{6,7},{7,6},{8,9},{9,8},{10,11... | collective-permute-start | bytes 786440 | tf_op jit(solution)/shard_map/ppermute | solution.py:485

commit v5 on v4

--- a/solution.py
+++ b/solution.py
@@ -270,7 +270,7 @@
     cq_ref[...] = cq.reshape(cq_ref.shape)
 
 
-def cross_kernel(states, list_ref, w0_ref, w1_ref, w2_ref, w3_ref, ckv_ref, cwo_ref, gf_ref, fin_hbm, fout_hbm, *refs):
+def cross_kernel(states, list_ref, w0_ref, w1_ref, w2_ref, w3_ref, w4_ref, w5_ref, ckv_ref, cwo_ref, gf_ref, fin_hbm, fout_hbm, *refs):
     first_refs, cq_refs, refs = refs[:states], refs[states : 2 * states], refs[2 * states :]
     out_hbm, window, out_buf, fin_ref, fout_ref, sems, out_sems = refs
     moves = copies(sems, [(fin_hbm, fin_ref), (fout_hbm, fout_ref)])
@@ -288,7 +288,7 @@
         return inner[quad - 1, j]
 
     at = 0
-    for part in (w0_ref, w1_ref, w2_ref, w3_ref):
+    for part in (w0_ref, w1_ref, w2_ref, w3_ref, w4_ref, w5_ref):
         window[at : at + part.shape[0]] = part[...]
         at += part.shape[0]
     toward_row = jnp.where(strip % 2 == 0, 1, -1)
@@ -440,7 +440,7 @@
     count = 2 * len(firsts)
     return call(
         functools.partial(cross_kernel, len(firsts)),
-        [SCALARS, *[FULL] * 7, HBM, HBM, *[FULL] * count],
+        [SCALARS, *[FULL] * 9, HBM, HBM, *[FULL] * count],
         out,
         [
             pltpu.VMEM((sum(w.shape[0] for w in windows), *windows[0].shape[1:]), BF16),
@@ -515,17 +515,21 @@
         gc,
         weights,
     )
-    first_a, cq_a, got_row, got_across, got_side = barrier(
-        (first_a, cq_a, got_row, got_across, got_side)
-    )
-    passed = jnp.concatenate([got_row[frames:], got_across[frames:]], axis=0)
-    mine_late = send(passed, to_side)
-    mine = jnp.concatenate([piece, got_side, passed], axis=0)
+    first_a, cq_a, got_row, got_side = barrier((first_a, cq_a, got_row, got_side))
+    row_piece = got_row[frames:]
+    late_row = send(row_piece, to_side)
+    mine = jnp.concatenate([piece, got_side, row_piece], axis=0)
     other = send(mine, to_core)
+    got_across, first_a, cq_a = barrier((got_across, first_a, cq_a))
+    across_piece = got_across[frames:]
+    late_across = send(across_piece, to_side)
+    other_across = send(across_piece, to_core)
     first_b, cq_b = edge_call(got_row, got_across, inputs, cover, gs, gc, weights)
-    first_b, cq_b, mine_late = barrier((first_b, cq_b, mine_late))
-    other_late = send(mine_late, to_core)
-    windows = [w.reshape(-1, tokens, features) for w in (mine, mine_late, other, other_late)]
+    first_b, cq_b, late_row, late_across = barrier((first_b, cq_b, late_row, late_across))
+    late = jnp.concatenate([late_row, late_across], axis=0)
+    other_late = send(late, to_core)
+    windows = [mine, across_piece, late, other, other_across, other_late]
+    windows = [w.reshape(-1, tokens, features) for w in windows]
     return cross_call(
         cross_list,
         windows,

time: 52.3 us -> 53.4 us (1.021)
  the two profiles are of different devices: /device:TPU:35 before, /device:TPU:169 now
where the time goes in v5:
time: 53.4 us; the launch traced here: 52.6 us
  Pallas kernels  33.8 us (63%)
  starting transfers between devices  12.2 us (23%)
  waiting for transfers between devices  5.86 us (11%)
    pallas_call x1, Pallas kernels, cross_call(): call(functools.partial(cross_kernel, len(firsts)), [SCALARS, *[FULL] * 9,...  16.5 us
    ppermute x8, starting transfers between devices, send(): return lax.ppermute(array, ('gx', 'gy'), pairs(strips, target))  12.2 us
    pallas_call x1, Pallas kernels, inner_call(): call(inner_kernel, [HBM, HBM, FULL, FULL, *[HBM] * len(weights)], [state,...  10.2 us
    ppermute x8, waiting for transfers between devices, send(): return lax.ppermute(array, ('gx', 'gy'), pairs(strips, target))  5.86 us
    pallas_call x1, Pallas kernels, edge_call(): call(edge_kernel, [FULL, FULL, HBM, HBM, FULL, FULL, *[HBM] * 4], [state,...  5.03 us
    pallas_call x1, Pallas kernels, pack_call(): pl.pallas_call(pack_kernel, in_specs=[ANY, ANY], out_specs=[FULL, FULL],...  2.04 us
  transfers between devices with their start and end apart: 8, of which 2 were waited for; matrix products, arithmetic and copies ran while one was open for 0% of the time, Pallas kernels for 33%

profile of v5, /device:TPU:169, one launch (start us, length us, event | category | flops | bytes accessed | tf_op | source)
XLA Modules:
  0.0 52.6 jit_solution(15917031814806692882)
XLA Ops:
  0.0 2.7 %collective-permute-start.1 = (bf16[2,4,16,512]{3,2,1,0:T(8,128)(2,1)}, bf16[2,4,16,512]{3,2,1,0:T(8,128)(2,1)S(1)}, u32[]{:S(2)}, u32[]{:S(2)}) collective-permute-start(bf16[2,4,16,512]{3,2,1,0:T(8,128)(2,1)} %bitcast.26), channel_id=1, source_target_pairs={{0,2},{1,3},{2,0},{3,1},{4,6},{5,7},{6,4},{7,5},{8,10},{9,11},{10,... | collective-permute-start | bytes 393224 | tf_op jit(solution)/shard_map/ppermute | solution.py:485
  2.7 2.0 %shard_map.146 = (bf16[6,4,16,512]{3,2,1,0:T(8,128)(2,1)}, bf16[6,4,16,512]{3,2,1,0:T(8,128)(2,1)}) custom-call(bf16[4,24,16,512]{3,2,1,0:T(8,128)(2,1)} %x_hbm.5, bf16[2,4,16,512]{3,2,1,0:T(8,128)(2,1)} %bitcast.27), custom_call_target="tpu_custom_call" | custom-call | bytes 2097152 | tf_op jit(solution)/shard_map/pallas_call | solution.py:380
  4.8 0.4 collective-permute-start
  5.2 2.9 %collective-permute-start.2 = (bf16[6,4,16,512]{3,2,1,0:T(8,128)(2,1)}, bf16[6,4,16,512]{3,2,1,0:T(8,128)(2,1)S(1)}, u32[]{:S(2)}, u32[]{:S(2)}) collective-permute-start(bf16[6,4,16,512]{3,2,1,0:T(8,128)(2,1)} %get-tuple-element.27), channel_id=1, source_target_pairs={{0,0},{1,1},{2,2},{3,3},{4,8},{5,9},{6,10},{7,11},{8,4},{9,5},{10,... | collective-permute-start | bytes 1179656 | tf_op jit(solution)/shard_map/ppermute | solution.py:485
  8.1 0.0 copy-start
  8.1 0.0 copy-start.3
  8.2 0.0 copy-start.5
  8.2 0.0 copy-start.6
  8.2 0.0 copy-start.7
  8.2 0.0 copy-start.9
  8.2 0.0 copy-start.11
  8.2 0.0 copy-start.12
  8.2 10.2 %shard_map.145 = (bf16[4,2,128,512]{3,2,1,0:T(8,128)(2,1)}, bf16[4,2,128,512]{3,2,1,0:T(8,128)(2,1)}) custom-call(bf16[4,24,16,512]{3,2,1,0:T(8,128)(2,1)} %x_hbm.5, s32[16,1536]{1,0:T(8,128)} %bitcast.18, f32[1,512]{1,0:T(1,128)} %bitcast.20, f32[1,512]{1,0:T(1,128)} %bitcast.22, bf16[512,512]{1,0:T(8,128)(2,1)} %wq_hbm.3, bf16[512,1024]{1,0:T(8,128)(2,1)} %wkv_hbm.3, ...), custom_call_target="tpu_custom_call" | custom-call | flops 8000000000 | bytes 10485760 | tf_op jit(solution)/shard_map/pallas_call | solution.py:395
  18.4 0.0 collective-permute-done.1
  18.4 0.0 collective-permute-done.row_ref
  18.4 4.6 %collective-permute-done.2.across_ref = bf16[6,4,16,512]{3,2,1,0:T(8,128)(2,1)S(1)} collective-permute-done((bf16[6,4,16,512]{3,2,1,0:T(8,128)(2,1)}, bf16[6,4,16,512]{3,2,1,0:T(8,128)(2,1)S(1)}, u32[]{:S(2)}, u32[]{:S(2)}) %collective-permute-start.2) | collective-permute-done | bytes 393248 | tf_op jit(solution)/shard_map/ppermute | solution.py:485
  23.1 0.0 copy-start.16
  23.1 2.1 %collective-permute-start.3 = (bf16[2,4,16,512]{3,2,1,0:T(8,128)(2,1)S(1)}, bf16[2,4,16,512]{3,2,1,0:T(8,128)(2,1)S(1)}, u32[]{:S(2)}, u32[]{:S(2)}) collective-permute-start(bf16[2,4,16,512]{3,2,1,0:T(8,128)(2,1)S(1)} %slice.6), channel_id=1, source_target_pairs={{0,2},{1,3},{2,0},{3,1},{4,6},{5,7},{6,4},{7,5},{8,10},{9,11},{10,... | collective-permute-start | bytes 393224 | tf_op jit(solution)/shard_map/ppermute | solution.py:485
  25.2 0.9 %collective-permute-start.4 = (bf16[2,4,16,512]{3,2,1,0:T(8,128)(2,1)S(1)}, bf16[2,4,16,512]{3,2,1,0:T(8,128)(2,1)S(1)}, u32[]{:S(2)}, u32[]{:S(2)}) collective-permute-start(bf16[2,4,16,512]{3,2,1,0:T(8,128)(2,1)S(1)} %slice.7), channel_id=1, source_target_pairs={{0,2},{1,3},{2,0},{3,1},{4,6},{5,7},{6,4},{7,5},{8,10},{9,11},{10,... | collective-permute-start | bytes 393224 | tf_op jit(solution)/shard_map/ppermute | solution.py:485
  26.2 0.0 copy-done
  26.2 0.0 copy-done.3
  26.2 0.0 copy-done.5
  26.2 0.0 copy-done.6
  26.2 0.0 copy-done.7
  26.2 0.0 copy-start.2
  26.2 0.0 copy-start.4
  26.2 0.0 copy-start.8
  26.3 0.0 copy-start.14
  26.3 5.0 %shard_map.147 = (bf16[2,2,128,512]{3,2,1,0:T(8,128)(2,1)S(1)}, bf16[2,2,128,512]{3,2,1,0:T(8,128)(2,1)S(1)}) custom-call(bf16[6,4,16,512]{3,2,1,0:T(8,128)(2,1)S(1)} %collective-permute-done.row_ref, bf16[6,4,16,512]{3,2,1,0:T(8,128)(2,1)S(1)} %collective-permute-done.2.across_ref, bf16[4,24,16,512]{3,2,1,0:T(8,128)(2,1)S(1)} %copy-done, ...), custom_call_target="tpu_custom_call" | custom-call | flops 6000000000 | bytes 4194304 | tf_op jit(solution)/shard_map/pallas_call | solution.py:419
  31.3 0.0 copy-start.1
  31.3 0.0 copy-start.10
  31.4 0.0 copy-start.13
  31.4 2.5 %collective-permute-start.5 = (bf16[6,4,16,512]{3,2,1,0:T(8,128)(2,1)S(1)}, bf16[6,4,16,512]{3,2,1,0:T(8,128)(2,1)S(1)}, u32[]{:S(2)}, u32[]{:S(2)}) collective-permute-start(bf16[6,4,16,512]{3,2,1,0:T(8,128)(2,1)S(1)} %pad_maximum_fusion.1), channel_id=1, source_target_pairs={{0,1},{1,0},{2,3},{3,2},{4,5},{5,4},{6,7},{7,6},{8,9},{9,8},{10,11... | collective-permute-start | bytes 1179656 | tf_op jit(solution)/shard_map/ppermute | solution.py:485
  33.9 0.0 collective-permute-done.3
  33.9 0.0 collective-permute-done.4
  34.0 0.2 collective-permute-start.7
  34.2 0.4 collective-permute-start.6
  34.6 1.2 %collective-permute-done.6 = bf16[2,4,16,512]{3,2,1,0:T(8,128)(2,1)S(1)} collective-permute-done((bf16[2,4,16,512]{3,2,1,0:T(8,128)(2,1)S(1)}, bf16[2,4,16,512]{3,2,1,0:T(8,128)(2,1)S(1)}, u32[]{:S(2)}, u32[]{:S(2)}) %collective-permute-start.6) | collective-permute-done | bytes 131104 | tf_op jit(solution)/shard_map/ppermute | solution.py:485
  35.8 0.0 collective-permute-done.7
  35.8 0.0 collective-permute-done.5
  35.9 0.0 copy-done.4
  35.9 0.0 copy-done.8
  35.9 0.0 copy-done.14
  35.9 0.0 copy-done.15
  35.9 0.0 copy-done.1
  35.9 0.0 copy-done.10
  35.9 0.0 copy-done.13
  35.9 16.5 %shard_map.148 = bf16[4,24,16,512]{3,2,1,0:T(8,128)(2,1)} custom-call(s32[3,2,4]{2,1,0:T(2,128)S(1)} %copy-done.10, bf16[6,64,512]{2,1,0:T(8,128)(2,1)S(1)} %pad_maximum_fusion.w0_ref, bf16[2,64,512]{2,1,0:T(8,128)(2,1)S(1)} %bitcast.13, bf16[4,64,512]{2,1,0:T(8,128)(2,1)S(1)} %bitcast.14, bf16[6,64,512]{2,1,0:T(8,128)(2,1)S(1)} %bitcast.15, ...), custom_call_target="tpu_custom_call" | custom-call | flops 15000000512 | bytes 12582912 | tf_op jit(solution)/shard_map/pallas_call | solution.py:441
  (12 shorter events, 0.1 us)
Async XLA Ops:
  0.0 18.4 %collective-permute-start.1 = (bf16[2,4,16,512]{3,2,1,0:T(8,128)(2,1)}, bf16[2,4,16,512]{3,2,1,0:T(8,128)(2,1)S(1)}, u32[]{:S(2)}, u32[]{:S(2)}) collective-permute-start(bf16[2,4,16,512]{3,2,1,0:T(8,128)(2,1)} %bitcast.26), channel_id=1, source_target_pairs={{0,2},{1,3},{2,0},{3,1},{4,6},{5,7},{6,4},{7,5},{8,10},{9,11},{10,... | collective-permute-start | bytes 393224 | tf_op jit(solution)/shard_map/ppermute | solution.py:485
  4.8 13.6 %collective-permute-start = (bf16[6,4,16,512]{3,2,1,0:T(8,128)(2,1)}, bf16[6,4,16,512]{3,2,1,0:T(8,128)(2,1)S(1)}, u32[]{:S(2)}, u32[]{:S(2)}) collective-permute-start(bf16[6,4,16,512]{3,2,1,0:T(8,128)(2,1)} %get-tuple-element.24), channel_id=1, source_target_pairs={{0,4},{1,5},{2,6},{3,7},{4,0},{5,1},{6,2},{7,3},{8,12},{9,13},{10,... | collective-permute-start | bytes 1179656 | tf_op jit(solution)/shard_map/ppermute | solution.py:485
  5.2 17.9 %collective-permute-start.2 = (bf16[6,4,16,512]{3,2,1,0:T(8,128)(2,1)}, bf16[6,4,16,512]{3,2,1,0:T(8,128)(2,1)S(1)}, u32[]{:S(2)}, u32[]{:S(2)}) collective-permute-start(bf16[6,4,16,512]{3,2,1,0:T(8,128)(2,1)} %get-tuple-element.27), channel_id=1, source_target_pairs={{0,0},{1,1},{2,2},{3,3},{4,8},{5,9},{6,10},{7,11},{8,4},{9,5},{10,... | collective-permute-start | bytes 1179656 | tf_op jit(solution)/shard_map/ppermute | solution.py:485
  8.1 18.0 %copy-start = (bf16[4,24,16,512]{3,2,1,0:T(8,128)(2,1)S(1)}, bf16[4,24,16,512]{3,2,1,0:T(8,128)(2,1)}, u32[]{:S(2)}) copy-start(bf16[4,24,16,512]{3,2,1,0:T(8,128)(2,1)} %x_hbm.5) | copy-start | bytes 4718596
  8.1 18.0 %copy-start.3 = (bf16[512,1024]{1,0:T(8,128)(2,1)S(1)}, bf16[512,1024]{1,0:T(8,128)(2,1)}, u32[]{:S(2)}) copy-start(bf16[512,1024]{1,0:T(8,128)(2,1)} %wkv_hbm.3) | copy-start | bytes 3145732
  8.2 18.0 %copy-start.5 = (bf16[512,512]{1,0:T(8,128)(2,1)S(1)}, bf16[512,512]{1,0:T(8,128)(2,1)}, u32[]{:S(2)}) copy-start(bf16[512,512]{1,0:T(8,128)(2,1)} %wq_hbm.3) | copy-start | bytes 1572868
  8.2 18.0 %copy-start.6 = (bf16[512,512]{1,0:T(8,128)(2,1)S(1)}, bf16[512,512]{1,0:T(8,128)(2,1)}, u32[]{:S(2)}) copy-start(bf16[512,512]{1,0:T(8,128)(2,1)} %wo_hbm.3) | copy-start | bytes 1572868
  8.2 18.0 %copy-start.7 = (bf16[512,512]{1,0:T(8,128)(2,1)S(1)}, bf16[512,512]{1,0:T(8,128)(2,1)}, u32[]{:S(2)}) copy-start(bf16[512,512]{1,0:T(8,128)(2,1)} %cwq_hbm.3) | copy-start | bytes 1572868
  8.2 18.0 %copy-start.9 = (s32[1536,16]{0,1:T(8,128)S(1)}, s32[1536,16]{0,1:T(8,128)}, u32[]{:S(2)}) copy-start(s32[1536,16]{0,1:T(8,128)} %param.16) | copy-start | bytes 294916
  8.2 18.0 %copy-start.11 = (f32[512]{0:T(512)S(1)}, f32[512]{0:T(512)}, u32[]{:S(2)}) copy-start(f32[512]{0:T(512)} %param.19) | copy-start | bytes 6148
  8.2 18.0 %copy-start.12 = (f32[512]{0:T(512)S(1)}, f32[512]{0:T(512)}, u32[]{:S(2)}) copy-start(f32[512]{0:T(512)} %param.20) | copy-start | bytes 6148
  23.1 8.2 %copy-start.16 = (bf16[1,2,64,512]{3,2,1,0:T(8,128)(2,1)S(1)}, bf16[1,2,64,512]{3,2,1,0:T(8,128)(2,1)}, u32[]{:S(2)}) copy-start(bf16[1,2,64,512]{3,2,1,0:T(8,128)(2,1)} %param.17) | copy-start | bytes 393220
  23.1 10.8 %collective-permute-start.3 = (bf16[2,4,16,512]{3,2,1,0:T(8,128)(2,1)S(1)}, bf16[2,4,16,512]{3,2,1,0:T(8,128)(2,1)S(1)}, u32[]{:S(2)}, u32[]{:S(2)}) collective-permute-start(bf16[2,4,16,512]{3,2,1,0:T(8,128)(2,1)S(1)} %slice.6), channel_id=1, source_target_pairs={{0,2},{1,3},{2,0},{3,1},{4,6},{5,7},{6,4},{7,5},{8,10},{9,11},{10,... | collective-permute-start | bytes 393224 | tf_op jit(solution)/shard_map/ppermute | solution.py:485
  25.2 8.7 %collective-permute-start.4 = (bf16[2,4,16,512]{3,2,1,0:T(8,128)(2,1)S(1)}, bf16[2,4,16,512]{3,2,1,0:T(8,128)(2,1)S(1)}, u32[]{:S(2)}, u32[]{:S(2)}) collective-permute-start(bf16[2,4,16,512]{3,2,1,0:T(8,128)(2,1)S(1)} %slice.7), channel_id=1, source_target_pairs={{0,2},{1,3},{2,0},{3,1},{4,6},{5,7},{6,4},{7,5},{8,10},{9,11},{10,... | collective-permute-start | bytes 393224 | tf_op jit(solution)/shard_map/ppermute | solution.py:485
  26.2 9.6 %copy-start.2 = (bf16[2048,512]{1,0:T(8,128)(2,1)S(1)}, bf16[2048,512]{1,0:T(8,128)(2,1)}, u32[]{:S(2)}) copy-start(bf16[2048,512]{1,0:T(8,128)(2,1)} %fout_hbm.1) | copy-start | bytes 6291460
  26.2 9.6 %copy-start.4 = (bf16[512,1024]{1,0:T(8,128)(2,1)S(1)}, bf16[512,1024]{1,0:T(8,128)(2,1)}, u32[]{:S(2)}) copy-start(bf16[512,1024]{1,0:T(8,128)(2,1)} %ckv_ref.1) | copy-start | bytes 3145732
  26.2 9.6 %copy-start.8 = (bf16[512,512]{1,0:T(8,128)(2,1)S(1)}, bf16[512,512]{1,0:T(8,128)(2,1)}, u32[]{:S(2)}) copy-start(bf16[512,512]{1,0:T(8,128)(2,1)} %cwo_ref.1) | copy-start | bytes 1572868
  26.3 9.6 %copy-start.14 = (bf16[4,2,128,512]{3,2,1,0:T(8,128)(2,1)S(1)}, bf16[4,2,128,512]{3,2,1,0:T(8,128)(2,1)}, u32[]{:S(2)}) copy-start(bf16[4,2,128,512]{3,2,1,0:T(8,128)(2,1)} %get-tuple-element.35.refs_0_) | copy-start | bytes 3145732
  26.3 9.6 %copy-start.15 = (bf16[4,2,128,512]{3,2,1,0:T(8,128)(2,1)S(1)}, bf16[4,2,128,512]{3,2,1,0:T(8,128)(2,1)}, u32[]{:S(2)}) copy-start(bf16[4,2,128,512]{3,2,1,0:T(8,128)(2,1)} %get-tuple-element.37.refs_2_) | copy-start | bytes 3145732
  31.3 4.6 %copy-start.1 = (bf16[512,2048]{1,0:T(8,128)(2,1)S(1)}, bf16[512,2048]{1,0:T(8,128)(2,1)}, u32[]{:S(2)}) copy-start(bf16[512,2048]{1,0:T(8,128)(2,1)} %fin_hbm.1) | copy-start | bytes 6291460
  31.3 4.6 %copy-start.10 = (s32[3,2,4]{2,1,0:T(2,128)S(1)}, s32[3,2,4]{2,1,0:T(2,128)}, u32[]{:S(2)}) copy-start(s32[3,2,4]{2,1,0:T(2,128)} %list_ref.1) | copy-start | bytes 292
  31.4 4.6 %copy-start.13 = (f32[512]{0:T(512)S(1)}, f32[512]{0:T(512)}, u32[]{:S(2)}) copy-start(f32[512]{0:T(512)} %param.21) | copy-start | bytes 6148
  31.4 4.4 %collective-permute-start.5 = (bf16[6,4,16,512]{3,2,1,0:T(8,128)(2,1)S(1)}, bf16[6,4,16,512]{3,2,1,0:T(8,128)(2,1)S(1)}, u32[]{:S(2)}, u32[]{:S(2)}) collective-permute-start(bf16[6,4,16,512]{3,2,1,0:T(8,128)(2,1)S(1)} %pad_maximum_fusion.1), channel_id=1, source_target_pairs={{0,1},{1,0},{2,3},{3,2},{4,5},{5,4},{6,7},{7,6},{8,9},{9,8},{10,11... | collective-permute-start | bytes 1179656 | tf_op jit(solution)/shard_map/ppermute | solution.py:485
  34.0 1.9 %collective-permute-start.7 = (bf16[4,4,16,512]{3,2,1,0:T(8,128)(2,1)S(1)}, bf16[4,4,16,512]{3,2,1,0:T(8,128)(2,1)S(1)}, u32[]{:S(2)}, u32[]{:S(2)}) collective-permute-start(bf16[4,4,16,512]{3,2,1,0:T(8,128)(2,1)S(1)} %constant_dynamic-update-slice_fusion), channel_id=1, source_target_pairs={{0,1},{1,0},{2,3},{3,2},{4,5},{5,4},{6,7},{7,6},{8,9},{9,8},{10,11... | collective-permute-start | bytes 786440 | tf_op jit(solution)/shard_map/ppermute | solution.py:485
  34.2 1.7 %collective-permute-start.6 = (bf16[2,4,16,512]{3,2,1,0:T(8,128)(2,1)S(1)}, bf16[2,4,16,512]{3,2,1,0:T(8,128)(2,1)S(1)}, u32[]{:S(2)}, u32[]{:S(2)}) collective-permute-start(bf16[2,4,16,512]{3,2,1,0:T(8,128)(2,1)S(1)} %slice.7), channel_id=1, source_target_pairs={{0,1},{1,0},{2,3},{3,2},{4,5},{5,4},{6,7},{7,6},{8,9},{9,8},{10,11... | collective-permute-start | bytes 393224 | tf_op jit(solution)/shard_map/ppermute | solution.py:485
